TPU v7x, 32 devices: a whole 2x2x4 slice. The times are simulated.
32 devices in a mesh: rows: 8 (over z, y), feat: 4 (over x, core).
Axes of the slice: x: 2, y: 2, z: 4, core: 2. Of those that a mesh axis runs over, the one named last changes fastest.
Arguments:
- inputs: bfloat16 [8, 48, 256, 512], P('rows', 'feat'), may hold values from -6 to 6
- feat_gain: bfloat16 [512], P(('rows', 'feat')), may hold values from 0.5 to 1.5
- feat_shift: bfloat16 [512], P(('rows', 'feat')), may hold values from -3 to 3
- feat_qkv: bfloat16 [512, 1536], P(('rows', 'feat')), may hold values from -0.25 to 0.25
- feat_out: bfloat16 [512, 512], P(('rows', 'feat')), may hold values from -0.75 to 0.75
- row_gain: bfloat16 [512], P(('rows', 'feat')), may hold values from 0.5 to 1.5
- row_shift: bfloat16 [512], P(('rows', 'feat')), may hold values from -3 to 3
- row_qkv: bfloat16 [512, 1536], P(('rows', 'feat')), may hold values from -0.25 to 0.25
- row_out: bfloat16 [512, 512], P(('rows', 'feat')), may hold values from -0.75 to 0.75
- mlp_gain: bfloat16 [512], P(('rows', 'feat')), may hold values from 0.5 to 1.5
- mlp_shift: bfloat16 [512], P(('rows', 'feat')), may hold values from -3 to 3
- mlp_in: bfloat16 [512, 2048], P(('rows', 'feat')), may hold values from -0.25 to 0.25
- mlp_out: bfloat16 [2048, 512], P(('rows', 'feat')), may hold values from -0.125 to 0.125
- cotangent: bfloat16 [8, 48, 256, 512], P('rows', 'feat'), may hold values from -6 to 6
- segments: int32 [8, 256], P('rows'), may hold values from 0 to 3, as said below
- context: int32 [8, 4], P('rows'), may hold values from 1 to 96, as said below
- feature_mask: int32 [8, 48], P('rows'), may hold values from 0 to 1, as said below
Outputs:
- output: bfloat16 [8, 48, 256, 512], P('rows', 'feat')
- input_grad: float32 [8, 48, 256, 512], P('rows', 'feat')
- feat_gain_grad: float32 [512], P(('rows', 'feat'))
- feat_shift_grad: float32 [512], P(('rows', 'feat'))
- feat_qkv_grad: float32 [512, 1536], P(('rows', 'feat'))
- feat_out_grad: float32 [512, 512], P(('rows', 'feat'))
- row_gain_grad: float32 [512], P(('rows', 'feat'))
- row_shift_grad: float32 [512], P(('rows', 'feat'))
- row_qkv_grad: float32 [512, 1536], P(('rows', 'feat'))
- row_out_grad: float32 [512, 512], P(('rows', 'feat'))
- mlp_gain_grad: float32 [512], P(('rows', 'feat'))
- mlp_shift_grad: float32 [512], P(('rows', 'feat'))
- mlp_in_grad: float32 [512, 2048], P(('rows', 'feat'))
- mlp_out_grad: float32 [2048, 512], P(('rows', 'feat'))
Inputs may be any that keep to these rules, and one draw needn't show every extreme that they name: `segments`: within a slot table numbers never fall along the rows and every table has at least one row. `context`: each table's count is at most its number of rows. `feature_mask`: feature 0 of every slot is real.
All inputs are finite; a program needn't handle non-finite values.
Results may differ from a plain program's by a relative error of at most 0.018.
Values may be sent and summed in bfloat16 or wider, within the bound.
No kernel may reach another device: no remote copies, remote signals or barrier semaphores. Data moves between devices by JAX's collectives and lax.ppermute only.
A program may use at most 320 MiB of HBM per device.

v0:
```python
from functools import partial

import jax
import jax.numpy as jnp
from jax import lax
from jax.sharding import PartitionSpec as P

D = 512
HEADS = 4
HEAD_DIM = 128


epsilon = 1e-05
masked_score = -1000000000.0


def layer_norm(hidden, scales, shifts):
    average = jnp.mean(hidden, axis=-1, keepdims=True)
    centred = hidden - average
    spread = jnp.mean(centred * centred, axis=-1, keepdims=True)
    return centred * lax.rsqrt(spread + epsilon) * scales + shifts


def row_allowed(segments, context):
    tables = jnp.arange(context.shape[1], dtype=jnp.int32)
    member = (segments[:, :, None] == tables[None, None, :]).astype(jnp.int32)
    table_sizes = jnp.sum(member, axis=1, keepdims=True)
    starts = jnp.cumsum(table_sizes, axis=2) - table_sizes
    places = jnp.arange(segments.shape[1], dtype=jnp.int32)[None, :] - jnp.sum(
        member * starts, axis=2
    )
    limits = jnp.sum(member * context[:, None, :], axis=2)
    usable = places < limits
    return (segments[:, :, None] == segments[:, None, :]) & usable[:, None, :]


def soft_rows(scores, allowed):
    scores = jnp.where(allowed, scores, masked_score)
    highest = jnp.max(scores, axis=-1, keepdims=True)
    weights = jnp.exp(scores - highest)
    totals = jnp.sum(weights, axis=-1, keepdims=True)
    return (weights / totals, highest + jnp.log(totals))


def soft_again(scores, allowed, logsum):
    return jnp.exp(jnp.where(allowed, scores, masked_score) - logsum)


def soft_back(attention, grad_attention):
    inner_sum = jnp.sum(attention * grad_attention, axis=-1, keepdims=True)
    return (attention * (grad_attention - inner_sum)).astype(jnp.bfloat16)


def matmul(left, right):
    return jnp.dot(left, right, preferred_element_type=jnp.float32)


def over_rows(left, right):
    return lax.dot_general(
        left, right, (((0,), (0,)), ((), ())), preferred_element_type=jnp.float32
    )


def by_rows(left, right):
    return lax.dot_general(
        left, right, (((1,), (1,)), ((), ())), preferred_element_type=jnp.float32
    )


def split_heads(packed, grid):
    shaped = packed.reshape(grid + (3, HEADS, HEAD_DIM))
    return (shaped[:, :, :, 0], shaped[:, :, :, 1], shaped[:, :, :, 2])


def feature_mix(query_one, key_all, value_all, feat_valid, scaling):
    scores = (
        jnp.einsum("sfrhd,sgrhd->srhfg", query_one, key_all, preferred_element_type=jnp.float32)
        * scaling
    )
    attention, logsum = soft_rows(scores, feat_valid)
    heads = jnp.einsum(
        "srhfg,sgrhd->sfrhd",
        attention.astype(jnp.bfloat16),
        value_all,
        preferred_element_type=jnp.float32,
    )
    return (heads.astype(jnp.bfloat16), logsum)


def feature_back(query_one, key_all, value_all, grad_heads, feat_valid, logsum, scaling):
    scores = (
        jnp.einsum("sfrhd,sgrhd->srhfg", query_one, key_all, preferred_element_type=jnp.float32)
        * scaling
    )
    attention = soft_again(scores, feat_valid, logsum)
    grad_attn = jnp.einsum(
        "sfrhd,sgrhd->srhfg", grad_heads, value_all, preferred_element_type=jnp.float32
    )
    grad_scores = soft_back(attention, grad_attn)
    grad_query = (
        jnp.einsum("srhfg,sgrhd->sfrhd", grad_scores, key_all, preferred_element_type=jnp.float32)
        * scaling
    )
    key_terms = (
        jnp.einsum("srhfg,sfrhd->sgrhd", grad_scores, query_one, preferred_element_type=jnp.float32)
        * scaling
    )
    value_terms = jnp.einsum(
        "srhfg,sfrhd->sgrhd",
        attention.astype(jnp.bfloat16),
        grad_heads,
        preferred_element_type=jnp.float32,
    )
    return (grad_query, key_terms, value_terms)


def per_device(
    inputs,
    feat_gain,
    feat_shift,
    feat_qkv,
    feat_out,
    row_gain,
    row_shift,
    row_qkv,
    row_out,
    mlp_gain,
    mlp_shift,
    mlp_in,
    mlp_out,
    cotangent,
    segments,
    context,
    feature_mask,
):
    shards = (
        feat_gain,
        feat_shift,
        feat_qkv,
        feat_out,
        row_gain,
        row_shift,
        row_qkv,
        row_out,
        mlp_gain,
        mlp_shift,
        mlp_in,
        mlp_out,
    )
    gathered = (
        lax.all_gather(shards[0], ("rows", "feat"), axis=0, tiled=True),
        lax.all_gather(shards[1], ("rows", "feat"), axis=0, tiled=True),
        lax.all_gather(shards[2], ("rows", "feat"), axis=0, tiled=True),
        lax.all_gather(shards[3], ("rows", "feat"), axis=0, tiled=True),
        lax.all_gather(shards[4], ("rows", "feat"), axis=0, tiled=True),
        lax.all_gather(shards[5], ("rows", "feat"), axis=0, tiled=True),
        lax.all_gather(shards[6], ("rows", "feat"), axis=0, tiled=True),
        lax.all_gather(shards[7], ("rows", "feat"), axis=0, tiled=True),
        lax.all_gather(shards[8], ("rows", "feat"), axis=0, tiled=True),
        lax.all_gather(shards[9], ("rows", "feat"), axis=0, tiled=True),
        lax.all_gather(shards[10], ("rows", "feat"), axis=0, tiled=True),
        lax.all_gather(shards[11], ("rows", "feat"), axis=0, tiled=True),
    )
    (
        gain_one,
        shift_one,
        qkv_one,
        out_one,
        gain_two,
        shift_two,
        qkv_two,
        out_two,
        gain_three,
        shift_three,
        up_weight,
        down_weight,
    ) = gathered
    grid = (inputs.shape[0], inputs.shape[1], inputs.shape[2])
    tokens_dev = grid[0] * grid[1] * grid[2]
    scaling = HEAD_DIM ** (-0.5)
    head_shape = grid + (HEADS, HEAD_DIM)
    feat_valid = (feature_mask > 0)[:, None, None, None, :]
    first = inputs.astype(jnp.float32).reshape(tokens_dev, D)
    normed_one, norm_back_one = jax.vjp(
        layer_norm, first, gain_one.astype(jnp.float32), shift_one.astype(jnp.float32)
    )
    low_one = normed_one.astype(jnp.bfloat16)
    packed_one = matmul(low_one, qkv_one).astype(jnp.bfloat16)
    query_one, key_one, value_one = split_heads(packed_one, grid)
    key_all, value_all = (
        lax.all_gather(key_one, "feat", axis=1, tiled=True),
        lax.all_gather(value_one, "feat", axis=1, tiled=True),
    )
    heads_local, logsum_one = feature_mix(query_one, key_all, value_all, feat_valid, scaling)
    heads_one = heads_local.reshape(tokens_dev, D)
    second = first + matmul(heads_one, out_one)
    allowed = row_allowed(segments, context)[:, None, None]
    normed_two, norm_back_two = jax.vjp(
        layer_norm, second, gain_two.astype(jnp.float32), shift_two.astype(jnp.float32)
    )
    low_two = normed_two.astype(jnp.bfloat16)
    query_two, key_two, value_two = split_heads(matmul(low_two, qkv_two).astype(jnp.bfloat16), grid)
    scores_two = (
        jnp.einsum("sfrhd,sfthd->sfhrt", query_two, key_two, preferred_element_type=jnp.float32)
        * scaling
    )
    attn_two, logsum_two = soft_rows(scores_two, allowed)
    heads_two = jnp.einsum(
        "sfhrt,sfthd->sfrhd",
        attn_two.astype(jnp.bfloat16),
        value_two,
        preferred_element_type=jnp.float32,
    )
    heads_two = heads_two.astype(jnp.bfloat16).reshape(tokens_dev, D)
    third = second + matmul(heads_two, out_two)
    normed_three, norm_back_three = jax.vjp(
        layer_norm, third, gain_three.astype(jnp.float32), shift_three.astype(jnp.float32)
    )
    low_three = normed_three.astype(jnp.bfloat16)
    hidden = matmul(low_three, up_weight)
    active, gelu_back = jax.vjp(partial(jax.nn.gelu, approximate=False), hidden)
    active_low = active.astype(jnp.bfloat16)
    output = (third + matmul(active_low, down_weight)).astype(jnp.bfloat16).reshape(inputs.shape)
    grad_out = cotangent.astype(jnp.float32).reshape(tokens_dev, D)
    grad_down = grad_out.astype(jnp.bfloat16)
    down_grad = over_rows(active_low, grad_down)
    grad_active = by_rows(grad_down, down_weight)
    grad_hidden = gelu_back(grad_active)[0].astype(jnp.bfloat16)
    up_grad = over_rows(low_three, grad_hidden)
    back_three, gain_three_grad, shift_three_grad = norm_back_three(by_rows(grad_hidden, up_weight))
    grad_third = grad_out + back_three
    grad_branch = grad_third.astype(jnp.bfloat16)
    out_two_grad = over_rows(heads_two, grad_branch)
    grad_heads = by_rows(grad_branch, out_two).astype(jnp.bfloat16).reshape(head_shape)
    scores_two = (
        jnp.einsum("sfrhd,sfthd->sfhrt", query_two, key_two, preferred_element_type=jnp.float32)
        * scaling
    )
    attn_two = soft_again(scores_two, allowed, logsum_two)
    grad_attn = jnp.einsum(
        "sfrhd,sfthd->sfhrt", grad_heads, value_two, preferred_element_type=jnp.float32
    )
    grad_scores = soft_back(attn_two, grad_attn)
    grad_query = (
        jnp.einsum("sfhrt,sfthd->sfrhd", grad_scores, key_two, preferred_element_type=jnp.float32)
        * scaling
    )
    grad_key = (
        jnp.einsum("sfhrt,sfrhd->sfthd", grad_scores, query_two, preferred_element_type=jnp.float32)
        * scaling
    )
    grad_value = jnp.einsum(
        "sfhrt,sfrhd->sfthd",
        attn_two.astype(jnp.bfloat16),
        grad_heads,
        preferred_element_type=jnp.float32,
    )
    grad_qkv = (
        jnp.stack((grad_query, grad_key, grad_value), axis=3)
        .astype(jnp.bfloat16)
        .reshape(tokens_dev, 3 * D)
    )
    qkv_two_grad = over_rows(low_two, grad_qkv)
    back_two, gain_two_grad, shift_two_grad = norm_back_two(by_rows(grad_qkv, qkv_two))
    grad_second = grad_third + back_two
    grad_branch = grad_second.astype(jnp.bfloat16)
    out_one_grad = over_rows(heads_one, grad_branch)
    grad_heads_low = by_rows(grad_branch, out_one).astype(jnp.bfloat16)
    grad_query, key_terms, value_terms = feature_back(
        query_one,
        key_all,
        value_all,
        grad_heads_low.reshape(head_shape),
        feat_valid,
        logsum_one,
        scaling,
    )
    grad_key, grad_value = (
        lax.psum_scatter(
            key_terms.astype(jnp.bfloat16), "feat", scatter_dimension=1, tiled=True
        ).astype(jnp.float32),
        lax.psum_scatter(
            value_terms.astype(jnp.bfloat16), "feat", scatter_dimension=1, tiled=True
        ).astype(jnp.float32),
    )
    grad_qkv = (
        jnp.stack((grad_query, grad_key, grad_value), axis=3)
        .astype(jnp.bfloat16)
        .reshape(tokens_dev, 3 * D)
    )
    qkv_one_grad = over_rows(low_one, grad_qkv)
    back_one, gain_one_grad, shift_one_grad = norm_back_one(by_rows(grad_qkv, qkv_one))
    input_grad = (grad_second + back_one).reshape(inputs.shape)
    summed = (
        lax.psum_scatter(gain_one_grad, ("rows", "feat"), scatter_dimension=0, tiled=True),
        lax.psum_scatter(shift_one_grad, ("rows", "feat"), scatter_dimension=0, tiled=True),
        lax.psum_scatter(qkv_one_grad, ("rows", "feat"), scatter_dimension=0, tiled=True),
        lax.psum_scatter(out_one_grad, ("rows", "feat"), scatter_dimension=0, tiled=True),
        lax.psum_scatter(gain_two_grad, ("rows", "feat"), scatter_dimension=0, tiled=True),
        lax.psum_scatter(shift_two_grad, ("rows", "feat"), scatter_dimension=0, tiled=True),
        lax.psum_scatter(qkv_two_grad, ("rows", "feat"), scatter_dimension=0, tiled=True),
        lax.psum_scatter(out_two_grad, ("rows", "feat"), scatter_dimension=0, tiled=True),
        lax.psum_scatter(gain_three_grad, ("rows", "feat"), scatter_dimension=0, tiled=True),
        lax.psum_scatter(shift_three_grad, ("rows", "feat"), scatter_dimension=0, tiled=True),
        lax.psum_scatter(up_grad, ("rows", "feat"), scatter_dimension=0, tiled=True),
        lax.psum_scatter(down_grad, ("rows", "feat"), scatter_dimension=0, tiled=True),
    )
    return (
        output,
        input_grad,
        summed[0],
        summed[1],
        summed[2],
        summed[3],
        summed[4],
        summed[5],
        summed[6],
        summed[7],
        summed[8],
        summed[9],
        summed[10],
        summed[11],
    )


def solution(mesh):
    placed = (
        P("rows", "feat", None, None),
        P(("rows", "feat")),
        P(("rows", "feat")),
        P(("rows", "feat"), None),
        P(("rows", "feat"), None),
        P(("rows", "feat")),
        P(("rows", "feat")),
        P(("rows", "feat"), None),
        P(("rows", "feat"), None),
        P(("rows", "feat")),
        P(("rows", "feat")),
        P(("rows", "feat"), None),
        P(("rows", "feat"), None),
        P("rows", "feat", None, None),
        P("rows", None),
        P("rows", None),
        P("rows", None),
    )
    return jax.shard_map(
        per_device,
        mesh=mesh,
        in_specs=placed,
        out_specs=(
            P("rows", "feat", None, None),
            P("rows", "feat", None, None),
            P(("rows", "feat")),
            P(("rows", "feat")),
            P(("rows", "feat"), None),
            P(("rows", "feat"), None),
            P(("rows", "feat")),
            P(("rows", "feat")),
            P(("rows", "feat"), None),
            P(("rows", "feat"), None),
            P(("rows", "feat")),
            P(("rows", "feat")),
            P(("rows", "feat"), None),
            P(("rows", "feat"), None),
        ),
        check_vma=False,
    )
```

profile of v0, /device:TPU:0, one launch (start us, length us, event | category | flops | bytes accessed | tf_op | source)
XLA Modules:
  0.0 1683.4 jit_solution(14117399684684827132)
XLA Ops:
  13.2 42.2 %all-reduce.13 = (bf16[512]{0:T(512)(128)(2,1)S(1)}, bf16[512]{0:T(512)(128)(2,1)S(1)}, bf16[512]{0:T(512)(128)(2,1)S(1)}, bf16[512]{0:T(512)(128)(2,1)S(1)}, bf...) all-reduce(bf16[512]{0:T(512)(128)(2,1)S(1)} %dynamic-update-slice., ...), channel_id=1, replica_groups=mesh['rows'=8,'feat'=4] {'rows','feat'}, use_global_device_ids=true, to_apply=%add.1 | all-reduce | flops 3072 | bytes 12288
  77.9 16.5 reshape.726
  112.4 44.2 %all_gather.47 = bf16[512,512]{1,0:T(8,128)(2,1)} all-gather(bf16[16,512]{1,0:T(8,128)(2,1)S(1)} %copy-done.61), channel_id=1, replica_groups=mesh['rows'=8,'feat'=4] {'rows','feat'}, dimensions={0}, use_global_device_ids=true | all-gather | bytes 540672 | tf_op jit(solution)/shard_map/all_gather | solution.py:154
  157.2 41.4 %all_gather.51 = bf16[512,512]{1,0:T(8,128)(2,1)} all-gather(bf16[16,512]{1,0:T(8,128)(2,1)S(1)} %copy-done.62), channel_id=1, replica_groups=mesh['rows'=8,'feat'=4] {'rows','feat'}, dimensions={0}, use_global_device_ids=true | all-gather | bytes 540672 | tf_op jit(solution)/shard_map/all_gather | solution.py:158
  198.7 30.4 %fusion.51 = (f32[256,4,12]{2,1,0:T(4,128)S(1)}, f32[256,4,12,48]{3,2,1,0:T(8,128)S(1)}) fusion(pred[48]{0:T(512)(128)(4,1)S(1)} %compare_bitcast_fusion, bf16[1,48,256,1,4,128]{5,2,4,3,0,1:T(8,128)(2,1)} %all-gather.19.cloned.1.call-done, bf16[1,12,256,1,4,128]{5,4,3,2,1,0:T(4,128)(2,1)} %get-tuple-element.49), kind=kOutput, calls=%fused_computation.105 | convolution fusion | flops 152752128 | bytes 18137136 | tf_op jit(solution)/shard_map/sfrhd,sgrhd->srhfg/dot_general | solution.py:77
  232.5 29.3 %fusion.21 = f32[256,4,12]{2,1,0:T(4,128)} fusion(f32[256,4,12]{2,1,0:T(4,128)S(1)} %get-tuple-element.52, f32[256,4,12,48]{3,2,1,0:T(8,128)S(1)} %get-tuple-element.53, pred[48]{0:T(512)(128)(4,1)S(1)} %compare_bitcast_fusion), kind=kLoop, calls=%fused_computation.53 | loop fusion | flops 2347008 | bytes 2457648 | tf_op jit(solution)/shard_map/reduce_sum | solution.py:41
  261.8 19.0 %all-gather.17.cloned.1.call-done = bf16[1,48,256,1,4,128]{5,2,4,3,0,1:T(8,128)(2,1)} async-done(((bf16[1,12,256,1,4,128]{5,2,4,3,0,1:T(8,128)(2,1)}), bf16[1,48,256,1,4,128]{5,2,4,3,0,1:T(8,128)(2,1)}) %all-gather.17.cloned.1.call-update) | async-done | bytes 12582928 | tf_op jit(solution)/shard_map/all_gather | solution.py:192
  280.8 28.8 %convert_bitcast_fusion.1 = bf16[1,12,256,4,128]{4,1,3,2,0:T(8,128)(2,1)S(1)} fusion(f32[256,4,12]{2,1,0:T(4,128)} %fusion.21, f32[256,4,12]{2,1,0:T(4,128)} %copy-done.29, f32[256,4,12,48]{3,2,1,0:T(8,128)} %copy-done.9, pred[48]{0:T(512)(128)(4,1)S(1)} %compare_bitcast_fusion, bf16[1,48,256,1,4,128]{5,2,4,3,0,1:T(8,128)(2,1)} %all-gather.17.cloned.1.call-done), kind=kOutput, calls=%fused_computation.101 | convolution fusion | flops 155516928 | bytes 18186288 | tf_op jit(solution)/shard_map/srhfg,sgrhd->sfrhd/dot_general | solution.py:81
  317.7 20.7 %all-gather.11.cloned.1.call-done = bf16[512,1536]{1,0:T(8,128)(2,1)} async-done(((bf16[16,1536]{1,0:T(8,128)(2,1)}), bf16[512,1536]{1,0:T(8,128)(2,1)}) %all-gather.11.cloned.1.call-update) | async-done | bytes 1572880 | tf_op jit(solution)/shard_map/all_gather | solution.py:157
  349.0 16.4 reshape.731
  411.8 64.8 %multiply_convert_fusion.1 = (bf16[3072,2048]{1,0:T(8,128)(2,1)}, f32[3072,2048]{1,0:T(8,128)}, f32[3072,2048]{1,0:T(8,128)}) fusion(bf16[512,2048]{1,0:T(8,128)(2,1)} %all-gather.13.cloned.1.call-done, f32[3072,512]{1,0:T(8,128)} %copy-done.6, f32[512]{0:T(512)S(1)} %convert_element_type.185, f32[512]{0:T(512)S(1)} %convert_element_type.184, ...), kind=kOutput, calls=%fused_computation.4 | convolution fusion | flops 6859259904 | bytes 71331840 | tf_op jit(solution)/shard_map/dot_general | solution.py:55
  476.6 25.8 %add_convert_fusion = bf16[3072,2048]{1,0:T(8,128)(2,1)} fusion(f32[3072,2048]{1,0:T(8,128)} %get-tuple-element.43, f32[3072,2048]{1,0:T(8,128)} %get-tuple-element.60, bf16[3072,512]{1,0:T(8,128)(2,1)S(1)} %bitcast.206, bf16[2048,512]{1,0:T(8,128)(2,1)} %all-gather.15.cloned.1.call-done), kind=kOutput, calls=%fused_computation.3 | convolution fusion | flops 6530531328 | bytes 68157440 | tf_op jit(solution)/shard_map/dot_general | solution.py:65
  502.4 16.9 %multiply_reduce_fusion.2 = (f32[512]{0:T(512)}, f32[3072]{0:T(1024)S(1)}, f32[512]{0:T(512)}, f32[3072,512]{1,0:T(8,128)S(1)}) fusion(f32[3072,512]{1,0:T(8,128)} %copy-done.6, f32[3072]{0:T(1024)S(1)} %fusion.79, f32[3072]{0:T(1024)S(1)} %broadcast_multiply_fusion.1, f32[512]{0:T(512)S(1)} %convert_element_type.184, ...), kind=kOutput, calls=%fused_computation.77 | convolution fusion | flops 6455029760 | bytes 27305984 | tf_op jit(solution)/shard_map/dot_general | solution.py:65
  591.5 15.1 copy.142
  606.6 16.1 convert_element_type.194
  622.7 14.0 multiply_reduce_fusion.3
  652.7 34.5 %multiply_reduce_fusion.1 = (f32[256,4,12]{2,1,0:T(4,128)S(1)}, f32[256,4,12,48]{3,2,1,0:T(8,128)}) fusion(f32[256,4,12]{2,1,0:T(4,128)S(1)} %bitcast.209, f32[256,4,12,48]{3,2,1,0:T(8,128)} %copy-done.9, pred[48]{0:T(512)(128)(4,1)S(1)} %copy-done.69, bf16[1,48,256,1,4,128]{5,2,4,3,0,1:T(8,128)(2,1)} %all-gather.17.cloned.1.call-done, ...), kind=kOutput, calls=%fused_computation.48 | convolution fusion | flops 153931776 | bytes 20545584 | tf_op jit(solution)/shard_map/sfrhd,sgrhd->srhfg/dot_general | solution.py:96
  703.1 13.3 copy.145
  718.3 15.0 convert_bitcast_fusion
  733.4 13.8 copy.148
  759.4 12.8 fusion.90
  772.3 15.5 fusion.91
  803.4 28.7 %fusion.7 = f32[256,4,128,12]{2,3,1,0:T(8,128)} fusion(bf16[256,4,12,48]{3,2,1,0:T(8,128)(2,1)S(1)} %copy-done.5, bf16[1,48,256,1,4,128]{5,2,4,3,0,1:T(8,128)(2,1)} %all-gather.19.cloned.1.call-done), kind=kOutput, calls=%fused_computation.20 | convolution fusion | flops 150994944 | bytes 20054016 | tf_op jit(solution)/shard_map/srhfg,sgrhd->sfrhd/dot_general | solution.py:101
  854.1 62.0 %reduce-scatter.11.cloned.1.call-done = bf16[1,12,256,4,128]{4,2,3,0,1:T(8,128)(2,1)} async-done(((bf16[1,48,256,4,128]{4,2,3,0,1:T(8,128)(2,1)}), bf16[1,12,256,4,128]{4,2,3,0,1:T(8,128)(2,1)}) %reduce-scatter.11.cloned.1.call-update) | async-done | bytes 3145744 | tf_op jit(solution)/shard_map/reduce_scatter | solution.py:282
  936.7 16.0 convert_element_type.206
  979.7 39.6 %all-reduce.12 = (f32[512]{0:T(512)S(1)}, f32[512]{0:T(512)S(1)}, f32[512]{0:T(512)S(1)}, f32[512]{0:T(512)S(1)}, f32[512]{0:T(512)S(1)}, /*index=5*/f32[512]{0:T(512)S(1)}) all-reduce(f32[512]{0:T(512)S(1)} %get-tuple-element.18, f32[512]{0:T(512)S(1)} %get-tuple-element.22, ...), channel_id=6, replica_groups=mesh['rows'=8,'feat'=4] {'rows','feat'}, use_global_device_ids=true, to_apply=%region_25.26.clone | all-reduce | flops 3072 | bytes 24576
  1031.6 22.3 %reduce-scatter.15.cloned.1.call-done = f32[16,512]{1,0:T(8,128)} async-done(((f32[512,512]{1,0:T(8,128)}), f32[16,512]{1,0:T(8,128)}) %reduce-scatter.15.cloned.1.call-update) | async-done | bytes 32784 | tf_op jit(solution)/shard_map/reduce_scatter | solution.py:298
  1053.9 133.5 %reduce-scatter.19.cloned.1.call-done = f32[16,512]{1,0:T(8,128)} async-done(((f32[512,512]{1,0:T(8,128)}), f32[16,512]{1,0:T(8,128)}) %reduce-scatter.19.cloned.1.call-update) | async-done | bytes 32784 | tf_op jit(solution)/shard_map/reduce_scatter | solution.py:302
  1187.4 103.5 %reduce-scatter.17.cloned.1.call-done = f32[16,1536]{1,0:T(8,128)} async-done(((f32[512,1536]{1,0:T(8,128)}), f32[16,1536]{1,0:T(8,128)}) %reduce-scatter.17.cloned.1.call-update) | async-done | bytes 98320 | tf_op jit(solution)/shard_map/reduce_scatter | solution.py:301
  1290.9 142.7 %reduce-scatter.21.cloned.1.call-done = f32[16,2048]{1,0:T(8,128)} async-done(((f32[512,2048]{1,0:T(8,128)}), f32[16,2048]{1,0:T(8,128)}) %reduce-scatter.21.cloned.1.call-update) | async-done | bytes 131088 | tf_op jit(solution)/shard_map/reduce_scatter | solution.py:305
  1433.6 139.8 %reduce-scatter.23.cloned.1.call-done = f32[64,512]{1,0:T(8,128)} async-done(((f32[2048,512]{1,0:T(8,128)}), f32[64,512]{1,0:T(8,128)}) %reduce-scatter.23.cloned.1.call-update) | async-done | bytes 131088 | tf_op jit(solution)/shard_map/reduce_scatter | solution.py:306
  1573.4 103.2 %reduce-scatter.13.cloned.1.call-done = f32[16,1536]{1,0:T(8,128)} async-done(((f32[512,1536]{1,0:T(8,128)}), f32[16,1536]{1,0:T(8,128)}) %reduce-scatter.13.cloned.1.call-update) | async-done | bytes 98320 | tf_op jit(solution)/shard_map/reduce_scatter | solution.py:297
  (308 shorter events, 330.3 us)
Async XLA Ops:
  7.2 54.7 %copy-start.1 = (bf16[1,12,256,512]{3,2,1,0:T(8,128)(2,1)S(1)}, bf16[1,12,256,512]{3,2,1,0:T(8,128)(2,1)}, u32[]{:S(2)}) copy-start(bf16[1,12,256,512]{3,2,1,0:T(8,128)(2,1)} %param.17) | copy-start | bytes 9437188
  7.2 61.4 %all-gather.9.cloned.1.call-start = ((), (), s32[]{:S(2)}) async-start(), calls=%async_computation.8 | async-start | bytes 1622016 | tf_op jit(solution)/shard_map/all_gather | solution.py:153
  7.9 190.7 %all-gather.19.cloned.1.call-start = ((), (), s32[]{:S(2)}) async-start(), calls=%async_computation.21 | async-start | bytes 15728640 | tf_op jit(solution)/shard_map/all_gather | solution.py:191
  106.1 50.6 %copy-start.63 = (s32[1,256]{1,0:T(1,128)S(1)}, s32[1,256]{1,0:T(1,128)}, u32[]{:S(2)}) copy-start(s32[1,256]{1,0:T(1,128)} %param.31) | copy-start | bytes 3076
  106.1 50.9 %copy-start.78 = (s32[1,4]{1,0:T(1,128)S(1)}, s32[1,4]{1,0:T(1,128)}, u32[]{:S(2)}) copy-start(s32[1,4]{1,0:T(1,128)} %param.32) | copy-start | bytes 52
  106.1 51.1 %copy-start.62 = (bf16[16,512]{1,0:T(8,128)(2,1)S(1)}, bf16[16,512]{1,0:T(8,128)(2,1)}, u32[]{:S(2)}) copy-start(bf16[16,512]{1,0:T(8,128)(2,1)} %param.25) | copy-start | bytes 49156
  106.1 174.7 %all-gather.17.cloned.1.call-start = ((), (), s32[]{:S(2)}) async-start(), calls=%async_computation.20 | async-start | bytes 15728640 | tf_op jit(solution)/shard_map/all_gather | solution.py:192
  110.6 227.9 %all-gather.11.cloned.1.call-start = ((), (), s32[]{:S(2)}) async-start(), calls=%async_computation.9 | async-start | bytes 1622016 | tf_op jit(solution)/shard_map/all_gather | solution.py:157
  111.2 300.6 %all-gather.13.cloned.1.call-start = ((), (), s32[]{:S(2)}) async-start(), calls=%async_computation.10 | async-start | bytes 2162688 | tf_op jit(solution)/shard_map/all_gather | solution.py:161
  111.7 364.9 %all-gather.15.cloned.1.call-start = ((), (), s32[]{:S(2)}) async-start(), calls=%async_computation.11 | async-start | bytes 2162688 | tf_op jit(solution)/shard_map/all_gather | solution.py:162
  112.3 741.8 %reduce-scatter.9.cloned.1.call-start = ((), (), s32[]{:S(2)}) async-start(), calls=%async_computation.12 | async-start | bytes 15728640 | tf_op jit(solution)/shard_map/reduce_scatter | solution.py:279
  112.4 168.4 %copy-start.68 = (pred[48]{0:T(512)(128)(4,1)}, pred[48]{0:T(512)(128)(4,1)S(1)}, u32[]{:S(2)}) copy-start(pred[48]{0:T(512)(128)(4,1)S(1)} %compare_bitcast_fusion) | copy-start | bytes 148
  156.6 181.9 %copy-start.64 = (f32[512]{0:T(512)}, f32[512]{0:T(512)S(1)}, u32[]{:S(2)}) copy-start(f32[512]{0:T(512)S(1)} %convert_element_type.175) | copy-start | bytes 6148
  156.6 181.8 %copy-start.70 = (f32[512]{0:T(512)}, f32[512]{0:T(512)S(1)}, u32[]{:S(2)}) copy-start(f32[512]{0:T(512)S(1)} %convert_element_type.176) | copy-start | bytes 6148
  157.2 231.4 %copy-start.30 = (pred[256,256]{0,1:T(8,128)(4,1)}, pred[256,256]{0,1:T(8,128)(4,1)S(1)}, u32[]{:S(2)}) copy-start(pred[256,256]{0,1:T(8,128)(4,1)S(1)} %compare_and_fusion) | copy-start | bytes 196612
  198.6 320.7 %copy-start.66 = (f32[512]{0:T(512)}, f32[512]{0:T(512)S(1)}, u32[]{:S(2)}) copy-start(f32[512]{0:T(512)S(1)} %convert_element_type.184) | copy-start | bytes 6148
  198.6 213.2 %copy-start.72 = (f32[512]{0:T(512)}, f32[512]{0:T(512)S(1)}, u32[]{:S(2)}) copy-start(f32[512]{0:T(512)S(1)} %convert_element_type.185) | copy-start | bytes 6148
  313.1 35.9 %copy-start.42 = (f32[3072]{0:T(1024)}, f32[3072]{0:T(1024)S(1)}, u32[]{:S(2)}) copy-start(f32[3072]{0:T(1024)S(1)} %broadcast_multiply_fusion.2) | copy-start | bytes 36868
  317.7 31.3 %copy-start.46 = (f32[3072]{0:T(1024)}, f32[3072]{0:T(1024)S(1)}, u32[]{:S(2)}) copy-start(f32[3072]{0:T(1024)S(1)} %multiply_reduce_fusion.7) | copy-start | bytes 36868
  406.4 112.9 %copy-start.44 = (f32[3072]{0:T(1024)}, f32[3072]{0:T(1024)S(1)}, u32[]{:S(2)}) copy-start(f32[3072]{0:T(1024)S(1)} %broadcast_multiply_fusion.1) | copy-start | bytes 36868
  411.7 107.6 %copy-start.57 = (f32[3072]{0:T(1024)}, f32[3072]{0:T(1024)S(1)}, u32[]{:S(2)}) copy-start(f32[3072]{0:T(1024)S(1)} %fusion.79) | copy-start | bytes 36868
  411.8 64.8 %copy-start.21 = (bf16[1,12,256,512]{3,2,1,0:T(8,128)(2,1)S(1)}, bf16[1,12,256,512]{3,2,1,0:T(8,128)(2,1)}, u32[]{:S(2)}) copy-start(bf16[1,12,256,512]{3,2,1,0:T(8,128)(2,1)} %param.30) | copy-start | bytes 9437188
  652.7 34.5 %copy-start.24 = (f32[128,8,12]{2,1,0:T(8,128)}, f32[128,8,12]{2,1,0:T(8,128)S(1)}, u32[]{:S(2)}) copy-start(f32[128,8,12]{2,1,0:T(8,128)S(1)} %log_add_fusion) | copy-start | bytes 147460
  716.5 199.6 %reduce-scatter.11.cloned.1.call-start = ((), (), s32[]{:S(2)}) async-start(), calls=%async_computation.13 | async-start | bytes 15728640 | tf_op jit(solution)/shard_map/reduce_scatter | solution.py:282
  747.2 306.7 %reduce-scatter.15.cloned.1.call-start = ((), (), s32[]{:S(2)}) async-start(), calls=%async_computation.15 | async-start | bytes 1081344 | tf_op jit(solution)/shard_map/reduce_scatter | solution.py:298
  754.0 433.4 %reduce-scatter.19.cloned.1.call-start = ((), (), s32[]{:S(2)}) async-start(), calls=%async_computation.17 | async-start | bytes 1081344 | tf_op jit(solution)/shard_map/reduce_scatter | solution.py:302
  759.3 531.6 %reduce-scatter.17.cloned.1.call-start = ((), (), s32[]{:S(2)}) async-start(), calls=%async_computation.16 | async-start | bytes 3244032 | tf_op jit(solution)/shard_map/reduce_scatter | solution.py:301
  772.2 661.4 %reduce-scatter.21.cloned.1.call-start = ((), (), s32[]{:S(2)}) async-start(), calls=%async_computation.18 | async-start | bytes 4325376 | tf_op jit(solution)/shard_map/reduce_scatter | solution.py:305
  787.8 785.6 %reduce-scatter.23.cloned.1.call-start = ((), (), s32[]{:S(2)}) async-start(), calls=%async_computation.19 | async-start | bytes 4325376 | tf_op jit(solution)/shard_map/reduce_scatter | solution.py:306
  799.1 877.5 %reduce-scatter.13.cloned.1.call-start = ((), (), s32[]{:S(2)}) async-start(), calls=%async_computation.14 | async-start | bytes 3244032 | tf_op jit(solution)/shard_map/reduce_scatter | solution.py:297
  800.9 41.7 %slice-start.5 = ((s8[6291456]{0:T(1024)(128)(4,1)}), s8[4194304]{0:T(1024)(128)(4,1)S(1)}, s32[]{:S(2)}) async-start(s8[6291456]{0:T(1024)(128)(4,1)} %bitcast.200), calls=%async_computation.27 | async-start | bytes 8388608
  803.4 39.2 %slice-start.6 = ((s8[6291456]{0:T(1024)(128)(4,1)}), s8[2097152]{0:T(1024)(128)(4,1)S(1)}, s32[]{:S(2)}) async-start(s8[6291456]{0:T(1024)(128)(4,1)} %bitcast.200), calls=%async_computation.28 | async-start | bytes 4194304
  (70 other events, 640.1 us)
Sparse Core Ops, SparseCore 0:
  10.9 57.6 all-gather.8
  106.2 90.8 all-gather.18
  198.7 82.0 all-gather.16
  283.5 54.9 all-gather.10
  341.2 55.2 all-gather.12
  399.2 55.2 all-gather.14
  716.6 97.7 reduce-scatter.8
  816.9 99.0 reduce-scatter.10
  918.9 135.0 reduce-scatter.14
  1056.7 130.7 reduce-scatter.18
  1193.4 97.4 reduce-scatter.16
  1293.6 139.9 reduce-scatter.20
  1436.4 136.9 reduce-scatter.22
  1579.3 97.3 reduce-scatter.12
where the time goes:
time: 1690 us; the launch traced here: 1680 us
  waiting for transfers between devices  753 us (45%)
  matrix products  424 us (25%)
  local copies, waits for them, and re-layouts  204 us (12%)
  blocking collectives  167 us (10%)
  other arithmetic  119 us (7%)
    reduce_scatter x1, waiting for transfers between devices, per_device(): lax.psum_scatter(up_grad, ('rows', 'feat'), scatter_dimension=0, tiled=True)  143 us
    reduce_scatter x1, waiting for transfers between devices, per_device(): lax.psum_scatter(down_grad, ('rows', 'feat'), scatter_dimension=0, tiled=...  140 us
    reduce_scatter x1, waiting for transfers between devices, per_device(): lax.psum_scatter(out_two_grad, ('rows', 'feat'), scatter_dimension=0, til...  134 us
    dot_general x6, matrix products, matmul(): return jnp.dot(left, right, preferred_element_type=jnp.float32)  104 us
    reduce_scatter x1, waiting for transfers between devices, per_device(): lax.psum_scatter(qkv_two_grad, ('rows', 'feat'), scatter_dimension=0, til...  103 us
    reduce_scatter x1, waiting for transfers between devices, per_device(): lax.psum_scatter(qkv_one_grad, ('rows', 'feat'), scatter_dimension=0, til...  103 us
    unnamed x2, blocking collectives  81.8 us
    dot_general x6, matrix products, by_rows(): lax.dot_general(left, right, (((1,), (1,)), ((), ())), preferred_element_...  72.1 us
  transfers between devices with their start and end apart: 14, of which 10 were waited for; matrix products, arithmetic and copies ran while one was open for 27% of the time, Pallas kernels for 0%

commit v1 on v0

v1 whole, which is shorter than its diff:
```python
import jax
import jax.numpy as jnp
import numpy as np
from jax import lax
from jax.experimental import pallas as pl
from jax.experimental.pallas import tpu as pltpu
from jax.sharding import PartitionSpec as P

D = 512
HEADS = 4
HEAD_DIM = 128
FF = 2048
QKV = 3 * D
EPS = 1e-05
MASKED = -1e30
SCALE = HEAD_DIM**-0.5
BF = jnp.bfloat16
F32 = jnp.float32
LOG2E = float(np.log2(np.e))
VMEM = 60 * 1024 * 1024

GRP2 = 4
GRP = 4
ROWS_P = 16
RC = 16
FCH = 512
FB = 2


def mm(a, b):
    return lax.dot_general(a, b, (((1,), (0,)), ((), ())), preferred_element_type=F32)


def mt(a, b):
    return lax.dot_general(a, b, (((1,), (1,)), ((), ())), preferred_element_type=F32)


def tm(a, b):
    return lax.dot_general(a, b, (((0,), (0,)), ((), ())), preferred_element_type=F32)


def norm(x):
    mean = jnp.mean(x, axis=-1, keepdims=True)
    centred = x - mean
    var = jnp.mean(centred * centred, axis=-1, keepdims=True)
    rstd = lax.rsqrt(var + EPS)
    return centred * rstd, rstd


def norm_back(n, xhat, rstd, gain):
    e = n * gain
    m1 = jnp.mean(e, axis=-1, keepdims=True)
    m2 = jnp.mean(e * xhat, axis=-1, keepdims=True)
    return rstd * (e - m1 - xhat * m2)


def fold8(a):
    return jnp.sum(a.reshape(a.shape[0] // 8, 8, a.shape[1]), axis=0)


def gelu_pair(h):
    e = jnp.exp2(h * h * (-0.5 * LOG2E))
    d = 1.0 + (0.3275911 * 2**-0.5) * jnp.abs(h)
    t = pl.reciprocal(d, approx=True)
    t = t * (2.0 - d * t)
    poly = 0.5 * 1.061405429
    for c in (-1.453152027, 1.421413741, -0.284496736, 0.254829592):
        poly = poly * t + 0.5 * c
    q = poly * t * e
    cdf = jnp.where(h >= 0, 1.0 - q, q)
    return h * cdf, cdf + h * e * (2 * np.pi) ** -0.5


def put_rows(ref, start, x):
    for c in range(HEADS):
        ref[c, start : start + x.shape[0]] = x[:, c * 128 : c * 128 + 128]


def get_row(ref, r, tot):
    return jnp.concatenate([ref[c, pl.ds(r, tot, stride=RC), :] for c in range(HEADS)], axis=1)


def full(shape):
    return pl.BlockSpec(shape, lambda *_: (0,) * len(shape), pipeline_mode=pl.Buffered(1))


def feature_forward_kernel(*refs, n, feats):
    x_refs, (gain, shift, wqkv, bias), outs = refs[:n], refs[n : n + 4], refs[n + 4 :]
    h_refs, (qkv_ref, p_ref), (xs, low, hs) = outs[:n], outs[n : n + 2], outs[n + 2 :]
    tot = n * feats
    pair = 2 * tot
    wide = bias.shape[1]
    for k in range(n):
        put_rows(xs, k * feats * RC, x_refs[k][...].reshape(feats * RC, D).astype(F32))
    for r in range(RC):
        xhat, _ = norm(get_row(xs, r, tot))
        low[r * tot : (r + 1) * tot] = (xhat * gain[...] + shift[...]).astype(BF)
    rows = tot * RC
    qkv_ref[0, :rows] = mm(low[...], wqkv[...]).astype(BF)
    qkv_ref[0, rows:] = jnp.zeros((qkv_ref.shape[1] - rows, QKV), BF)
    mask = bias[...]
    for b0 in range(0, RC // 2, GRP):
        jobs = [(b, h) for b in range(b0, b0 + GRP) for h in range(HEADS)]
        at = lambda b, h, c, w: (0, slice(b * pair, b * pair + w), slice(c * D + h * 128, c * D + h * 128 + 128))
        ss = [mt(qkv_ref[at(b, h, 0, pair)], qkv_ref[at(b, h, 1, wide)]) * (SCALE * LOG2E) + mask for b, h in jobs]
        es = [jnp.exp2(s - jnp.max(s, axis=-1, keepdims=True)) for s in ss]
        ps = [(e * (1.0 / jnp.sum(e, axis=-1, keepdims=True))).astype(BF) for e in es]
        os = [mm(p, qkv_ref[at(b, h, 2, wide)]) for p, (b, h) in zip(ps, jobs)]
        for p, o, (b, h) in zip(ps, os, jobs):
            p_ref[0, b, h] = p
            for j in range(2):
                hs[h, pl.ds(2 * b + j, tot, stride=RC), :] = o[j * tot : (j + 1) * tot]
    for k in range(n):
        for h in range(HEADS):
            h_refs[k][:, :, h * 128 : h * 128 + 128] = hs[h, k * feats * RC : (k + 1) * feats * RC].reshape(feats, RC, 128).astype(BF)


def feature_forward(xs, gain, shift, wqkv, bias):
    n = len(xs)
    feats, rows, _ = xs[0].shape
    tot = n * feats
    steps = rows // RC
    pad = tot * RC - 2 * tot + bias.shape[1]
    blk = pl.BlockSpec((feats, RC, D), lambda i: (0, i, 0))
    return pl.pallas_call(
        lambda *r: feature_forward_kernel(*r, n=n, feats=feats),
        grid=(steps,),
        in_specs=[blk] * n + [full((1, D)), full((1, D)), full((D, QKV)), full(bias.shape)],
        out_specs=[blk] * n
        + [
            pl.BlockSpec((1, pad, QKV), lambda i: (i, 0, 0)),
            pl.BlockSpec((1, RC // 2, HEADS, 2 * tot, bias.shape[1]), lambda i: (i, 0, 0, 0, 0)),
        ],
        out_shape=[jax.ShapeDtypeStruct((feats, rows, D), BF)] * n
        + [
            jax.ShapeDtypeStruct((steps, pad, QKV), BF),
            jax.ShapeDtypeStruct((steps, RC // 2, HEADS, 2 * tot, bias.shape[1]), BF),
        ],
        scratch_shapes=[
            pltpu.VMEM((HEADS, tot * RC, 128), F32),
            pltpu.VMEM((tot * RC, D), BF),
            pltpu.VMEM((HEADS, tot * RC, 128), F32),
        ],
        compiler_params=pltpu.CompilerParams(vmem_limit_bytes=VMEM),
        cost_estimate=pl.CostEstimate(flops=2 * tot * rows * D * QKV, bytes_accessed=24 * 10**6, transcendentals=0),
        name="feature_forward",
    )(*xs, gain, shift, wqkv, bias)


def feature_backward_kernel(*refs, n, feats):
    x_refs, g_refs, (qkv_ref, p_ref, gain, shift, wqkv), others, outs = refs[:n], refs[n : 2 * n], refs[2 * n : 2 * n + 5], refs[2 * n + 5 : 2 * n + 9], refs[2 * n + 9 :]
    d_refs, (dw_ref,), (dgain, dshift, vecs, xs, gs, ns, low, gh, gqkv, acc) = outs[:n], outs[n : n + 1], outs[n + 1 :]
    tot = n * feats
    pair = 2 * tot
    wide = p_ref.shape[-1]
    i = pl.program_id(0)

    @pl.when(i == 0)
    def _():
        acc[...] = jnp.zeros_like(acc)
        dgain[...] = jnp.zeros_like(dgain)
        dshift[...] = jnp.zeros_like(dshift)

    for k in range(n):
        put_rows(xs, k * feats * RC, x_refs[k][...].reshape(feats * RC, D).astype(F32))
        put_rows(gs, k * feats * RC, g_refs[k][...].reshape(feats * RC, D).astype(F32))
    for r in range(RC):
        gh[r * tot : (r + 1) * tot] = get_row(gs, r, tot).astype(BF)
        xhat, _ = norm(get_row(xs, r, tot))
        low[r * tot : (r + 1) * tot] = (xhat * gain[...] + shift[...]).astype(BF)
    for b0 in range(0, RC // 2, GRP):
        jobs = [(b, h) for b in range(b0, b0 + GRP) for h in range(HEADS)]
        at = lambda b, h, c, w: (0, slice(b * pair, b * pair + w), slice(c * D + h * 128, c * D + h * 128 + 128))
        gs_ = [gh[b * pair : (b + 1) * pair, h * 128 : h * 128 + 128] for b, h in jobs]
        dps = [mt(g, qkv_ref[at(b, h, 2, wide)]) for g, (b, h) in zip(gs_, jobs)]
        ps = [p_ref[0, b, h] for b, h in jobs]
        dvs = [tm(p, g) for p, g in zip(ps, gs_)]
        pds = [p.astype(F32) * dp for p, dp in zip(ps, dps)]
        dss = [(pd - p.astype(F32) * jnp.sum(pd, axis=-1, keepdims=True)).astype(BF) for p, pd in zip(ps, pds)]
        dqs = [mm(ds, qkv_ref[at(b, h, 1, wide)]) for ds, (b, h) in zip(dss, jobs)]
        dks = [tm(ds, qkv_ref[at(b, h, 0, pair)]) for ds, (b, h) in zip(dss, jobs)]
        for (b, h), dq, dk, dv in zip(jobs, dqs, dks, dvs):
            span = slice(b * pair, (b + 1) * pair)
            gqkv[span, h * 128 : h * 128 + 128] = (dq * SCALE).astype(BF)
            gqkv[span, D + h * 128 : D + h * 128 + 128] = (dk * SCALE).astype(BF)[:pair]
            gqkv[span, 2 * D + h * 128 : 2 * D + h * 128 + 128] = dv.astype(BF)[:pair]
    acc[...] += tm(low[...], gqkv[...])
    ns[...] = mt(gqkv[...], wqkv[...])
    for r in range(RC):
        xhat, rstd = norm(get_row(xs, r, tot))
        nn = ns[r * tot : (r + 1) * tot]
        dgain[...] += fold8(nn * xhat)
        dshift[...] += fold8(nn)
        d = norm_back(nn, xhat, rstd, gain[...])
        for c in range(HEADS):
            xs[c, pl.ds(r, tot, stride=RC), :] = d[:, c * 128 : c * 128 + 128]
    for k in range(n):
        for c in range(HEADS):
            d_refs[k][:, :, c * 128 : c * 128 + 128] = xs[c, k * feats * RC : (k + 1) * feats * RC].reshape(feats, RC, 128).astype(BF)

    @pl.when(i == pl.num_programs(0) - 1)
    def _():
        dw_ref[:, :QKV] = acc[...].astype(BF)
        vecs[...] = jnp.zeros_like(vecs)
        for j, v in enumerate((dgain, dshift) + others):
            vecs[j : j + 1] = jnp.sum(v[...], axis=0, keepdims=True)
        dw_ref[:, QKV:] = vecs[...].T.astype(BF)


def feature_backward(xs, gs, qkv, p, gain, shift, wqkv, others):
    n = len(xs)
    feats, rows, _ = xs[0].shape
    tot = n * feats
    steps = rows // RC
    blk = pl.BlockSpec((feats, RC, D), lambda i: (0, i, 0))
    return pl.pallas_call(
        lambda *r: feature_backward_kernel(*r, n=n, feats=feats),
        grid=(steps,),
        in_specs=[blk] * (2 * n)
        + [
            pl.BlockSpec((1,) + qkv.shape[1:], lambda i: (i, 0, 0)),
            pl.BlockSpec((1,) + p.shape[1:], lambda i: (i, 0, 0, 0, 0)),
            full((1, D)),
            full((1, D)),
            full((D, QKV)),
        ]
        + [full((8, D))] * 4,
        out_specs=[blk] * n + [pl.BlockSpec((D, QKV + 128), lambda i: (0, 0))],
        out_shape=[jax.ShapeDtypeStruct((feats, rows, D), BF)] * n + [jax.ShapeDtypeStruct((D, QKV + 128), BF)],
        scratch_shapes=[
            pltpu.VMEM((8, D), F32),
            pltpu.VMEM((8, D), F32),
            pltpu.VMEM((128, D), F32),
            pltpu.VMEM((HEADS, tot * RC, 128), F32),
            pltpu.VMEM((HEADS, tot * RC, 128), F32),
            pltpu.VMEM((tot * RC, D), F32),
            pltpu.VMEM((tot * RC, D), BF),
            pltpu.VMEM((tot * RC, D), BF),
            pltpu.VMEM((tot * RC, QKV), BF),
            pltpu.VMEM((D, QKV), F32),
        ],
        compiler_params=pltpu.CompilerParams(vmem_limit_bytes=VMEM),
        cost_estimate=pl.CostEstimate(flops=4 * tot * rows * D * QKV, bytes_accessed=30 * 10**6, transcendentals=0),
        name="feature_backward",
    )(*xs, *gs, qkv, p, gain, shift, wqkv, *others)


class Flat:
    def __init__(self, ref):
        self.ref = ref

    def __getitem__(self, key):
        rows, cols = (slice(None), slice(None)) if key is Ellipsis else key
        r = self.ref.shape[1]
        if rows.start is not None:
            rows = slice(rows.start // r, rows.stop // r)
        w = self.ref[rows, :, cols]
        return w.reshape(w.shape[0] * w.shape[1], w.shape[2])


def unpack_copies(pack, weights, sems):
    copies, at = [], 0
    for w in weights:
        r = w.shape[1]
        for j in range(w.shape[2] // D):
            src = pack.at[:, pl.ds(at, r), :]
            copies.append(pltpu.make_async_copy(src, w.at[:, :, pl.ds(j * D, D)], sems.at[len(copies)]))
            at += r
    return copies


def middle_kernel(me_ref, *refs, n, rows, part):
    it = iter(refs)
    take = lambda c: [next(it) for _ in range(c)]
    (x_ref,) = take(1)
    h_refs = take(n)
    cot_ref, bias, pack, g2, b2, g3, b3 = take(7)
    out_ref, gaf_ref = take(2)
    gh_refs = take(n)
    dpack, dg2, db2, dg3, db3 = take(5)
    h1_s, qkv_s, p_s, gq_s, heads_s, gh2_s, afo, arq, aro, ain, aout, wfo_s, wrq_s, wro_s, win_s, wout_s, sems = take(17)
    i = pl.program_id(0)
    me = me_ref[0]
    m = FB * rows

    @pl.when(i == 0)
    def _():
        copies = unpack_copies(pack, (wfo_s, wrq_s, wro_s, win_s, wout_s), sems)
        for c in copies:
            c.start()
        for a in (afo, arq, aro, ain, aout, dg2, db2, dg3, db3):
            a[...] = jnp.zeros_like(a)
        for c in copies:
            c.wait()

    wfo, wrq, wro, win, wout = (Flat(w) for w in (wfo_s, wrq_s, wro_s, win_s, wout_s))
    for k in range(n):
        off = pl.multiple_of((me ^ k) * part, part)
        for f in range(FB):
            h1_s[pl.ds(f * rows + off, part), :] = h_refs[k][f]
    x = x_ref[0].reshape(m, D).astype(F32)
    h1 = h1_s[...]
    after_feat = x + mm(h1, wfo[...])
    xhat2, rstd2 = norm(after_feat)
    low2 = (xhat2 * g2[...] + b2[...]).astype(BF)
    qkv_s[...] = mm(low2, wrq[...]).astype(BF)
    mask = bias[...]
    jobs = [(f, h) for f in range(FB) for h in range(HEADS)]
    at = lambda f, h, c: (slice(f * rows, (f + 1) * rows), slice(c * D + h * 128, c * D + h * 128 + 128))
    for g0 in range(0, len(jobs), GRP2):
        some = jobs[g0 : g0 + GRP2]
        ss = [mt(qkv_s[at(f, h, 0)], qkv_s[at(f, h, 1)]) * (SCALE * LOG2E) + mask for f, h in some]
        es = [jnp.exp2(s - jnp.max(s, axis=-1, keepdims=True)) for s in ss]
        ps = [(e * (1.0 / jnp.sum(e, axis=-1, keepdims=True))).astype(BF) for e in es]
        for p, (f, h) in zip(ps, some):
            p_s[f * HEADS + h] = p
            heads_s[at(f, h, 0)] = mm(p, qkv_s[at(f, h, 2)]).astype(BF)
    heads = heads_s[...]
    after_row = after_feat + mm(heads, wro[...])
    xhat3, rstd3 = norm(after_row)
    low3 = (xhat3 * g3[...] + b3[...]).astype(BF)
    cot = cot_ref[0].reshape(m, D)
    out = after_row
    n3 = None
    for j in range(FF // FCH):
        cols = slice(j * FCH, (j + 1) * FCH)
        act, slope = gelu_pair(mm(low3, win[:, cols]))
        act = act.astype(BF)
        out = out + mm(act, wout[cols, :])
        ghid = (mt(cot, wout[cols, :]) * slope).astype(BF)
        aout[:, cols] += tm(cot, act)
        ain[:, cols] += tm(low3, ghid)
        back = mt(ghid, win[:, cols])
        n3 = back if n3 is None else n3 + back
    out_ref[0] = out.astype(BF).reshape(FB, rows, D)
    dg3[...] += fold8(n3 * xhat3)
    db3[...] += fold8(n3)
    g_row = cot.astype(F32) + norm_back(n3, xhat3, rstd3, g3[...])
    gb = g_row.astype(BF)
    aro[...] += tm(heads, gb)
    gh2_s[...] = mt(gb, wro[...]).astype(BF)
    for g0 in range(0, len(jobs), GRP2):
        some = jobs[g0 : g0 + GRP2]
        gs = [gh2_s[at(f, h, 0)] for f, h in some]
        ps = [p_s[f * HEADS + h] for f, h in some]
        dps = [mt(g, qkv_s[at(f, h, 2)]) for g, (f, h) in zip(gs, some)]
        pds = [p.astype(F32) * dp for p, dp in zip(ps, dps)]
        dss = [(pd - p.astype(F32) * jnp.sum(pd, axis=-1, keepdims=True)).astype(BF) for p, pd in zip(ps, pds)]
        for (f, h), g, p, ds in zip(some, gs, ps, dss):
            gq_s[at(f, h, 2)] = tm(p, g).astype(BF)
            gq_s[at(f, h, 0)] = (mm(ds, qkv_s[at(f, h, 1)]) * SCALE).astype(BF)
            gq_s[at(f, h, 1)] = (tm(ds, qkv_s[at(f, h, 0)]) * SCALE).astype(BF)
    gq = gq_s[...]
    arq[...] += tm(low2, gq)
    n2 = mt(gq, wrq[...])
    dg2[...] += fold8(n2 * xhat2)
    db2[...] += fold8(n2)
    g_feat = g_row + norm_back(n2, xhat2, rstd2, g2[...])
    gaf_ref[...] = g_feat.reshape(FB, rows, D)
    gf = g_feat.astype(BF)
    afo[...] += tm(h1, gf)
    h1_s[...] = mt(gf, wfo[...]).astype(BF)
    for k in range(n):
        off = pl.multiple_of((me ^ k) * part, part)
        for f in range(FB):
            gh_refs[k][f] = h1_s[pl.ds(f * rows + off, part), :]

    @pl.when(i == pl.num_programs(0) - 1)
    def _():
        at = 0
        for acc in (afo, arq, aro, ain):
            for j in range(acc.shape[1] // D):
                dpack[:, at : at + ROWS_P, :] = acc[:, j * D : (j + 1) * D].astype(BF).reshape(D // ROWS_P, ROWS_P, D)
                at += ROWS_P
        for j in range(FF // D):
            dpack[j * 8 : (j + 1) * 8, at:, :] = aout[:, j * D : (j + 1) * D].T.astype(BF).reshape(8, 4 * ROWS_P, D)


def middle(me, x, hs, cot, bias, pack, g2, b2, g3, b3):
    n = len(hs)
    _, feats, rows, _ = x.shape
    part = rows // n
    m = FB * rows
    xblk = pl.BlockSpec((1, FB, rows, D), lambda i, me: (0, i, 0, 0))
    hblk = pl.BlockSpec((FB, part, D), lambda i, me: (i, 0, 0))
    acc = lambda *s: pl.BlockSpec(s, lambda i, me: (0, 0))
    sds = jax.ShapeDtypeStruct
    return pl.pallas_call(
        lambda *r: middle_kernel(*r, n=n, rows=rows, part=part),
        grid_spec=pltpu.PrefetchScalarGridSpec(
            num_scalar_prefetch=1,
            grid=(feats // FB,),
            in_specs=[xblk]
            + [hblk] * n
            + [
                xblk,
                full((rows, rows)),
                pl.BlockSpec(memory_space=pl.ANY),
                full((1, D)),
                full((1, D)),
                full((1, D)),
                full((1, D)),
            ],
            out_specs=[xblk, pl.BlockSpec((FB, rows, D), lambda i, me: (i, 0, 0))]
            + [hblk] * n
            + [pl.BlockSpec(pack.shape, lambda i, me: (0, 0, 0))]
            + [acc(8, D)] * 4,
            scratch_shapes=[
                pltpu.VMEM((m, D), BF),
                pltpu.VMEM((m, QKV), BF),
                pltpu.VMEM((FB * HEADS, rows, rows), BF),
                pltpu.VMEM((m, QKV), BF),
                pltpu.VMEM((m, D), BF),
                pltpu.VMEM((m, D), BF),
                pltpu.VMEM((D, D), F32),
                pltpu.VMEM((D, QKV), F32),
                pltpu.VMEM((D, D), F32),
                pltpu.VMEM((D, FF), F32),
                pltpu.VMEM((D, FF), F32),
                pltpu.VMEM((32, ROWS_P, D), BF),
                pltpu.VMEM((32, ROWS_P, QKV), BF),
                pltpu.VMEM((32, ROWS_P, D), BF),
                pltpu.VMEM((32, ROWS_P, FF), BF),
                pltpu.VMEM((32, 4 * ROWS_P, D), BF),
                pltpu.SemaphoreType.DMA((10,)),
            ],
        ),
        out_shape=[sds(x.shape, BF), sds((feats, rows, D), F32)]
        + [sds((feats, part, D), BF)] * n
        + [sds(pack.shape, BF)]
        + [sds((8, D), F32)] * 4,
        compiler_params=pltpu.CompilerParams(vmem_limit_bytes=VMEM),
        cost_estimate=pl.CostEstimate(flops=70 * 10**9, bytes_accessed=50 * 10**6, transcendentals=0),
        name="middle",
    )(me, x, *hs, cot, bias, pack, g2, b2, g3, b3)


def final_kernel(me_ref, g_ref, *refs, n, part):
    d_refs, out = refs[:n], refs[n]
    me = me_ref[0]
    for k in range(n):
        off = pl.multiple_of((me ^ k) * part, part)
        out[0, :, pl.ds(off, part), :] = g_ref[:, pl.ds(off, part), :] + d_refs[k][...].astype(F32)


def final(me, g, ds):
    n = len(ds)
    feats, rows, _ = g.shape
    part = rows // n
    fb = 3
    return pl.pallas_call(
        lambda *r: final_kernel(*r, n=n, part=part),
        grid_spec=pltpu.PrefetchScalarGridSpec(
            num_scalar_prefetch=1,
            grid=(feats // fb,),
            in_specs=[pl.BlockSpec((fb, rows, D), lambda i, me: (i, 0, 0))] + [pl.BlockSpec((fb, part, D), lambda i, me: (i, 0, 0))] * n,
            out_specs=pl.BlockSpec((1, fb, rows, D), lambda i, me: (0, i, 0, 0)),
        ),
        out_shape=jax.ShapeDtypeStruct((1, feats, rows, D), F32),
        compiler_params=pltpu.CompilerParams(vmem_limit_bytes=VMEM),
        name="final",
    )(me, g, *ds)


def row_allowed(segments, context):
    tables = jnp.arange(context.shape[0], dtype=jnp.int32)
    member = (segments[:, None] == tables[None, :]).astype(jnp.int32)
    sizes = jnp.sum(member, axis=0)
    starts = jnp.cumsum(sizes) - sizes
    places = jnp.arange(segments.shape[0], dtype=jnp.int32) - jnp.sum(member * starts[None, :], axis=1)
    limits = jnp.sum(member * context[None, :], axis=1)
    usable = places < limits
    return (segments[:, None] == segments[None, :]) & usable[None, :]


def swap(arrays, n):
    return [arrays[0]] + [lax.ppermute(arrays[k], "feat", [(d, d ^ k) for d in range(n)]) for k in range(1, n)]


class Shards:
    def __init__(self, rows, n):
        self.count = rows * n
        self.bits = [("rows", 1 << b) for b in reversed(range(rows.bit_length() - 1))]
        self.bits += [("feat", 1 << b) for b in reversed(range(n.bit_length() - 1))]
        self.sizes = {"rows": rows, "feat": n}
        last = len(self.bits) - 1
        self.rows_bits = list(range(rows.bit_length() - 1))
        self.near = last
        self.feat_bits = list(range(rows.bit_length() - 1, last))

    def other(self, a, at):
        axis, bit = self.bits[at]
        return lax.ppermute(a, axis, [(d, d ^ bit) for d in range(self.sizes[axis])])

    def side(self, at):
        axis, bit = self.bits[at]
        return (lax.axis_index(axis) // bit) % 2

    def gather(self, a, order):
        shape = a.shape
        a = a.reshape((1,) * len(self.bits) + shape)
        for at in order:
            b = self.other(a, at)
            low = self.side(at) == 0
            a = jnp.concatenate([jnp.where(low, a, b), jnp.where(low, b, a)], axis=at)
        return a.reshape((self.count,) + shape)

    def scatter(self, a, order):
        shape = a.shape[1:]
        a = a.reshape((2,) * len(self.bits) + shape)
        for step, at in enumerate(order):
            side = self.side(at)
            sent = self.other(lax.dynamic_index_in_dim(a, 1 - side, at, True), at)
            a = lax.dynamic_index_in_dim(a, side, at, True).astype(F32) + sent.astype(F32)
            if step < len(order) - 1:
                a = a.astype(BF)
        return a.reshape(shape)


def pack_shards(mats, down):
    return jnp.concatenate([m[:, j * D : (j + 1) * D] for m in mats for j in range(m.shape[1] // D)] + [down], axis=0)


def repack(a, blocks):
    count = a.shape[0]
    if count == blocks:
        return a
    r, q = D // count, D // blocks
    parts = [a[:, j * r : (j + 1) * r].reshape(blocks, q, D) for j in range(9)]
    return jnp.concatenate(parts + [a[:, 9 * r :].reshape(blocks, 4 * q, D)], axis=1)


def per_device(rows_axis, n, inputs, *rest):
    weights, (cotangent, segments, context, feature_mask) = rest[:12], rest[12:]
    gain_one, shift_one, qkv_one, out_one, gain_two, shift_two, qkv_two, out_two, gain_three, shift_three, up, down = weights
    shards = Shards(rows_axis, n)
    _, feats, rows, _ = inputs.shape
    part = rows // n
    tot = n * feats
    me = lax.axis_index("feat").astype(jnp.int32)
    me_arr = me.reshape(1)

    vectors = jnp.stack((gain_one, shift_one, gain_two, shift_two, gain_three, shift_three), axis=1)
    first = jnp.concatenate([qkv_one, jnp.pad(vectors, ((0, 0), (0, 128 - 6)))], axis=1)
    first = shards.gather(first, shards.feat_bits + shards.rows_bits + [shards.near]).reshape(D, QKV + 128)
    pack = lax.all_gather(pack_shards((out_one, qkv_two, out_two, up), down), ("rows", "feat"), axis=0)
    pack = repack(pack, D // ROWS_P)
    gains = first[:, QKV : QKV + 6].astype(F32).T
    g1, b1, g2, b2, g3, b3 = [gains[j : j + 1] for j in range(6)]

    mine = [lax.dynamic_slice(inputs[0], (0, (me ^ k) * part, 0), (feats, part, D)) for k in range(n)]
    xs = swap(mine, n)
    order = me ^ jnp.arange(n, dtype=jnp.int32)
    valid = jnp.take(feature_mask[0].reshape(n, feats), order, axis=0).reshape(tot) > 0
    wide = -(-2 * tot // 128) * 128
    lane = jnp.arange(wide)
    same = (lane[None, :] // tot == jnp.arange(2 * tot)[:, None] // tot) & (lane < 2 * tot)[None, :]
    bias_one = jnp.where(same & jnp.pad(jnp.tile(valid, 2), (0, wide - 2 * tot))[None, :], 0.0, MASKED).astype(F32)
    bias_two = jnp.where(row_allowed(segments[0], context[0]), 0.0, MASKED).astype(F32)

    *heads, qkv, p = feature_forward(xs, g1, b1, first, bias_one)
    hs = swap(heads, n)
    res = middle(me_arr, inputs, hs, cotangent, bias_two, pack, g2, b2, g3, b3)
    output, gaf, gh = res[0], res[1], res[2 : 2 + n]
    dpack, dg2, db2, dg3, db3 = res[2 + n :]
    gs = swap(gh, n)
    *dx, dfirst = feature_backward(xs, gs, qkv, p, g1, b1, first, (dg2, db2, dg3, db3))
    back = swap(dx, n)
    input_grad = final(me_arr, gaf, back)

    down_order = [shards.near] + shards.rows_bits[::-1] + shards.feat_bits
    dpack = shards.scatter(repack(dpack, shards.count), down_order)
    dfirst = shards.scatter(dfirst.reshape(shards.count, -1, QKV + 128), down_order)
    r = D // shards.count
    cut = lambda a, b: jnp.concatenate([dpack[j * r : (j + 1) * r] for j in range(a, b)], axis=1)
    v = [dfirst[:, QKV + j] for j in range(6)]
    return (output, input_grad, v[0], v[1], dfirst[:, :QKV], cut(0, 1), v[2], v[3], cut(1, 4), cut(4, 5), v[4], v[5], cut(5, 9), dpack[9 * r :])


def solution(mesh):
    rows_axis, n = mesh.shape["rows"], mesh.shape["feat"]
    vec, mat, act, tab = P(("rows", "feat")), P(("rows", "feat"), None), P("rows", "feat", None, None), P("rows", None)
    weights = (vec, vec, mat, mat, vec, vec, mat, mat, vec, vec, mat, mat)
    return jax.shard_map(
        lambda *a: per_device(rows_axis, n, *a),
        mesh=mesh,
        in_specs=(act,) + weights + (act, tab, tab, tab),
        out_specs=(act, act) + weights,
        check_vma=False,
    )
```

time: 1690 us -> 485 us (0.29)
  waiting for transfers between devices: 753 us -> 196 us
  matrix products: 424 us -> 0 us
  Pallas kernels: 0 us -> 189 us
  local copies, waits for them, and re-layouts: 204 us -> 30.9 us
  blocking collectives: 167 us -> 0 us
  other arithmetic: 119 us -> 20.9 us
  starting transfers between devices: 0.74 us -> 29 us
    reduce_scatter x8 -> x0, waiting for transfers between devices: 707 us -> none  [the longest x1 143 us: per_device(): lax.psum_scatter(up_grad, ('rows', 'feat'), scatter_dimension=0, tiled=True)]
    dot_general x30 -> x0, matrix products: 424 us -> none  [the longest x6 104 us: matmul(): return jnp.dot(left, right, preferred_element_type=jnp.float32)]
    ppermute x0 -> x27, waiting for transfers between devices: none -> 196 us  [the longest x12 104 us: swap(): lax.ppermute(arrays[k], 'feat', [(d, d ^ k) for d in range(n)])]
    pallas_call x0 -> x4, Pallas kernels: none -> 189 us  [the longest x1 127 us: middle(): pl.pallas_call(lambda *r: middle_kernel(*r, n=n, rows=rows, part=part), g...]
    all_gather x2 -> x0, blocking collectives: 85.6 us -> none  [the longest x1 44.2 us: per_device(): lax.all_gather(shards[3], ('rows', 'feat'), axis=0, tiled=True)]
    unnamed x2 -> x0, blocking collectives: 81.8 us -> none
    convert_element_type x7 -> x0, local copies, waits for them, and re-layouts: 77.2 us -> none  [the longest x3 44.3 us: per_device(): grad_qkv = jnp.stack((grad_query, grad_key, grad_value), axis=3).astype(j...]
    reduce_sum x11 -> x2, other arithmetic: 51.7 us -> 0.2 us  [the longest x1 0.12 us: row_allowed(): sizes = jnp.sum(member, axis=0)]
  transfers between devices with their start and end apart: 14 -> 28, of which waited for: 10 -> 16; matrix products, arithmetic and copies ran while one was open for 27% -> 7% of each run, Pallas kernels for 0% -> 13%
where the time goes in v1:
time: 485 us; the launch traced here: 480 us
  waiting for transfers between devices  196 us (40%)
  Pallas kernels  189 us (39%)
  local copies, waits for them, and re-layouts  30.9 us (6%)
  starting transfers between devices  29 us (6%)
  other arithmetic  20.9 us (4%)
  between operations  14.4 us (3%)
    pallas_call x1, Pallas kernels, middle(): pl.pallas_call(lambda *r: middle_kernel(*r, n=n, rows=rows, part=part), g...  127 us
    ppermute x12, waiting for transfers between devices, swap(): lax.ppermute(arrays[k], 'feat', [(d, d ^ k) for d in range(n)])  104 us
    ppermute x15, waiting for transfers between devices, other(): lax.ppermute(a, axis, [(d, d ^ bit) for d in range(self.sizes[axis])])  91.2 us
    pallas_call x1, Pallas kernels, feature_backward(): pl.pallas_call(lambda *r: feature_backward_kernel(*r, n=n, feats=feats),...  34.8 us
    ppermute x15, starting transfers between devices, other(): lax.ppermute(a, axis, [(d, d ^ bit) for d in range(self.sizes[axis])])  21.1 us
    pallas_call x1, Pallas kernels, feature_forward(): pl.pallas_call(lambda *r: feature_forward_kernel(*r, n=n, feats=feats), g...  21 us
    unnamed x55, local copies, waits for them, and re-layouts  11.7 us
    convert_element_type x8, other arithmetic, scatter(): a = a.astype(BF)  10.1 us
  transfers between devices with their start and end apart: 28, of which 16 were waited for; matrix products, arithmetic and copies ran while one was open for 7% of the time, Pallas kernels for 13%

profile of v1, /device:TPU:0, one launch (start us, length us, event | category | flops | bytes accessed | tf_op | source)
XLA Modules:
  0.0 480.1 jit_solution(9016029794608238007)
XLA Ops:
  17.1 2.9 collective-permute-start.3
  20.0 2.1 collective-permute-done.3
  23.0 3.2 collective-permute-start.4
  26.2 3.7 collective-permute-done.4
  31.6 2.7 collective-permute-start.5
  34.3 5.4 %collective-permute-done.5 = bf16[2,1,1,2,1,16,1664]{6,5,4,3,2,1,0:T(8,128)(2,1)} collective-permute-done((bf16[2,1,1,2,1,16,1664]{6,5,4,3,2,1,0:T(8,128)(2,1)}, bf16[2,1,1,2,1,16,1664]{6,5,4,3,2,1,0:T(8,128)(2,1)}, u32[]{:S(2)}, u32[]{:S(2)}) %collective-permute-start.5) | collective-permute-done | bytes 213024 | tf_op jit(solution)/shard_map/ppermute | solution.py:493
  42.2 2.0 collective-permute-start.6
  44.2 1.8 dynamic-slice_bitcast_fusion
  49.7 4.4 collective-permute-done.6
  60.0 10.6 %collective-permute-done.1.r_2_ = bf16[12,64,512]{2,1,0:T(8,128)(2,1)} collective-permute-done((bf16[12,64,512]{2,1,0:T(8,128)(2,1)}, bf16[12,64,512]{2,1,0:T(8,128)(2,1)}, u32[]{:S(2)}, u32[]{:S(2)}) %collective-permute-start.1) | collective-permute-done | bytes 786464 | tf_op jit(solution)/shard_map/ppermute | solution.py:477
  70.5 28.6 %collective-permute-done.2.r_3_ = bf16[12,64,512]{2,1,0:T(8,128)(2,1)} collective-permute-done((bf16[12,64,512]{2,1,0:T(8,128)(2,1)}, bf16[12,64,512]{2,1,0:T(8,128)(2,1)}, u32[]{:S(2)}, u32[]{:S(2)}) %collective-permute-start.2) | collective-permute-done | bytes 786464 | tf_op jit(solution)/shard_map/ppermute | solution.py:477
  99.2 21.0 %feature_forward.1 = (bf16[12,64,512]{2,1,0:T(8,128)(2,1)}, bf16[12,64,512]{2,1,0:T(8,128)(2,1)}, bf16[12,64,512]{2,1,0:T(8,128)(2,1)}, bf16[12,64,512]{2,1,0:T(...) custom-call(bf16[12,64,512]{2,1,0:T(8,128)(2,1)} %get-tuple-element.69.r_0_, ...), custom_call_target="tpu_custom_call" | custom-call | flops 4831838208 | bytes 24000000 | tf_op jit(solution)/shard_map/feature_forward/pallas_call | solution.py:125
  120.7 1.7 collective-permute-start.9
  126.1 13.8 %collective-permute-done.10.r_5_ = bf16[12,64,512]{2,1,0:T(8,128)(2,1)S(1)} collective-permute-done((bf16[12,64,512]{2,1,0:T(8,128)(2,1)}, bf16[12,64,512]{2,1,0:T(8,128)(2,1)S(1)}, u32[]{:S(2)}, u32[]{:S(2)}) %collective-permute-start.10) | collective-permute-done | bytes 786464 | tf_op jit(solution)/shard_map/ppermute | solution.py:477
  139.9 17.4 %collective-permute-done.9.r_4_ = bf16[12,64,512]{2,1,0:T(8,128)(2,1)} collective-permute-done((bf16[12,64,512]{2,1,0:T(8,128)(2,1)}, bf16[12,64,512]{2,1,0:T(8,128)(2,1)}, u32[]{:S(2)}, u32[]{:S(2)}) %collective-permute-start.9) | collective-permute-done | bytes 786464 | tf_op jit(solution)/shard_map/ppermute | solution.py:477
  157.3 126.6 %middle.1 = (bf16[1,12,256,512]{3,2,1,0:T(8,128)(2,1)}, f32[12,256,512]{2,1,0:T(8,128)}, bf16[12,64,512]{2,1,0:T(8,128)(2,1)}, bf16[12,64,512]{2,1,0:T(8,128)(2,...) custom-call(s32[1]{0:T(128)} %bitcast.r_0_, ...), custom_call_target="tpu_custom_call" | custom-call | flops 70000001024 | bytes 50000000 | tf_op jit(solution)/shard_map/middle/pallas_call | solution.py:388
  283.9 2.5 constant_dynamic-slice_fusion.4
  288.4 4.8 %collective-permute-done.11.r_5_ = bf16[12,64,512]{2,1,0:T(8,128)(2,1)S(1)} collective-permute-done((bf16[12,64,512]{2,1,0:T(8,128)(2,1)S(1)}, bf16[12,64,512]{2,1,0:T(8,128)(2,1)S(1)}, u32[]{:S(2)}, u32[]{:S(2)}) %collective-permute-start.11) | collective-permute-done | bytes 786464 | tf_op jit(solution)/shard_map/ppermute | solution.py:477
  293.2 14.1 %collective-permute-done.12.r_6_ = bf16[12,64,512]{2,1,0:T(8,128)(2,1)S(1)} collective-permute-done((bf16[12,64,512]{2,1,0:T(8,128)(2,1)S(1)}, bf16[12,64,512]{2,1,0:T(8,128)(2,1)S(1)}, u32[]{:S(2)}, u32[]{:S(2)}) %collective-permute-start.12) | collective-permute-done | bytes 786464 | tf_op jit(solution)/shard_map/ppermute | solution.py:477
  307.3 15.1 %collective-permute-done.13.r_7_ = bf16[12,64,512]{2,1,0:T(8,128)(2,1)S(1)} collective-permute-done((bf16[12,64,512]{2,1,0:T(8,128)(2,1)S(1)}, bf16[12,64,512]{2,1,0:T(8,128)(2,1)S(1)}, u32[]{:S(2)}, u32[]{:S(2)}) %collective-permute-start.13) | collective-permute-done | bytes 786464 | tf_op jit(solution)/shard_map/ppermute | solution.py:477
  323.3 34.8 %feature_backward.1 = (bf16[12,64,512]{2,1,0:T(8,128)(2,1)}, bf16[12,64,512]{2,1,0:T(8,128)(2,1)}, bf16[12,64,512]{2,1,0:T(8,128)(2,1)}, bf16[12,64,512]{2,1,0:T(8,128)(2,1)}, bf16[512,1664]{1,0:T(8,128)(2,1)}) custom-call(bf16[12,64,512]{2,1,0:T(8,128)(2,1)} %get-tuple-element.69.r_0_, bf16[12,64,512]{2,1,0:T(8,128)(2,1)} %collective-permute-done.r_1_, ...), custom_call_target="tpu_custom_call" | custom-call | flops 9663676416 | bytes 30000000 | tf_op jit(solution)/shard_map/feature_backward/pallas_call | solution.py:216
  358.1 2.2 constant_dynamic-slice_fusion.9
  361.0 4.2 add_convert_fusion
  366.5 1.6 collective-permute-start.23
  373.8 41.3 %collective-permute-done.18 = bf16[2,2,1,2,1,16,1664]{6,5,4,3,2,1,0:T(8,128)(2,1)} collective-permute-done((bf16[2,2,1,2,1,16,1664]{6,5,4,3,2,1,0:T(8,128)(2,1)}, bf16[2,2,1,2,1,16,1664]{6,5,4,3,2,1,0:T(8,128)(2,1)}, u32[]{:S(2)}, u32[]{:S(2)}) %collective-permute-start.18) | collective-permute-done | bytes 426016 | tf_op jit(solution)/shard_map/ppermute | solution.py:493
  418.6 1.9 add_convert_fusion.1
  422.5 6.8 %final.1 = f32[1,12,256,512]{3,2,1,0:T(8,128)} custom-call(s32[1]{0:T(128)} %bitcast.r_0_, f32[12,256,512]{2,1,0:T(8,128)} %get-tuple-element.41.r_1_, bf16[12,64,512]{2,1,0:T(8,128)(2,1)} %get-tuple-element.52.r_2_, bf16[12,64,512]{2,1,0:T(8,128)(2,1)} %collective-permute-done.14.r_3_, bf16[12,64,512]{2,1,0:T(8,128)(2,1)} %collective-permute-done.15.r_4_, ...), custom_call_target="tpu_custom_call" | custom-call | tf_op jit(solution)/shard_map/final/pallas_call | solution.py:451
  430.3 2.5 collective-permute-start.20
  432.8 11.4 %collective-permute-done.24 = bf16[2,1,1,2,1,208,512]{6,5,4,3,2,1,0:T(8,128)(2,1)S(1)} collective-permute-done((bf16[2,1,1,2,1,208,512]{6,5,4,3,2,1,0:T(8,128)(2,1)S(1)}, bf16[2,1,1,2,1,208,512]{6,5,4,3,2,1,0:T(8,128)(2,1)S(1)}, u32[]{:S(2)}, u32[]{:S(2)}) %collective-permute-start.24) | collective-permute-done | bytes 852000 | tf_op jit(solution)/shard_map/ppermute | solution.py:493
  444.5 1.5 collective-permute-start.25
  446.8 17.7 %collective-permute-done.25 = bf16[1,1,1,2,1,208,512]{6,5,4,3,2,1,0:T(8,128)(2,1)S(1)} collective-permute-done((bf16[1,1,1,2,1,208,512]{6,5,4,3,2,1,0:T(8,128)(2,1)S(1)}, bf16[1,1,1,2,1,208,512]{6,5,4,3,2,1,0:T(8,128)(2,1)S(1)}, u32[]{:S(2)}, u32[]{:S(2)}) %collective-permute-start.25) | collective-permute-done | bytes 426016 | tf_op jit(solution)/shard_map/ppermute | solution.py:493
  466.5 4.1 collective-permute-done.26
  (153 shorter events, 51.3 us)
Async XLA Ops:
  7.2 37.0 %copy-start.3 = (bf16[1,12,256,512]{3,2,1,0:T(8,128)(2,1)S(1)}, bf16[1,12,256,512]{3,2,1,0:T(8,128)(2,1)}, u32[]{:S(2)}) copy-start(bf16[1,12,256,512]{3,2,1,0:T(8,128)(2,1)} %r_1_.1) | copy-start | bytes 9437188
  7.2 150.1 %all-gather.3.cloned.1.call-start = ((), (), s32[]{:S(2)}) async-start(), calls=%async_computation | async-start | bytes 7028736 | tf_op jit(solution)/shard_map/all_gather | solution.py:546
  17.1 5.0 %collective-permute-start.3 = (bf16[1,1,1,1,1,16,1664]{6,5,4,3,2,1,0:T(8,128)(2,1)S(1)}, bf16[1,1,1,1,1,16,1664]{6,5,4,3,2,1,0:T(8,128)(2,1)S(1)}, u32[]{:S(2)}, u32[]{:S(2)}) collective-permute-start(bf16[1,1,1,1,1,16,1664]{6,5,4,3,2,1,0:T(8,128)(2,1)S(1)} %fusion.2), channel_id=1, source_target_pairs={{0,2},{1,3},{2,0},{3,1},{4,6},{5,7},{6,4},{7,5},{8,10},{9,11},{10,... | collective-permute-start | bytes 159752 | tf_op jit(solution)/shard_map/ppermute | solution.py:493
  23.0 6.9 %collective-permute-start.4 = (bf16[1,1,1,2,1,16,1664]{6,5,4,3,2,1,0:T(8,128)(2,1)S(1)}, bf16[1,1,1,2,1,16,1664]{6,5,4,3,2,1,0:T(8,128)(2,1)}, u32[]{:S(2)}, u32[]{:S(2)}) collective-permute-start(bf16[1,1,1,2,1,16,1664]{6,5,4,3,2,1,0:T(8,128)(2,1)S(1)} %pad_maximum_fusion.5), channel_id=1, source_target_pairs={{0,16},{4,20},{8,24},{12,28},{16,0},{20,4},{24,8},{28,12},{1,17},{... | collective-permute-start | bytes 319496 | tf_op jit(solution)/shard_map/ppermute | solution.py:493
  31.6 8.1 %collective-permute-start.5 = (bf16[2,1,1,2,1,16,1664]{6,5,4,3,2,1,0:T(8,128)(2,1)}, bf16[2,1,1,2,1,16,1664]{6,5,4,3,2,1,0:T(8,128)(2,1)}, u32[]{:S(2)}, u32[]{:S(2)}) collective-permute-start(bf16[2,1,1,2,1,16,1664]{6,5,4,3,2,1,0:T(8,128)(2,1)} %pad_maximum_fusion.3), channel_id=1, source_target_pairs={{0,8},{4,12},{8,0},{12,4},{16,24},{20,28},{24,16},{28,20},{1,9},{5... | collective-permute-start | bytes 638984 | tf_op jit(solution)/shard_map/ppermute | solution.py:493
  42.2 11.9 %collective-permute-start.6 = (bf16[2,2,1,2,1,16,1664]{6,5,4,3,2,1,0:T(8,128)(2,1)}, bf16[2,2,1,2,1,16,1664]{6,5,4,3,2,1,0:T(8,128)(2,1)}, u32[]{:S(2)}, u32[]{:S(2)}) collective-permute-start(bf16[2,2,1,2,1,16,1664]{6,5,4,3,2,1,0:T(8,128)(2,1)} %pad_maximum_fusion.2), channel_id=1, source_target_pairs={{0,4},{4,0},{8,12},{12,8},{16,20},{20,16},{24,28},{28,24},{1,5},{5... | collective-permute-start | bytes 1277960 | tf_op jit(solution)/shard_map/ppermute | solution.py:493
  46.0 14.0 %collective-permute-start = (bf16[12,64,512]{2,1,0:T(8,128)(2,1)}, bf16[12,64,512]{2,1,0:T(8,128)(2,1)}, u32[]{:S(2)}, u32[]{:S(2)}) collective-permute-start(bf16[12,64,512]{2,1,0:T(8,128)(2,1)} %get-tuple-element.68), channel_id=1, source_target_pairs={{0,1},{1,0},{2,3},{3,2},{4,5},{5,4},{6,7},{7,6},{8,9},{9,8},{10,11... | collective-permute-start | bytes 2359304 | tf_op jit(solution)/shard_map/ppermute | solution.py:477
  46.0 24.6 %collective-permute-start.1 = (bf16[12,64,512]{2,1,0:T(8,128)(2,1)}, bf16[12,64,512]{2,1,0:T(8,128)(2,1)}, u32[]{:S(2)}, u32[]{:S(2)}) collective-permute-start(bf16[12,64,512]{2,1,0:T(8,128)(2,1)} %get-tuple-element.67), channel_id=1, source_target_pairs={{0,2},{1,3},{2,0},{3,1},{4,6},{5,7},{6,4},{7,5},{8,10},{9,11},{10,... | collective-permute-start | bytes 2359304 | tf_op jit(solution)/shard_map/ppermute | solution.py:477
  47.4 51.7 %collective-permute-start.2 = (bf16[12,64,512]{2,1,0:T(8,128)(2,1)}, bf16[12,64,512]{2,1,0:T(8,128)(2,1)}, u32[]{:S(2)}, u32[]{:S(2)}) collective-permute-start(bf16[12,64,512]{2,1,0:T(8,128)(2,1)} %get-tuple-element.66), channel_id=1, source_target_pairs={{0,3},{1,2},{2,1},{3,0},{4,7},{5,6},{6,5},{7,4},{8,11},{9,10},{10,... | collective-permute-start | bytes 2359304 | tf_op jit(solution)/shard_map/ppermute | solution.py:477
  55.3 2.4 collective-permute-start.7
  58.2 41.0 %copy-start.4 = (bf16[2,2,2,2,2,16,1664]{6,5,4,3,2,1,0:T(8,128)(2,1)}, bf16[2,2,2,2,2,16,1664]{6,5,4,3,2,1,0:T(8,128)(2,1)S(1)}, u32[]{:S(2)}) copy-start(bf16[2,2,2,2,2,16,1664]{6,5,4,3,2,1,0:T(8,128)(2,1)S(1)} %pad_maximum_fusion) | copy-start | bytes 5111812
  99.2 23.2 %copy-start.12 = (s32[1,4]{1,0:T(1,128)S(1)}, s32[1,4]{1,0:T(1,128)}, u32[]{:S(2)}) copy-start(s32[1,4]{1,0:T(1,128)} %param.32) | copy-start | bytes 52
  120.2 19.7 %collective-permute-start.10 = (bf16[12,64,512]{2,1,0:T(8,128)(2,1)}, bf16[12,64,512]{2,1,0:T(8,128)(2,1)S(1)}, u32[]{:S(2)}, u32[]{:S(2)}) collective-permute-start(bf16[12,64,512]{2,1,0:T(8,128)(2,1)} %get-tuple-element.39), channel_id=1, source_target_pairs={{0,3},{1,2},{2,1},{3,0},{4,7},{5,6},{6,5},{7,4},{8,11},{9,10},{10,... | collective-permute-start | bytes 2359304 | tf_op jit(solution)/shard_map/ppermute | solution.py:477
  120.3 19.6 %collective-permute-start.8 = (bf16[12,64,512]{2,1,0:T(8,128)(2,1)}, bf16[12,64,512]{2,1,0:T(8,128)(2,1)S(1)}, u32[]{:S(2)}, u32[]{:S(2)}) collective-permute-start(bf16[12,64,512]{2,1,0:T(8,128)(2,1)} %get-tuple-element.37), channel_id=1, source_target_pairs={{0,1},{1,0},{2,3},{3,2},{4,5},{5,4},{6,7},{7,6},{8,9},{9,8},{10,11... | collective-permute-start | bytes 2359304 | tf_op jit(solution)/shard_map/ppermute | solution.py:477
  120.7 36.6 %collective-permute-start.9 = (bf16[12,64,512]{2,1,0:T(8,128)(2,1)}, bf16[12,64,512]{2,1,0:T(8,128)(2,1)}, u32[]{:S(2)}, u32[]{:S(2)}) collective-permute-start(bf16[12,64,512]{2,1,0:T(8,128)(2,1)} %get-tuple-element.38), channel_id=1, source_target_pairs={{0,2},{1,3},{2,0},{3,1},{4,6},{5,7},{6,4},{7,5},{8,10},{9,11},{10,... | collective-permute-start | bytes 2359304 | tf_op jit(solution)/shard_map/ppermute | solution.py:477
  286.4 74.6 %collective-permute-start.22 = (bf16[2,2,2,2,1,208,512]{6,5,4,3,2,1,0:T(8,128)(2,1)S(1)}, bf16[2,2,2,2,1,208,512]{6,5,4,3,2,1,0:T(8,128)(2,1)}, u32[]{:S(2)}, u32[]{:S(2)}) collective-permute-start(bf16[2,2,2,2,1,208,512]{6,5,4,3,2,1,0:T(8,128)(2,1)S(1)} %constant_dynamic-slice_fusion.4), channel_id=1, source_target_pairs={{0,1},{1,0},{2,3},{3,2},{4,5},{5,4},{6,7},{7,6},{8,9},{9,8},{10,11... | collective-permute-start | bytes 10223624 | tf_op jit(solution)/shard_map/ppermute | solution.py:493
  286.5 6.8 %collective-permute-start.11 = (bf16[12,64,512]{2,1,0:T(8,128)(2,1)S(1)}, bf16[12,64,512]{2,1,0:T(8,128)(2,1)S(1)}, u32[]{:S(2)}, u32[]{:S(2)}) collective-permute-start(bf16[12,64,512]{2,1,0:T(8,128)(2,1)S(1)} %copy-done.18), channel_id=1, source_target_pairs={{0,1},{1,0},{2,3},{3,2},{4,5},{5,4},{6,7},{7,6},{8,9},{9,8},{10,11... | collective-permute-start | bytes 2359304 | tf_op jit(solution)/shard_map/ppermute | solution.py:477
  286.9 20.4 %collective-permute-start.12 = (bf16[12,64,512]{2,1,0:T(8,128)(2,1)S(1)}, bf16[12,64,512]{2,1,0:T(8,128)(2,1)S(1)}, u32[]{:S(2)}, u32[]{:S(2)}) collective-permute-start(bf16[12,64,512]{2,1,0:T(8,128)(2,1)S(1)} %copy-done.16), channel_id=1, source_target_pairs={{0,2},{1,3},{2,0},{3,1},{4,6},{5,7},{6,4},{7,5},{8,10},{9,11},{10,... | collective-permute-start | bytes 2359304 | tf_op jit(solution)/shard_map/ppermute | solution.py:477
  287.3 35.2 %collective-permute-start.13 = (bf16[12,64,512]{2,1,0:T(8,128)(2,1)S(1)}, bf16[12,64,512]{2,1,0:T(8,128)(2,1)S(1)}, u32[]{:S(2)}, u32[]{:S(2)}) collective-permute-start(bf16[12,64,512]{2,1,0:T(8,128)(2,1)S(1)} %copy-done.15), channel_id=1, source_target_pairs={{0,3},{1,2},{2,1},{3,0},{4,7},{5,6},{6,5},{7,4},{8,11},{9,10},{10,... | collective-permute-start | bytes 2359304 | tf_op jit(solution)/shard_map/ppermute | solution.py:477
  293.2 29.2 %copy-start.17 = (bf16[12,64,512]{2,1,0:T(8,128)(2,1)}, bf16[12,64,512]{2,1,0:T(8,128)(2,1)S(1)}, u32[]{:S(2)}) copy-start(bf16[12,64,512]{2,1,0:T(8,128)(2,1)S(1)} %collective-permute-done.11.r_5_) | copy-start | bytes 2359300
  360.3 7.8 %collective-permute-start.17 = (bf16[2,2,2,2,1,16,1664]{6,5,4,3,2,1,0:T(8,128)(2,1)}, bf16[2,2,2,2,1,16,1664]{6,5,4,3,2,1,0:T(8,128)(2,1)}, u32[]{:S(2)}, u32[]{:S(2)}) collective-permute-start(bf16[2,2,2,2,1,16,1664]{6,5,4,3,2,1,0:T(8,128)(2,1)} %constant_dynamic-slice_fusion.9), channel_id=1, source_target_pairs={{0,1},{1,0},{2,3},{3,2},{4,5},{5,4},{6,7},{7,6},{8,9},{9,8},{10,11... | collective-permute-start | bytes 2555912 | tf_op jit(solution)/shard_map/ppermute | solution.py:493
  366.5 52.1 %collective-permute-start.23 = (bf16[2,2,1,2,1,208,512]{6,5,4,3,2,1,0:T(8,128)(2,1)}, bf16[2,2,1,2,1,208,512]{6,5,4,3,2,1,0:T(8,128)(2,1)}, u32[]{:S(2)}, u32[]{:S(2)}) collective-permute-start(bf16[2,2,1,2,1,208,512]{6,5,4,3,2,1,0:T(8,128)(2,1)} %constant_dynamic-slice_fusion.3), channel_id=1, source_target_pairs={{0,4},{4,0},{8,12},{12,8},{16,20},{20,16},{24,28},{28,24},{1,5},{5... | collective-permute-start | bytes 5111816 | tf_op jit(solution)/shard_map/ppermute | solution.py:493
  371.2 43.9 %collective-permute-start.18 = (bf16[2,2,1,2,1,16,1664]{6,5,4,3,2,1,0:T(8,128)(2,1)}, bf16[2,2,1,2,1,16,1664]{6,5,4,3,2,1,0:T(8,128)(2,1)}, u32[]{:S(2)}, u32[]{:S(2)}) collective-permute-start(bf16[2,2,1,2,1,16,1664]{6,5,4,3,2,1,0:T(8,128)(2,1)} %constant_dynamic-slice_fusion.8), channel_id=1, source_target_pairs={{0,4},{4,0},{8,12},{12,8},{16,20},{20,16},{24,28},{28,24},{1,5},{5... | collective-permute-start | bytes 1277960 | tf_op jit(solution)/shard_map/ppermute | solution.py:493
  371.9 50.5 %collective-permute-start.14 = (bf16[12,64,512]{2,1,0:T(8,128)(2,1)}, bf16[12,64,512]{2,1,0:T(8,128)(2,1)}, u32[]{:S(2)}, u32[]{:S(2)}) collective-permute-start(bf16[12,64,512]{2,1,0:T(8,128)(2,1)} %get-tuple-element.53), channel_id=1, source_target_pairs={{0,1},{1,0},{2,3},{3,2},{4,5},{5,4},{6,7},{7,6},{8,9},{9,8},{10,11... | collective-permute-start | bytes 2359304 | tf_op jit(solution)/shard_map/ppermute | solution.py:477
  371.9 50.5 %collective-permute-start.15 = (bf16[12,64,512]{2,1,0:T(8,128)(2,1)}, bf16[12,64,512]{2,1,0:T(8,128)(2,1)}, u32[]{:S(2)}, u32[]{:S(2)}) collective-permute-start(bf16[12,64,512]{2,1,0:T(8,128)(2,1)} %get-tuple-element.54), channel_id=1, source_target_pairs={{0,2},{1,3},{2,0},{3,1},{4,6},{5,7},{6,4},{7,5},{8,10},{9,11},{10,... | collective-permute-start | bytes 2359304 | tf_op jit(solution)/shard_map/ppermute | solution.py:477
  372.4 50.1 %collective-permute-start.16 = (bf16[12,64,512]{2,1,0:T(8,128)(2,1)}, bf16[12,64,512]{2,1,0:T(8,128)(2,1)}, u32[]{:S(2)}, u32[]{:S(2)}) collective-permute-start(bf16[12,64,512]{2,1,0:T(8,128)(2,1)} %get-tuple-element.55), channel_id=1, source_target_pairs={{0,3},{1,2},{2,1},{3,0},{4,7},{5,6},{6,5},{7,4},{8,11},{9,10},{10,... | collective-permute-start | bytes 2359304 | tf_op jit(solution)/shard_map/ppermute | solution.py:477
  417.1 12.2 %collective-permute-start.19 = (bf16[2,1,1,2,1,16,1664]{6,5,4,3,2,1,0:T(8,128)(2,1)}, bf16[2,1,1,2,1,16,1664]{6,5,4,3,2,1,0:T(8,128)(2,1)}, u32[]{:S(2)}, u32[]{:S(2)}) collective-permute-start(bf16[2,1,1,2,1,16,1664]{6,5,4,3,2,1,0:T(8,128)(2,1)} %constant_dynamic-slice_fusion.7), channel_id=1, source_target_pairs={{0,8},{4,12},{8,0},{12,4},{16,24},{20,28},{24,16},{28,20},{1,9},{5... | collective-permute-start | bytes 638984 | tf_op jit(solution)/shard_map/ppermute | solution.py:493
  421.8 22.3 %collective-permute-start.24 = (bf16[2,1,1,2,1,208,512]{6,5,4,3,2,1,0:T(8,128)(2,1)S(1)}, bf16[2,1,1,2,1,208,512]{6,5,4,3,2,1,0:T(8,128)(2,1)S(1)}, u32[]{:S(2)}, u32[]{:S(2)}) collective-permute-start(bf16[2,1,1,2,1,208,512]{6,5,4,3,2,1,0:T(8,128)(2,1)S(1)} %constant_dynamic-slice_fusion.2), channel_id=1, source_target_pairs={{0,8},{4,12},{8,0},{12,4},{16,24},{20,28},{24,16},{28,20},{1,9},{5... | collective-permute-start | bytes 2555912 | tf_op jit(solution)/shard_map/ppermute | solution.py:493
  430.3 15.7 %collective-permute-start.20 = (bf16[1,1,1,2,1,16,1664]{6,5,4,3,2,1,0:T(8,128)(2,1)S(1)}, bf16[1,1,1,2,1,16,1664]{6,5,4,3,2,1,0:T(8,128)(2,1)S(1)}, u32[]{:S(2)}, u32[]{:S(2)}) collective-permute-start(bf16[1,1,1,2,1,16,1664]{6,5,4,3,2,1,0:T(8,128)(2,1)S(1)} %constant_dynamic-slice_fusion.6), channel_id=1, source_target_pairs={{0,16},{4,20},{8,24},{12,28},{16,0},{20,4},{24,8},{28,12},{1,17},{... | collective-permute-start | bytes 319496 | tf_op jit(solution)/shard_map/ppermute | solution.py:493
  444.5 20.0 %collective-permute-start.25 = (bf16[1,1,1,2,1,208,512]{6,5,4,3,2,1,0:T(8,128)(2,1)S(1)}, bf16[1,1,1,2,1,208,512]{6,5,4,3,2,1,0:T(8,128)(2,1)S(1)}, u32[]{:S(2)}, u32[]{:S(2)}) collective-permute-start(bf16[1,1,1,2,1,208,512]{6,5,4,3,2,1,0:T(8,128)(2,1)S(1)} %constant_dynamic-slice_fusion.1), channel_id=1, source_target_pairs={{0,16},{4,20},{8,24},{12,28},{16,0},{20,4},{24,8},{28,12},{1,17},{... | collective-permute-start | bytes 1277960 | tf_op jit(solution)/shard_map/ppermute | solution.py:493
  446.1 19.0 %collective-permute-start.21 = (bf16[1,1,1,1,1,16,1664]{6,5,4,3,2,1,0:T(8,128)(2,1)S(1)}, bf16[1,1,1,1,1,16,1664]{6,5,4,3,2,1,0:T(8,128)(2,1)S(1)}, u32[]{:S(2)}, u32[]{:S(2)}) collective-permute-start(bf16[1,1,1,1,1,16,1664]{6,5,4,3,2,1,0:T(8,128)(2,1)S(1)} %constant_dynamic-slice_fusion.5), channel_id=1, source_target_pairs={{0,2},{1,3},{2,0},{3,1},{4,6},{5,7},{6,4},{7,5},{8,10},{9,11},{10,... | collective-permute-start | bytes 159752 | tf_op jit(solution)/shard_map/ppermute | solution.py:493
  464.6 5.9 %collective-permute-start.26 = (bf16[1,1,1,1,1,208,512]{6,5,4,3,2,1,0:T(8,128)(2,1)S(1)}, bf16[1,1,1,1,1,208,512]{6,5,4,3,2,1,0:T(8,128)(2,1)S(1)}, u32[]{:S(2)}, u32[]{:S(2)}) collective-permute-start(bf16[1,1,1,1,1,208,512]{6,5,4,3,2,1,0:T(8,128)(2,1)S(1)} %constant_dynamic-slice_fusion), channel_id=1, source_target_pairs={{0,2},{1,3},{2,0},{3,1},{4,6},{5,7},{6,4},{7,5},{8,10},{9,11},{10,... | collective-permute-start | bytes 638984 | tf_op jit(solution)/shard_map/ppermute | solution.py:493
  (18 other events, 116.4 us)
Sparse Core Ops, SparseCore 0:
  15.6 91.5 all-gather.2

commit v2 on v1

v2 whole, which is shorter than its diff:
```python
import jax
import jax.numpy as jnp
import numpy as np
from jax import lax
from jax.experimental import pallas as pl
from jax.experimental.pallas import tpu as pltpu
from jax.sharding import PartitionSpec as P

D = 512
HEADS = 4
HEAD_DIM = 128
FF = 2048
QKV = 3 * D
EPS = 1e-05
MASKED = -1e30
SCALE = HEAD_DIM**-0.5
BF = jnp.bfloat16
F32 = jnp.float32
LOG2E = float(np.log2(np.e))
VMEM = 60 * 1024 * 1024

GRP2 = 4
GRP = 4
ROWS_P = 16
COST = pl.CostEstimate(flops=10**11, bytes_accessed=10**6, transcendentals=0)
RC = 16
FCH = 512
FB = 2


def mm(a, b):
    return lax.dot_general(a, b, (((1,), (0,)), ((), ())), preferred_element_type=F32)


def mt(a, b):
    return lax.dot_general(a, b, (((1,), (1,)), ((), ())), preferred_element_type=F32)


def tm(a, b):
    return lax.dot_general(a, b, (((0,), (0,)), ((), ())), preferred_element_type=F32)


def norm(x):
    mean = jnp.mean(x, axis=-1, keepdims=True)
    centred = x - mean
    var = jnp.mean(centred * centred, axis=-1, keepdims=True)
    rstd = lax.rsqrt(var + EPS)
    return centred * rstd, rstd


def norm_back(n, xhat, rstd, gain):
    e = n * gain
    m1 = jnp.mean(e, axis=-1, keepdims=True)
    m2 = jnp.mean(e * xhat, axis=-1, keepdims=True)
    return rstd * (e - m1 - xhat * m2)


def fold8(a):
    return jnp.sum(a.reshape(a.shape[0] // 8, 8, a.shape[1]), axis=0)


def gelu_pair(h):
    e = jnp.exp2(h * h * (-0.5 * LOG2E))
    d = 1.0 + (0.3275911 * 2**-0.5) * jnp.abs(h)
    t = pl.reciprocal(d, approx=True)
    t = t * (2.0 - d * t)
    poly = 0.5 * 1.061405429
    for c in (-1.453152027, 1.421413741, -0.284496736, 0.254829592):
        poly = poly * t + 0.5 * c
    q = poly * t * e
    cdf = jnp.where(h >= 0, 1.0 - q, q)
    return h * cdf, cdf + h * e * (2 * np.pi) ** -0.5


def put_rows(ref, start, x):
    for c in range(HEADS):
        ref[c, start : start + x.shape[0]] = x[:, c * 128 : c * 128 + 128]


def get_row(ref, r, tot):
    return jnp.concatenate([ref[c, pl.ds(r, tot, stride=RC), :] for c in range(HEADS)], axis=1)


def full(shape):
    return pl.BlockSpec(shape, lambda *_: (0,) * len(shape), pipeline_mode=pl.Buffered(1))


def feature_forward_kernel(_, *refs, n, feats, cuts):
    x_refs, (gain, shift, wqkv, bias), outs = refs[:n], refs[n : n + 4], refs[n + 4 :]
    nc = n * len(cuts)
    h_refs, (qkv_ref, p_ref), (xs, low, hs) = outs[:nc], outs[nc : nc + 2], outs[nc + 2 :]
    tot = n * feats
    pair = 2 * tot
    wide = bias.shape[1]
    for k in range(n):
        put_rows(xs, k * feats * RC, x_refs[k][...].reshape(feats * RC, D).astype(F32))
    for r in range(RC):
        xhat, _ = norm(get_row(xs, r, tot))
        low[r * tot : (r + 1) * tot] = (xhat * gain[...] + shift[...]).astype(BF)
    rows = tot * RC
    qkv_ref[0, :rows] = mm(low[...], wqkv[...]).astype(BF)
    qkv_ref[0, rows:] = jnp.zeros((qkv_ref.shape[1] - rows, QKV), BF)
    mask = bias[...]
    for b0 in range(0, RC // 2, GRP):
        jobs = [(b, h) for b in range(b0, b0 + GRP) for h in range(HEADS)]
        at = lambda b, h, c, w: (0, slice(b * pair, b * pair + w), slice(c * D + h * 128, c * D + h * 128 + 128))
        ss = [mt(qkv_ref[at(b, h, 0, pair)], qkv_ref[at(b, h, 1, wide)]) * (SCALE * LOG2E) + mask for b, h in jobs]
        es = [jnp.exp2(s - jnp.max(s, axis=-1, keepdims=True)) for s in ss]
        ps = [(e * (1.0 / jnp.sum(e, axis=-1, keepdims=True))).astype(BF) for e in es]
        os = [mm(p, qkv_ref[at(b, h, 2, wide)]) for p, (b, h) in zip(ps, jobs)]
        for p, o, (b, h) in zip(ps, os, jobs):
            p_ref[0, b, h] = p
            for j in range(2):
                hs[h, pl.ds(2 * b + j, tot, stride=RC), :] = o[j * tot : (j + 1) * tot]
    for c, (f0, f1) in enumerate(cuts):
        for k in range(n):
            for h in range(HEADS):
                part = hs[h, (k * feats + f0) * RC : (k * feats + f1) * RC].reshape(f1 - f0, RC, 128)
                h_refs[c * n + k][:, :, h * 128 : h * 128 + 128] = part.astype(BF)


def feature_forward(x_rows, xs, gain, shift, wqkv, bias, cuts, rows):
    n = len(xs)
    feats = xs[0].shape[0]
    tot = n * feats
    steps = rows // RC
    pad = tot * RC - 2 * tot + bias.shape[1]
    sds = jax.ShapeDtypeStruct
    return pl.pallas_call(
        lambda *r: feature_forward_kernel(*r, n=n, feats=feats, cuts=cuts),
        grid_spec=pltpu.PrefetchScalarGridSpec(
            num_scalar_prefetch=1,
            grid=(steps,),
            in_specs=[pl.BlockSpec((feats, RC, D), lambda i, at, k=k: (0, i + at[k], 0)) for k in range(n)]
            + [full((1, D)), full((1, D)), full((D, QKV)), full(bias.shape)],
            out_specs=[pl.BlockSpec((f1 - f0, RC, D), lambda i, at: (0, i, 0)) for f0, f1 in cuts for _ in range(n)]
            + [
                pl.BlockSpec((1, pad, QKV), lambda i, at: (i, 0, 0)),
                pl.BlockSpec((1, RC // 2, HEADS, 2 * tot, bias.shape[1]), lambda i, at: (i, 0, 0, 0, 0)),
            ],
            scratch_shapes=[
                pltpu.VMEM((HEADS, tot * RC, 128), F32),
                pltpu.VMEM((tot * RC, D), BF),
                pltpu.VMEM((HEADS, tot * RC, 128), F32),
            ],
        ),
        out_shape=[sds((f1 - f0, rows, D), BF) for f0, f1 in cuts for _ in range(n)]
        + [sds((steps, pad, QKV), BF), sds((steps, RC // 2, HEADS, 2 * tot, bias.shape[1]), BF)],
        compiler_params=pltpu.CompilerParams(vmem_limit_bytes=VMEM),
        cost_estimate=COST,
        name="feature_forward",
    )(x_rows, *xs, gain, shift, wqkv, bias)


def feature_backward_kernel(_, *refs, n, feats, cuts, first, last):
    it = iter(refs)
    take = lambda c: [next(it) for _ in range(c)]
    x_refs = take(n)
    g_refs = take(n * len(cuts))
    qkv_ref, p_ref, gain, shift, wqkv = take(5)
    carried = [] if first else take(3)
    others = take(4) if last else []
    d_refs = take(n)
    outs = take(1) if last else take(3)
    dgain, dshift, vecs, xs, gs, ns, low, gh, gqkv, acc = take(10)
    if not last:
        acc, dgain, dshift = outs
    tot = n * feats
    pair = 2 * tot
    wide = p_ref.shape[-1]
    i = pl.program_id(0)

    @pl.when(i == 0)
    def _():
        for j, a in enumerate((acc, dgain, dshift)):
            a[...] = jnp.zeros_like(a) if first else carried[j][...]

    for k in range(n):
        put_rows(xs, k * feats * RC, x_refs[k][...].reshape(feats * RC, D).astype(F32))
        for c, (f0, f1) in enumerate(cuts):
            put_rows(gs, (k * feats + f0) * RC, g_refs[c * n + k][...].reshape((f1 - f0) * RC, D).astype(F32))
    for r in range(RC):
        gh[r * tot : (r + 1) * tot] = get_row(gs, r, tot).astype(BF)
        xhat, _ = norm(get_row(xs, r, tot))
        low[r * tot : (r + 1) * tot] = (xhat * gain[...] + shift[...]).astype(BF)
    for b0 in range(0, RC // 2, GRP):
        jobs = [(b, h) for b in range(b0, b0 + GRP) for h in range(HEADS)]
        at = lambda b, h, c, w: (0, slice(b * pair, b * pair + w), slice(c * D + h * 128, c * D + h * 128 + 128))
        gs_ = [gh[b * pair : (b + 1) * pair, h * 128 : h * 128 + 128] for b, h in jobs]
        dps = [mt(g, qkv_ref[at(b, h, 2, wide)]) for g, (b, h) in zip(gs_, jobs)]
        ps = [p_ref[0, b, h] for b, h in jobs]
        dvs = [tm(p, g) for p, g in zip(ps, gs_)]
        pds = [p.astype(F32) * dp for p, dp in zip(ps, dps)]
        dss = [(pd - p.astype(F32) * jnp.sum(pd, axis=-1, keepdims=True)).astype(BF) for p, pd in zip(ps, pds)]
        dqs = [mm(ds, qkv_ref[at(b, h, 1, wide)]) for ds, (b, h) in zip(dss, jobs)]
        dks = [tm(ds, qkv_ref[at(b, h, 0, pair)]) for ds, (b, h) in zip(dss, jobs)]
        for (b, h), dq, dk, dv in zip(jobs, dqs, dks, dvs):
            span = slice(b * pair, (b + 1) * pair)
            gqkv[span, h * 128 : h * 128 + 128] = (dq * SCALE).astype(BF)
            gqkv[span, D + h * 128 : D + h * 128 + 128] = (dk * SCALE).astype(BF)[:pair]
            gqkv[span, 2 * D + h * 128 : 2 * D + h * 128 + 128] = dv.astype(BF)[:pair]
    acc[...] += tm(low[...], gqkv[...])
    ns[...] = mt(gqkv[...], wqkv[...])
    for r in range(RC):
        xhat, rstd = norm(get_row(xs, r, tot))
        nn = ns[r * tot : (r + 1) * tot]
        dgain[...] += fold8(nn * xhat)
        dshift[...] += fold8(nn)
        d = norm_back(nn, xhat, rstd, gain[...])
        for c in range(HEADS):
            xs[c, pl.ds(r, tot, stride=RC), :] = d[:, c * 128 : c * 128 + 128]
    for k in range(n):
        for c in range(HEADS):
            d_refs[k][:, :, c * 128 : c * 128 + 128] = xs[c, k * feats * RC : (k + 1) * feats * RC].reshape(feats, RC, 128).astype(BF)

    if last:

        @pl.when(i == pl.num_programs(0) - 1)
        def _():
            outs[0][:, :QKV] = acc[...].astype(BF)
            vecs[...] = jnp.zeros_like(vecs)
            for j, v in enumerate([dgain, dshift] + others):
                vecs[j : j + 1] = jnp.sum(v[...], axis=0, keepdims=True)
            outs[0][:, QKV:] = vecs[...].T.astype(BF)


def feature_backward(x_rows, xs, gs, qkv, p, gain, shift, wqkv, cuts, r0, r1, carried, others):
    n = len(xs)
    feats = xs[0].shape[0]
    tot = n * feats
    s0, steps = r0 // RC, (r1 - r0) // RC
    first, last = not carried, bool(others)
    sds = jax.ShapeDtypeStruct
    at = lambda f, row: pl.BlockSpec((f, RC, D), lambda i, _: (0, i + (r0 - row) // RC, 0))
    sums = [(D, QKV), (8, D), (8, D)]
    if last:
        out_specs, out_shape = [pl.BlockSpec((D, QKV + 128), lambda i, _: (0, 0))], [sds((D, QKV + 128), BF)]
    else:
        out_specs, out_shape = [pl.BlockSpec(q, lambda i, _: (0, 0)) for q in sums], [sds(q, F32) for q in sums]
    return pl.pallas_call(
        lambda *r: feature_backward_kernel(*r, n=n, feats=feats, cuts=cuts, first=first, last=last),
        grid_spec=pltpu.PrefetchScalarGridSpec(
            num_scalar_prefetch=1,
            grid=(steps,),
            in_specs=[pl.BlockSpec((feats, RC, D), lambda i, q, k=k: (0, i + s0 + q[k], 0)) for k in range(n)]
            + [at(f1 - f0, row) for (f0, f1), (row, _) in zip(cuts, gs) for _ in range(n)]
            + [
                pl.BlockSpec((1,) + qkv.shape[1:], lambda i, _: (i + s0, 0, 0)),
                pl.BlockSpec((1,) + p.shape[1:], lambda i, _: (i + s0, 0, 0, 0, 0)),
                full((1, D)),
                full((1, D)),
                full((D, QKV)),
            ]
            + [full(q.shape) for q in carried]
            + [full((8, D)) for _ in others],
            out_specs=[at(feats, r0)] * n + out_specs,
            scratch_shapes=[
                pltpu.VMEM((8, D), F32),
                pltpu.VMEM((8, D), F32),
                pltpu.VMEM((128, D), F32),
                pltpu.VMEM((HEADS, tot * RC, 128), F32),
                pltpu.VMEM((HEADS, tot * RC, 128), F32),
                pltpu.VMEM((tot * RC, D), F32),
                pltpu.VMEM((tot * RC, D), BF),
                pltpu.VMEM((tot * RC, D), BF),
                pltpu.VMEM((tot * RC, QKV), BF),
                pltpu.VMEM((D, QKV), F32),
            ],
        ),
        out_shape=[sds((feats, r1 - r0, D), BF)] * n + out_shape,
        compiler_params=pltpu.CompilerParams(vmem_limit_bytes=VMEM),
        cost_estimate=COST,
        name="feature_backward",
    )(x_rows, *xs, *[a for _, part in gs for a in part], qkv, p, gain, shift, wqkv, *carried, *others)


class Flat:
    def __init__(self, ref):
        self.ref = ref

    def __getitem__(self, key):
        rows, cols = (slice(None), slice(None)) if key is Ellipsis else key
        r = self.ref.shape[1]
        if rows.start is not None:
            rows = slice(rows.start // r, rows.stop // r)
        w = self.ref[rows, :, cols]
        return w.reshape(w.shape[0] * w.shape[1], w.shape[2])


def unpack_copies(pack, weights, sems):
    copies, at = [], 0
    for w in weights:
        r = w.shape[1]
        for j in range(w.shape[2] // D):
            src = pack.at[:, pl.ds(at, r), :]
            copies.append(pltpu.make_async_copy(src, w.at[:, :, pl.ds(j * D, D)], sems.at[len(copies)]))
            at += r
    return copies


def middle_kernel(me_ref, core_ref, *refs, n, rows, part, spans, first, last):
    it = iter(refs)
    take = lambda c: [next(it) for _ in range(c)]
    (x_ref,) = take(1)
    h_refs = take(n)
    cot_ref, bias, pack, g2, b2, g3, b3 = take(7)
    carried = [] if first else take(9)
    _ = [] if first else take(2)
    out_ref, gaf_ref = take(2)
    gh_refs = take(n * len(spans))
    kept = take(2) if last else take(5)
    dg2, db2, dg3, db3 = take(4)
    h1_s, qkv_s, p_s, gq_s, heads_s, gh2_s, afo, arq, aro, ain, aout, wfo_s, wrq_s, wro_s, win_s, wout_s, sems, asems = take(18)
    i = pl.program_id(0)
    me = me_ref[0]
    m = FB * rows
    accs = (afo, arq, aro, ain, aout)

    @pl.when(i == 0)
    def _():
        copies = unpack_copies(pack, (wfo_s, wrq_s, wro_s, win_s, wout_s), sems)
        for c in copies:
            c.start()
        if first:
            for a in (afo, arq, aro, ain, aout, dg2, db2, dg3, db3):
                a[...] = jnp.zeros_like(a)
        else:
            more = [pltpu.make_async_copy(c, a, asems.at[j]) for j, (c, a) in enumerate(zip(carried, accs))]
            for c in more:
                c.start()
            for c, a in zip(carried[5:], (dg2, db2, dg3, db3)):
                a[...] = c[...]

    def need(*which):
        @pl.when(i == 0)
        def _():
            at = 0
            for j, w in enumerate((wfo_s, wrq_s, wro_s, win_s, wout_s)):
                for _ in range(w.shape[2] // D):
                    if j in which:
                        pltpu.make_async_copy(pack.at[:, pl.ds(0, w.shape[1]), :], w.at[:, :, pl.ds(0, D)], sems.at[at]).wait()
                    at += 1

    def settle(*which):
        if not first:

            @pl.when(i == 0)
            def _():
                for j in which:
                    pltpu.make_async_copy(carried[j], accs[j], asems.at[j]).wait()

    def keep(*which):
        if not last:

            @pl.when(i == pl.num_programs(0) - 1)
            def _():
                for j in which:
                    pltpu.make_async_copy(accs[j], kept[j], asems.at[j]).start()

    wfo, wrq, wro, win, wout = (Flat(w) for w in (wfo_s, wrq_s, wro_s, win_s, wout_s))
    for k in range(n):
        off = pl.multiple_of((me ^ k) * part, part)
        for f in range(FB):
            h1_s[pl.ds(f * rows + off, part), :] = h_refs[k][f]
    x = x_ref[0].reshape(m, D).astype(F32)
    h1 = h1_s[...]
    need(0)
    after_feat = x + mm(h1, wfo[...])
    xhat2, rstd2 = norm(after_feat)
    low2 = (xhat2 * g2[...] + b2[...]).astype(BF)
    need(1, 2, 3, 4)
    settle(3, 4)
    qkv_s[...] = mm(low2, wrq[...]).astype(BF)
    mask = bias[...]
    jobs = [(f, h) for f in range(FB) for h in range(HEADS)]
    at = lambda f, h, c: (slice(f * rows, (f + 1) * rows), slice(c * D + h * 128, c * D + h * 128 + 128))
    for g0 in range(0, len(jobs), GRP2):
        some = jobs[g0 : g0 + GRP2]
        ss = [mt(qkv_s[at(f, h, 0)], qkv_s[at(f, h, 1)]) * (SCALE * LOG2E) + mask for f, h in some]
        es = [jnp.exp2(s - jnp.max(s, axis=-1, keepdims=True)) for s in ss]
        ps = [(e * (1.0 / jnp.sum(e, axis=-1, keepdims=True))).astype(BF) for e in es]
        for p, (f, h) in zip(ps, some):
            p_s[f * HEADS + h] = p
            heads_s[at(f, h, 0)] = mm(p, qkv_s[at(f, h, 2)]).astype(BF)
    heads = heads_s[...]
    after_row = after_feat + mm(heads, wro[...])
    xhat3, rstd3 = norm(after_row)
    low3 = (xhat3 * g3[...] + b3[...]).astype(BF)
    cot = cot_ref[0].reshape(m, D)
    out = after_row
    n3 = None
    for j in range(FF // FCH):
        cols = slice(j * FCH, (j + 1) * FCH)
        act, slope = gelu_pair(mm(low3, win[:, cols]))
        act = act.astype(BF)
        out = out + mm(act, wout[cols, :])
        ghid = (mt(cot, wout[cols, :]) * slope).astype(BF)
        aout[:, cols] += tm(cot, act)
        ain[:, cols] += tm(low3, ghid)
        back = mt(ghid, win[:, cols])
        n3 = back if n3 is None else n3 + back
    keep(3, 4)
    out_ref[0] = out.astype(BF).reshape(FB, rows, D)
    dg3[...] += fold8(n3 * xhat3)
    db3[...] += fold8(n3)
    g_row = cot.astype(F32) + norm_back(n3, xhat3, rstd3, g3[...])
    gb = g_row.astype(BF)
    settle(0, 1, 2)
    aro[...] += tm(heads, gb)
    gh2_s[...] = mt(gb, wro[...]).astype(BF)
    for g0 in range(0, len(jobs), GRP2):
        some = jobs[g0 : g0 + GRP2]
        gs = [gh2_s[at(f, h, 0)] for f, h in some]
        ps = [p_s[f * HEADS + h] for f, h in some]
        dps = [mt(g, qkv_s[at(f, h, 2)]) for g, (f, h) in zip(gs, some)]
        pds = [p.astype(F32) * dp for p, dp in zip(ps, dps)]
        dss = [(pd - p.astype(F32) * jnp.sum(pd, axis=-1, keepdims=True)).astype(BF) for p, pd in zip(ps, pds)]
        for (f, h), g, p, ds in zip(some, gs, ps, dss):
            gq_s[at(f, h, 2)] = tm(p, g).astype(BF)
            gq_s[at(f, h, 0)] = (mm(ds, qkv_s[at(f, h, 1)]) * SCALE).astype(BF)
            gq_s[at(f, h, 1)] = (tm(ds, qkv_s[at(f, h, 0)]) * SCALE).astype(BF)
    gq = gq_s[...]
    arq[...] += tm(low2, gq)
    n2 = mt(gq, wrq[...])
    dg2[...] += fold8(n2 * xhat2)
    db2[...] += fold8(n2)
    g_feat = g_row + norm_back(n2, xhat2, rstd2, g2[...])
    gaf_ref[...] = g_feat.reshape(FB, rows, D)
    gf = g_feat.astype(BF)
    afo[...] += tm(h1, gf)
    keep(0, 1, 2)
    h1_s[...] = mt(gf, wfo[...]).astype(BF)
    for k in range(n):
        for f in range(FB):
            for c, (r0, r1) in enumerate(spans):
                off = pl.multiple_of((me ^ k) * part + r0, 16)
                gh_refs[c * n + k][f] = h1_s[pl.ds(f * rows + off, r1 - r0), :]

    @pl.when(i == pl.num_programs(0) - 1)
    def _():
        if not last:
            for j in range(5):
                pltpu.make_async_copy(accs[j], kept[j], asems.at[j]).wait()
        else:
            core = core_ref[0]
            at = 0
            for acc in accs[:4]:
                for j in range(acc.shape[1] // D):
                    for b in range(D // (2 * ROWS_P)):
                        for side, ref in ((core, kept[0]), (1 - core, kept[1])):
                            row = pl.multiple_of((2 * b + side) * ROWS_P, ROWS_P)
                            ref[b, at : at + ROWS_P, :] = acc[pl.ds(row, ROWS_P), j * D : (j + 1) * D].astype(BF)
                    at += ROWS_P
            for j in range(FF // D):
                unit = jnp.where(lax.broadcasted_iota(jnp.int32, (D, D), 0) == lax.broadcasted_iota(jnp.int32, (D, D), 1), 1.0, 0.0)
                turned = mt(unit.astype(BF), aout[:, j * D : (j + 1) * D].astype(BF)).astype(BF).reshape(4, 2, 4 * ROWS_P, D)
                even, odd = turned[:, 0], turned[:, 1]
                blocks = slice(j * 4, (j + 1) * 4)
                kept[0][blocks, at:, :] = jnp.where(core == 0, even, odd)
                kept[1][blocks, at:, :] = jnp.where(core == 0, odd, even)


def middle(me, core, x, hs, cot, bias, pack, g2, b2, g3, b3, f0, spans, carried, last):
    n = len(hs)
    _, feats, rows, _ = x.shape
    part = rows // n
    m = FB * rows
    count = hs[0].shape[0]
    first = not carried
    any_ = pl.BlockSpec(memory_space=pl.ANY)
    xblk = pl.BlockSpec((1, FB, rows, D), lambda i, *_: (0, i + f0 // FB, 0, 0))
    hblk = lambda r: pl.BlockSpec((FB, r, D), lambda i, *_: (i, 0, 0))
    sds = jax.ShapeDtypeStruct
    sums = [(D, D), (D, QKV), (D, D), (D, FF), (D, FF)]
    half = (pack.shape[0] // 2,) + pack.shape[1:]
    kept_specs = [pl.BlockSpec(half, lambda i, *_: (0, 0, 0))] * 2 if last else [any_] * 5
    kept_shape = [sds(half, BF)] * 2 if last else [sds(q, F32) for q in sums]
    args = [x, *hs, cot, bias, pack, g2, b2, g3, b3, *carried]
    return pl.pallas_call(
        lambda *r: middle_kernel(*r, n=n, rows=rows, part=part, spans=spans, first=first, last=last),
        grid_spec=pltpu.PrefetchScalarGridSpec(
            num_scalar_prefetch=2,
            grid=(count // FB,),
            in_specs=[xblk]
            + [hblk(part)] * n
            + [xblk, full((rows, rows)), any_, full((1, D)), full((1, D)), full((1, D)), full((1, D))]
            + ([] if first else [any_] * 5 + [full((8, D))] * 4 + [any_] * 2),
            out_specs=[xblk, pl.BlockSpec((FB, rows, D), lambda i, *_: (i + f0 // FB, 0, 0))]
            + [hblk(r1 - r0) for r0, r1 in spans for _ in range(n)]
            + kept_specs
            + [pl.BlockSpec((8, D), lambda i, *_: (0, 0))] * 4,
            scratch_shapes=[
                pltpu.VMEM((m, D), BF),
                pltpu.VMEM((m, QKV), BF),
                pltpu.VMEM((FB * HEADS, rows, rows), BF),
                pltpu.VMEM((m, QKV), BF),
                pltpu.VMEM((m, D), BF),
                pltpu.VMEM((m, D), BF),
            ]
            + [pltpu.VMEM(q, F32) for q in sums]
            + [
                pltpu.VMEM((32, ROWS_P, D), BF),
                pltpu.VMEM((32, ROWS_P, QKV), BF),
                pltpu.VMEM((32, ROWS_P, D), BF),
                pltpu.VMEM((32, ROWS_P, FF), BF),
                pltpu.VMEM((32, 4 * ROWS_P, D), BF),
                pltpu.SemaphoreType.DMA((10,)),
                pltpu.SemaphoreType.DMA((5,)),
            ],
        ),
        out_shape=[sds(x.shape, BF), sds((feats, rows, D), F32)]
        + [sds((count, r1 - r0, D), BF) for r0, r1 in spans for _ in range(n)]
        + kept_shape
        + [sds((8, D), F32)] * 4,
        input_output_aliases={} if first else {2 + len(args) - 2: 0, 2 + len(args) - 1: 1},
        compiler_params=pltpu.CompilerParams(vmem_limit_bytes=VMEM),
        cost_estimate=COST,
        name="middle",
    )(me, core, *args)


def final_kernel(me_ref, g_ref, *refs, n):
    out = refs[-1]
    for k in range(n):

        @pl.when(pl.program_id(0) == k)
        def _():
            out[0] = g_ref[...] + refs[k][...].astype(F32)


def final(me, g, ds, r0, before):
    n = len(ds)
    feats, rows, _ = g.shape
    count = ds[0].shape[1]
    each = rows // n // count
    place = lambda i, me: (me[0] ^ i) * each + r0 // count
    more = [] if before is None else [before]
    return pl.pallas_call(
        lambda *r: final_kernel(*r, n=n),
        grid_spec=pltpu.PrefetchScalarGridSpec(
            num_scalar_prefetch=1,
            grid=(n,),
            in_specs=[pl.BlockSpec((feats, count, D), lambda i, me: (0, place(i, me), 0))]
            + [full((feats, count, D))] * n
            + [pl.BlockSpec(memory_space=pl.ANY)] * len(more),
            out_specs=pl.BlockSpec((1, feats, count, D), lambda i, me: (0, 0, place(i, me), 0)),
        ),
        out_shape=jax.ShapeDtypeStruct((1, feats, rows, D), F32),
        input_output_aliases={2 + n: 0} if more else {},
        compiler_params=pltpu.CompilerParams(vmem_limit_bytes=VMEM),
        cost_estimate=COST,
        name="final",
    )(me, g, *ds, *more)


def pack_kernel(*refs):
    vectors, qkv, *mats, down, first, pack = refs
    first[:, :QKV] = qkv[...]
    r = qkv.shape[0]
    first[:, QKV:] = jnp.broadcast_to(vectors[...], (r, 128))
    at = 0
    for m in mats:
        for j in range(m.shape[1] // D):
            pack[at : at + r] = m[:, j * D : (j + 1) * D]
            at += r
    pack[at:] = down[...]


def pack_shards(vectors, qkv, mats, down):
    r = qkv.shape[0]
    if r % ROWS_P:
        pack = jnp.concatenate([m[:, j * D : (j + 1) * D] for m in mats for j in range(m.shape[1] // D)] + [down], axis=0)
        return jnp.concatenate([qkv, jnp.broadcast_to(vectors, (r, 128))], axis=1), pack
    return pl.pallas_call(
        pack_kernel, out_shape=[jax.ShapeDtypeStruct((r, QKV + 128), BF), jax.ShapeDtypeStruct((13 * r, D), BF)], name="pack"
    )(vectors, qkv, *mats, down)


def row_allowed(segments, context):
    tables = jnp.arange(context.shape[0], dtype=jnp.int32)
    member = (segments[:, None] == tables[None, :]).astype(jnp.int32)
    sizes = jnp.sum(member, axis=0)
    starts = jnp.cumsum(sizes) - sizes
    places = jnp.arange(segments.shape[0], dtype=jnp.int32) - jnp.sum(member * starts[None, :], axis=1)
    limits = jnp.sum(member * context[None, :], axis=1)
    usable = places < limits
    return (segments[:, None] == segments[None, :]) & usable[None, :]


def swap(arrays, n):
    return [arrays[0]] + [lax.ppermute(arrays[k], "feat", [(d, d ^ k) for d in range(n)]) for k in range(1, n)]


def exchange(x, me, n, after):
    feats, rows, _ = x.shape

    def move(a, at, rows, bit):
        low = ((me // bit) % 2) * rows
        sent = lax.dynamic_slice(a, (0, at + rows - low, 0), (feats, rows, D))
        if bit == n // 2:
            sent, _ = together(sent, after)
        return lax.ppermute(sent, "feat", [(d, d ^ bit) for d in range(n)]), at + low

    bit = n // 2
    got, low = move(x, 0, rows // 2, bit)
    got = [got]

    def finish():
        have, places, half, bit = [(x, low), (got[0], 0)], [0, n // 2], rows // 2, n // 4
        while bit:
            half //= 2
            moved = [move(a, at, half, bit) for a, at in have]
            have = [(a, at) for (a, _), (_, at) in zip(have, moved)] + [(a, 0) for a, _ in moved]
            places = places + [q ^ bit for q in places]
            bit //= 2
        return [have[places.index(k)] for k in range(n)]

    return got, finish


class Shards:
    def __init__(self, rows, n):
        self.count = rows * n
        self.bits = [("rows", 1 << b) for b in reversed(range(rows.bit_length() - 1))]
        self.bits += [("feat", 1 << b) for b in reversed(range(n.bit_length() - 1))]
        self.sizes = {"rows": rows, "feat": n}
        last = len(self.bits) - 1
        self.rows_bits = list(range(rows.bit_length() - 1))
        self.near = last
        self.feat_bits = list(range(rows.bit_length() - 1, last))

    def other(self, a, at):
        axis, bit = self.bits[at]
        return lax.ppermute(a, axis, [(d, d ^ bit) for d in range(self.sizes[axis])])

    def side(self, at):
        axis, bit = self.bits[at]
        return (lax.axis_index(axis) // bit) % 2

    def gather(self, a, order):
        if a.ndim == 2:
            a = a.reshape((1,) * len(self.bits) + a.shape)
        while order:
            at, *rest = order
            if rest and rest[0] == at + 1 and self.bits[at][0] == "rows" == self.bits[at + 1][0] and self.sizes["rows"] <= 8:
                a = self.gather_two(a, at)
                order = rest[1:]
                continue
            b = self.other(a, at)
            low = self.side(at) == 0
            a = jnp.concatenate([jnp.where(low, a, b), jnp.where(low, b, a)], axis=at)
            order = rest
        return a

    def gather_two(self, a, at):
        axis, high = self.bits[at]
        low = self.bits[at + 1][1]
        move = lambda mask: lax.ppermute(a, axis, [(d, d ^ mask) for d in range(self.sizes[axis])])
        all_ = [[a, move(low)], [move(high), move(high | low)]]
        line = lambda q, side: jnp.concatenate([jnp.where(side, q[1], q[0]), jnp.where(side, q[0], q[1])], axis=at + 1)
        q = [line(pair, self.side(at + 1) == 1) for pair in all_]
        side = self.side(at) == 1
        return jnp.concatenate([jnp.where(side, q[1], q[0]), jnp.where(side, q[0], q[1])], axis=at)

    def spread(self, a):
        return a.reshape((2,) * len(self.bits) + a.shape[1:])

    def halve(self, a, at):
        side = self.side(at)
        return lax.dynamic_index_in_dim(a, side, at, True), lax.dynamic_index_in_dim(a, 1 - side, at, True)

    def quarter(self, a, at):
        high, low = self.side(at), self.side(at + 1)
        pick = lambda i, j: lax.dynamic_index_in_dim(lax.dynamic_index_in_dim(a, i, at, True), j, at + 1, True)
        return pick(high, low), [pick(high, 1 - low), pick(1 - high, low), pick(1 - high, 1 - low)]

    def others(self, parts, at):
        axis, high = self.bits[at]
        low = self.bits[at + 1][1]
        masks = (low, high, high | low)
        return [lax.ppermute(a, axis, [(d, d ^ mask) for d in range(self.sizes[axis])]) for a, mask in zip(parts, masks)]

    def step(self, a, at, held=BF):
        mine, others = self.halve(a, at)
        return (mine.astype(F32) + self.other(others, at).astype(F32)).astype(held)

    def scatter(self, a, order):
        for at in order[:-1]:
            a = self.step(a, at)
        a = self.step(a, order[-1], F32)
        return a.reshape(a.shape[-2:])


def begin(shards, sums, ats):
    halves = [shards.halve(a, at) for a, at in zip(sums, ats)]
    return [mine for mine, _ in halves], [shards.other(others, at) for (_, others), at in zip(halves, ats)]


def add(mine, got, held=BF):
    return [(a.astype(F32) + b.astype(F32)).astype(held) for a, b in zip(mine, got)]


def together(a, b):
    return lax.optimization_barrier((a, b))


def repack(a, blocks):
    count = a.shape[0]
    if count == blocks:
        return a
    r, q = D // count, D // blocks
    parts = [a[:, j * r : (j + 1) * r].reshape(blocks, q, D) for j in range(9)]
    return jnp.concatenate(parts + [a[:, 9 * r :].reshape(blocks, 4 * q, D)], axis=1)


def per_device(rows_axis, n, inputs, *rest):
    weights, (cotangent, segments, context, feature_mask) = rest[:12], rest[12:]
    gain_one, shift_one, qkv_one, out_one, gain_two, shift_two, qkv_two, out_two, gain_three, shift_three, up, down = weights
    shards = Shards(rows_axis, n)
    _, feats, rows, _ = inputs.shape
    part = rows // n
    tot = n * feats
    me = lax.axis_index("feat").astype(jnp.int32)
    me_arr = me.reshape(1)

    core = (me % 2).reshape(1)
    vectors = (gain_one, shift_one, gain_two, shift_two, gain_three, shift_three)
    r = D // shards.count
    vectors = sum(jnp.pad(v, (j * r, 128 - (j + 1) * r)) for j, v in enumerate(vectors)).reshape(1, 128)
    first, pack = pack_shards(vectors, qkv_one, (out_one, qkv_two, out_two, up), down)
    pack = repack(lax.all_gather(pack, ("rows", "feat"), axis=0), D // ROWS_P)
    first = shards.gather(first, shards.feat_bits[:1])
    got, xs_at = exchange(inputs[0], me, n, first)
    first = shards.gather(first, shards.feat_bits[1:] + shards.rows_bits)
    got[0], first = together(got[0], first)
    xs_at = xs_at()
    first = shards.gather(first, [shards.near]).reshape(D, QKV + 128)
    gains = first.reshape(shards.count, r, QKV + 128)[:, 0, QKV : QKV + 6 * r].reshape(shards.count, 6, r)
    gains = gains.transpose(1, 0, 2).reshape(6, D).astype(F32)
    g1, b1, g2, b2, g3, b3 = [gains[j : j + 1] for j in range(6)]

    xs = [a for a, _ in xs_at]
    x_rows = jnp.stack([jnp.asarray(at, jnp.int32) for _, at in xs_at]) // RC
    order = me ^ jnp.arange(n, dtype=jnp.int32)
    valid = jnp.take(feature_mask[0].reshape(n, feats), order, axis=0).reshape(tot) > 0
    wide = -(-2 * tot // 128) * 128
    lane = jnp.arange(wide)
    same = (lane[None, :] // tot == jnp.arange(2 * tot)[:, None] // tot) & (lane < 2 * tot)[None, :]
    bias_one = jnp.where(same & jnp.pad(jnp.tile(valid, 2), (0, wide - 2 * tot))[None, :], 0.0, MASKED).astype(F32)
    bias_two = jnp.where(row_allowed(segments[0], context[0]), 0.0, MASKED).astype(F32)

    cut = feats // 2
    cuts = ((0, cut), (cut, feats))
    half = part // 2
    res = feature_forward(x_rows, xs, g1, b1, first, bias_one, cuts, part)
    qkv, p = res[2 * n :]
    h_a, h_b = swap(res[:n], n), swap(res[n : 2 * n], n)
    gains_two = (g2, b2, g3, b3)
    res = middle(me_arr, core, inputs, h_a, cotangent, bias_two, pack, *gains_two, 0, ((0, part),), [], False)
    output, gaf, carried = res[0], res[1], res[2 + n :]
    g_a = swap(res[2 : 2 + n], n)
    spans = ((0, half), (half, part))
    res = middle(me_arr, core, inputs, h_b, cotangent, bias_two, pack, *gains_two, cut, spans, [*carried, output, gaf], True)
    g_a, res = together(g_a, res)
    output, gaf = res[:2]
    g_b, g_c = swap(res[2 : 2 + n], n), swap(res[2 + n : 2 + 2 * n], n)
    mine, others, *vector_grads = res[2 + 2 * n :]

    wide_first, tall_first = shards.rows_bits[::-1], shards.rows_bits[-2::-1] + shards.rows_bits[-1:]
    if shards.count == D // ROWS_P:
        dpack = (mine.astype(F32) + shards.other(others, shards.near).astype(F32)).astype(BF)
        dpack = dpack.reshape((2,) * (len(shards.bits) - 1) + (1,) + dpack.shape[1:])
    else:
        dpack = jnp.where(core[0] == 0, jnp.stack((mine, others), 1), jnp.stack((others, mine), 1))
        dpack = shards.step(shards.spread(repack(dpack.reshape(pack.shape), shards.count)), shards.near)
    g_b, dpack = together(g_b, dpack)
    share = dpack.shape[-2] // 2 // ROWS_P * ROWS_P
    two = [dpack[..., :share, :], dpack[..., share:, :]]
    ways = [wide_first + shards.feat_bits, tall_first + shards.feat_bits]

    mine, got = begin(shards, two, [way[0] for way in ways])
    *d_a, acc, dg1, db1 = feature_backward(
        x_rows, xs, [(0, g_a), (0, g_b)], qkv, p, g1, b1, first, cuts, 0, half, [], []
    )
    got, d_a, g_c = lax.optimization_barrier((got, d_a, g_c))
    two = add(mine, got)
    two, g_c = together(two, g_c)

    mine, got = begin(shards, two, [way[1] for way in ways])
    d_a = swap(d_a, n)
    *d_b, dfirst = feature_backward(
        x_rows, xs, [(0, g_a), (half, g_c)], qkv, p, g1, b1, first, cuts, half, part, [acc, dg1, db1], vector_grads
    )
    got, d_a, d_b, dfirst = lax.optimization_barrier((got, d_a, d_b, dfirst))
    d_b = swap(d_b, n)
    dfirst = shards.step(shards.spread(dfirst.reshape(shards.count, -1, QKV + 128)), shards.near)
    two = add(mine, got)
    for i in range(2, len(ways[0]) - 2):
        two = add(*begin(shards, two, [way[i] for way in ways]))
    d_a, dfirst = together(d_a, dfirst)

    mine, got = begin(shards, [*two, dfirst], [way[-2] for way in ways] + wide_first[:1])
    input_grad = final(me_arr, gaf, d_a, 0, None)
    got, input_grad = together(got, input_grad)
    *two, dfirst = add(mine, got)
    last = wide_first[1:] + shards.feat_bits
    if len(last) == 3:
        two, dfirst = together(two, dfirst)
        mine, got = begin(shards, two, [way[-1] for way in ways])
        kept, others = shards.quarter(dfirst, last[1])
        others, d_b, got = lax.optimization_barrier((shards.others(others, last[1]), d_b, got))
        input_grad = final(me_arr, gaf, d_b, half, input_grad)
        others, input_grad, got = lax.optimization_barrier((others, input_grad, got))
        dfirst = sum([b.astype(F32) for b in others], kept.astype(F32)).astype(BF)
        last = last[2:]
    else:
        input_grad = final(me_arr, gaf, d_b, half, input_grad)
        mine, got = begin(shards, two, [way[-1] for way in ways])
    dpack = jnp.concatenate([a.reshape(a.shape[-2:]) for a in add(mine, got, F32)])
    dfirst = shards.scatter(dfirst, last)
    piece = lambda a, b: jnp.concatenate([dpack[j * r : (j + 1) * r] for j in range(a, b)], axis=1)
    v = [dfirst[:, QKV + j] for j in range(6)]
    return (
        output,
        input_grad,
        v[0],
        v[1],
        dfirst[:, :QKV],
        piece(0, 1),
        v[2],
        v[3],
        piece(1, 4),
        piece(4, 5),
        v[4],
        v[5],
        piece(5, 9),
        dpack[9 * r :],
    )


def solution(mesh):
    rows_axis, n = mesh.shape["rows"], mesh.shape["feat"]
    vec, mat, act, tab = P(("rows", "feat")), P(("rows", "feat"), None), P("rows", "feat", None, None), P("rows", None)
    weights = (vec, vec, mat, mat, vec, vec, mat, mat, vec, vec, mat, mat)
    return jax.shard_map(
        lambda *a: per_device(rows_axis, n, *a),
        mesh=mesh,
        in_specs=(act,) + weights + (act, tab, tab, tab),
        out_specs=(act, act) + weights,
        check_vma=False,
    )
```

time: 485 us -> 377 us (0.78)
  waiting for transfers between devices: 196 us -> 70.7 us
  Pallas kernels: 189 us -> 204 us
  starting transfers between devices: 29 us -> 42.5 us
  local copies, waits for them, and re-layouts: 30.9 us -> 22 us
    ppermute x12 -> x21, waiting for transfers between devices: 104 us -> 12.8 us  [swap(): lax.ppermute(arrays[k], 'feat', [(d, d ^ k) for d in range(n)])]
    ppermute x15, waiting for transfers between devices: 91.2 us -> 28.3 us  [other(): lax.ppermute(a, axis, [(d, d ^ bit) for d in range(self.sizes[axis])])]
    ppermute x0 -> x9, waiting for transfers between devices: none -> 29.6 us  [the longest x3 16.9 us: move(): lax.ppermute(sent, 'feat', [(d, d ^ bit) for d in range(n)])]
    pallas_call x4 -> x8, Pallas kernels: 189 us -> 204 us  [the longest x2 129 us: middle(): pl.pallas_call(lambda *r: middle_kernel(*r, n=n, rows=rows, part=part, sp...]
    ppermute x0 -> x9, starting transfers between devices: none -> 10.8 us  [the longest x3 4.52 us: others(): lax.ppermute(a, axis, [(d, d ^ mask) for d in range(self.sizes[axis])])]
    unnamed x55 -> x52, local copies, waits for them, and re-layouts: 11.7 us -> 4.54 us
    ppermute x12 -> x21, starting transfers between devices: 7.85 us -> 14.1 us  [swap(): lax.ppermute(arrays[k], 'feat', [(d, d ^ k) for d in range(n)])]
    convert_element_type x8 -> x11, other arithmetic: 10.1 us -> 10 us  [the longest x7 5.58 us: add(): (a.astype(F32) + b.astype(F32)).astype(held)]
  transfers between devices with their start and end apart: 28 -> 46, of which waited for: 16 -> 15; matrix products, arithmetic and copies ran while one was open for 7% -> 7% of each run, Pallas kernels for 13% -> 54%
where the time goes in v2:
time: 377 us; the launch traced here: 371 us
  Pallas kernels  204 us (54%)
  waiting for transfers between devices  70.7 us (19%)
  starting transfers between devices  42.5 us (11%)
  local copies, waits for them, and re-layouts  22 us (6%)
  other arithmetic  16.7 us (4%)
  between operations  15 us (4%)
    pallas_call x2, Pallas kernels, middle(): pl.pallas_call(lambda *r: middle_kernel(*r, n=n, rows=rows, part=part, sp...  129 us
    pallas_call x2, Pallas kernels, feature_backward(): pl.pallas_call(lambda *r: feature_backward_kernel(*r, n=n, feats=feats, c...  42.5 us
    ppermute x15, waiting for transfers between devices, other(): lax.ppermute(a, axis, [(d, d ^ bit) for d in range(self.sizes[axis])])  28.3 us
    pallas_call x1, Pallas kernels, feature_forward(): pl.pallas_call(lambda *r: feature_forward_kernel(*r, n=n, feats=feats, cu...  21.9 us
    ppermute x15, starting transfers between devices, other(): lax.ppermute(a, axis, [(d, d ^ bit) for d in range(self.sizes[axis])])  17.6 us
    ppermute x3, waiting for transfers between devices, move(): lax.ppermute(sent, 'feat', [(d, d ^ bit) for d in range(n)])  16.9 us
    ppermute x21, starting transfers between devices, swap(): lax.ppermute(arrays[k], 'feat', [(d, d ^ k) for d in range(n)])  14.1 us
    ppermute x21, waiting for transfers between devices, swap(): lax.ppermute(arrays[k], 'feat', [(d, d ^ k) for d in range(n)])  12.8 us
  transfers between devices with their start and end apart: 46, of which 15 were waited for; matrix products, arithmetic and copies ran while one was open for 7% of the time, Pallas kernels for 54%

profile of v2, /device:TPU:0, one launch (start us, length us, event | category | flops | bytes accessed | tf_op | source)
XLA Modules:
  0.0 371.1 jit_solution(3613722584565646617)
XLA Ops:
  10.4 1.7 pack.1
  12.0 2.5 collective-permute-start.1
  14.6 1.6 dynamic-slice_bitcast_fusion
  18.2 1.6 collective-permute-start.5
  19.9 2.5 collective-permute-start.3
  23.4 5.1 %collective-permute-done.3 = bf16[1,1,1,2,1,16,1664]{6,5,4,3,2,1,0:T(8,128)(2,1)S(1)} collective-permute-done((bf16[1,1,1,2,1,16,1664]{6,5,4,3,2,1,0:T(8,128)(2,1)S(1)}, bf16[1,1,1,2,1,16,1664]{6,5,4,3,2,1,0:T(8,128)(2,1)S(1)}, u32[]{:S(2)}, u32[]{:S(2)}) %collective-permute-start.3) | collective-permute-done | bytes 106528 | tf_op jit(solution)/shard_map/ppermute | solution.py:658
  28.5 7.2 %collective-permute-done.4 = bf16[1,1,1,2,1,16,1664]{6,5,4,3,2,1,0:T(8,128)(2,1)S(1)} collective-permute-done((bf16[1,1,1,2,1,16,1664]{6,5,4,3,2,1,0:T(8,128)(2,1)S(1)}, bf16[1,1,1,2,1,16,1664]{6,5,4,3,2,1,0:T(8,128)(2,1)S(1)}, u32[]{:S(2)}, u32[]{:S(2)}) %collective-permute-start.4) | collective-permute-done | bytes 106528 | tf_op jit(solution)/shard_map/ppermute | solution.py:658
  35.8 1.6 collective-permute-start.6
  37.6 11.5 %collective-permute-done.6 = bf16[2,2,1,2,1,16,1664]{6,5,4,3,2,1,0:T(8,128)(2,1)S(1)} collective-permute-done((bf16[2,2,1,2,1,16,1664]{6,5,4,3,2,1,0:T(8,128)(2,1)S(1)}, bf16[2,2,1,2,1,16,1664]{6,5,4,3,2,1,0:T(8,128)(2,1)S(1)}, u32[]{:S(2)}, u32[]{:S(2)}) %collective-permute-start.6) | collective-permute-done | bytes 426016 | tf_op jit(solution)/shard_map/ppermute | solution.py:634
  49.3 16.9 %collective-permute-done.2.r_3_ = bf16[12,128,512]{2,1,0:T(8,128)(2,1)} collective-permute-done((bf16[12,128,512]{2,1,0:T(8,128)(2,1)S(1)}, bf16[12,128,512]{2,1,0:T(8,128)(2,1)}, u32[]{:S(2)}, u32[]{:S(2)}) %collective-permute-start.2) | collective-permute-done | bytes 1572896 | tf_op jit(solution)/shard_map/ppermute | solution.py:602
  67.9 2.2 constant_dynamic-slice_fusion.14
  73.0 21.9 %feature_forward.1 = (bf16[6,64,512]{2,1,0:T(8,128)(2,1)}, bf16[6,64,512]{2,1,0:T(8,128)(2,1)}, bf16[6,64,512]{2,1,0:T(8,128)(2,1)}, bf16[6,64,512]{2,1,0:T(8,12...) custom-call(s32[4]{0:T(128)} %and_select_fusion.4.r_0_, ...), custom_call_target="tpu_custom_call" | custom-call | flops 99999997952 | bytes 1000000 | tf_op jit(solution)/shard_map/feature_forward/pallas_call | solution.py:129
  102.7 4.9 %collective-permute-done.10.r_5_ = bf16[6,64,512]{2,1,0:T(8,128)(2,1)S(1)} collective-permute-done((bf16[6,64,512]{2,1,0:T(8,128)(2,1)}, bf16[6,64,512]{2,1,0:T(8,128)(2,1)S(1)}, u32[]{:S(2)}, u32[]{:S(2)}) %collective-permute-start.10) | collective-permute-done | bytes 393248 | tf_op jit(solution)/shard_map/ppermute | solution.py:591
  107.6 7.2 %collective-permute-done.11.r_6_ = bf16[6,64,512]{2,1,0:T(8,128)(2,1)S(1)} collective-permute-done((bf16[6,64,512]{2,1,0:T(8,128)(2,1)}, bf16[6,64,512]{2,1,0:T(8,128)(2,1)S(1)}, u32[]{:S(2)}, u32[]{:S(2)}) %collective-permute-start.11) | collective-permute-done | bytes 393248 | tf_op jit(solution)/shard_map/ppermute | solution.py:591
  115.6 60.9 %middle.2 = (bf16[1,12,256,512]{3,2,1,0:T(8,128)(2,1)}, f32[12,256,512]{2,1,0:T(8,128)}, bf16[6,64,512]{2,1,0:T(8,128)(2,1)}, bf16[6,64,512]{2,1,0:T(8,128)(2,1)...) custom-call(s32[1]{0:T(128)} %bitcast.r_0_, ...), custom_call_target="tpu_custom_call" | custom-call | flops 99999997952 | bytes 1000000 | tf_op jit(solution)/shard_map/middle/pallas_call | solution.py:479
  179.9 67.8 %middle.3 = (bf16[1,12,256,512]{3,2,1,0:T(8,128)(2,1)}, f32[12,256,512]{2,1,0:T(8,128)}, bf16[6,32,512]{2,1,0:T(8,128)(2,1)}, bf16[6,32,512]{2,1,0:T(8,128)(2,1)...) custom-call(s32[1]{0:T(128)} %bitcast.r_0_, ...), custom_call_target="tpu_custom_call", output_to_operand_aliasing={{0}: (23, {}), {1}: (24, {})} | custom-call | flops 99999997952 | bytes 1000000 | tf_op jit(solution)/shard_map/middle/pallas_call | solution.py:479
  251.6 3.7 %collective-permute-done.21 = bf16[16,208,512]{2,1,0:T(8,128)(2,1)S(1)} collective-permute-done((bf16[16,208,512]{2,1,0:T(8,128)(2,1)}, bf16[16,208,512]{2,1,0:T(8,128)(2,1)S(1)}, u32[]{:S(2)}, u32[]{:S(2)}) %collective-permute-start.21) | collective-permute-done | bytes 3407904 | tf_op jit(solution)/shard_map/ppermute | solution.py:634
  256.5 3.0 add_convert_fusion
  266.1 20.7 %feature_backward.2 = (bf16[12,32,512]{2,1,0:T(8,128)(2,1)}, bf16[12,32,512]{2,1,0:T(8,128)(2,1)}, bf16[12,32,512]{2,1,0:T(8,128)(2,1)}, bf16[12,32,512]{2,1,0:T...) custom-call(s32[4]{0:T(128)} %and_select_fusion.4.r_0_, bf16[12,256,512]{2,1,0:T(8,128)(2,1)} %bitcast.56, ...), custom_call_target="tpu_custom_call" | custom-call | flops 99999997952 | bytes 1000000 | tf_op jit(solution)/shard_map/feature_backward/pallas_call | solution.py:240
  289.0 1.7 add_convert_fusion.1
  290.8 1.4 collective-permute-start.27
  292.3 2.4 collective-permute-start.28
  296.5 21.8 %feature_backward.3 = (bf16[12,32,512]{2,1,0:T(8,128)(2,1)}, bf16[12,32,512]{2,1,0:T(8,128)(2,1)}, bf16[12,32,512]{2,1,0:T(8,128)(2,1)}, bf16[12,32,512]{2,1,0:T(8,128)(2,1)}, bf16[512,1664]{1,0:T(8,128)(2,1)}) custom-call(s32[4]{0:T(128)} %and_select_fusion.4.r_0_, bf16[12,256,512]{2,1,0:T(8,128)(2,1)} %bitcast.57, ...), custom_call_target="tpu_custom_call" | custom-call | flops 99999997952 | bytes 1000000 | tf_op jit(solution)/shard_map/feature_backward/pallas_call | solution.py:240
  324.1 1.5 collective-permute-start.40
  327.0 1.5 collective-permute-start.35
  328.5 4.7 %final.2.r_6_ = f32[1,12,256,512]{3,2,1,0:T(8,128)} custom-call(s32[1]{0:T(128)} %bitcast.r_0_, f32[12,256,512]{2,1,0:T(8,128)} %get-tuple-element.257.r_1_, bf16[12,32,512]{2,1,0:T(8,128)(2,1)} %get-tuple-element.258.r_2_, bf16[12,32,512]{2,1,0:T(8,128)(2,1)} %copy-done.11, bf16[12,32,512]{2,1,0:T(8,128)(2,1)} %copy-done.12, ...), custom_call_target="tpu_custom_call" | custom-call | flops 99999997952 | bytes 1000000 | tf_op jit(solution)/shard_map/final/pallas_call | solution.py:538
  333.2 2.0 collective-permute-done.32
  335.5 4.7 %collective-permute-done.35 = bf16[2,2,1,2,1,16,1664]{6,5,4,3,2,1,0:T(8,128)(2,1)S(1)} collective-permute-done((bf16[2,2,1,2,1,16,1664]{6,5,4,3,2,1,0:T(8,128)(2,1)S(1)}, bf16[2,2,1,2,1,16,1664]{6,5,4,3,2,1,0:T(8,128)(2,1)S(1)}, u32[]{:S(2)}, u32[]{:S(2)}) %collective-permute-start.35) | collective-permute-done | bytes 426016 | tf_op jit(solution)/shard_map/ppermute | solution.py:634
  342.1 2.6 collective-permute-start.37
  345.9 1.4 collective-permute-start.43
  348.1 4.4 %collective-permute-done.42 = bf16[1,1,1,1,1,96,512]{6,5,4,3,2,1,0:T(8,128)(2,1)S(1)} collective-permute-done((bf16[1,1,1,1,1,96,512]{6,5,4,3,2,1,0:T(8,128)(2,1)S(1)}, bf16[1,1,1,1,1,96,512]{6,5,4,3,2,1,0:T(8,128)(2,1)S(1)}, u32[]{:S(2)}, u32[]{:S(2)}) %collective-permute-start.42) | collective-permute-done | bytes 98336 | tf_op jit(solution)/shard_map/ppermute | solution.py:634
  352.9 4.7 %final.3 = f32[1,12,256,512]{3,2,1,0:T(8,128)} custom-call(s32[1]{0:T(128)} %bitcast.r_0_, f32[12,256,512]{2,1,0:T(8,128)} %get-tuple-element.257.r_1_, bf16[12,32,512]{2,1,0:T(8,128)(2,1)} %get-tuple-element.275.r_2_, bf16[12,32,512]{2,1,0:T(8,128)(2,1)} %collective-permute-done.39.r_3_, ...), custom_call_target="tpu_custom_call", output_to_operand_aliasing={{}: (6, {})} | custom-call | flops 99999997952 | bytes 1000000 | tf_op jit(solution)/shard_map/final/pallas_call | solution.py:538
  (206 shorter events, 56.7 us)
Async XLA Ops:
  7.2 107.6 %all-gather.3.cloned.1.call-start = ((), (), s32[]{:S(2)}) async-start(), calls=%async_computation | async-start | bytes 7028736 | tf_op jit(solution)/shard_map/all_gather | solution.py:731
  8.5 64.4 %collective-permute-start = (bf16[12,64,512]{2,1,0:T(8,128)(2,1)S(1)}, bf16[12,64,512]{2,1,0:T(8,128)(2,1)}, u32[]{:S(2)}, u32[]{:S(2)}) collective-permute-start(bf16[12,64,512]{2,1,0:T(8,128)(2,1)S(1)} %dynamic-slice_bitcast_fusion.1), channel_id=1, source_target_pairs={{0,1},{1,0},{2,3},{3,2},{4,5},{5,4},{6,7},{7,6},{8,9},{9,8},{10,11... | collective-permute-start | bytes 2359304 | tf_op jit(solution)/shard_map/ppermute | solution.py:602
  22.3 13.3 %collective-permute-start.4 = (bf16[1,1,1,2,1,16,1664]{6,5,4,3,2,1,0:T(8,128)(2,1)S(1)}, bf16[1,1,1,2,1,16,1664]{6,5,4,3,2,1,0:T(8,128)(2,1)S(1)}, u32[]{:S(2)}, u32[]{:S(2)}) collective-permute-start(bf16[1,1,1,2,1,16,1664]{6,5,4,3,2,1,0:T(8,128)(2,1)S(1)} %pad_maximum_fusion.6), channel_id=1, source_target_pairs={{0,16},{4,20},{8,24},{12,28},{16,0},{20,4},{24,8},{28,12},{1,17},{... | collective-permute-start | bytes 319496 | tf_op jit(solution)/shard_map/ppermute | solution.py:658
  22.5 43.6 %collective-permute-start.2 = (bf16[12,128,512]{2,1,0:T(8,128)(2,1)S(1)}, bf16[12,128,512]{2,1,0:T(8,128)(2,1)}, u32[]{:S(2)}, u32[]{:S(2)}) collective-permute-start(bf16[12,128,512]{2,1,0:T(8,128)(2,1)S(1)} %dynamic-slice_bitcast_fusion), channel_id=1, source_target_pairs={{0,2},{1,3},{2,0},{3,1},{4,6},{5,7},{6,4},{7,5},{8,10},{9,11},{10,... | collective-permute-start | bytes 4718600 | tf_op jit(solution)/shard_map/ppermute | solution.py:602
  35.8 13.3 %collective-permute-start.6 = (bf16[2,2,1,2,1,16,1664]{6,5,4,3,2,1,0:T(8,128)(2,1)S(1)}, bf16[2,2,1,2,1,16,1664]{6,5,4,3,2,1,0:T(8,128)(2,1)S(1)}, u32[]{:S(2)}, u32[]{:S(2)}) collective-permute-start(bf16[2,2,1,2,1,16,1664]{6,5,4,3,2,1,0:T(8,128)(2,1)S(1)} %pad_maximum_fusion.2), channel_id=1, source_target_pairs={{0,4},{4,0},{8,12},{12,8},{16,20},{20,16},{24,28},{28,24},{1,5},{5... | collective-permute-start | bytes 1277960 | tf_op jit(solution)/shard_map/ppermute | solution.py:634
  95.4 12.2 %collective-permute-start.10 = (bf16[6,64,512]{2,1,0:T(8,128)(2,1)}, bf16[6,64,512]{2,1,0:T(8,128)(2,1)S(1)}, u32[]{:S(2)}, u32[]{:S(2)}) collective-permute-start(bf16[6,64,512]{2,1,0:T(8,128)(2,1)} %get-tuple-element.157), channel_id=1, source_target_pairs={{0,2},{1,3},{2,0},{3,1},{4,6},{5,7},{6,4},{7,5},{8,10},{9,11},{10,... | collective-permute-start | bytes 1179656 | tf_op jit(solution)/shard_map/ppermute | solution.py:591
  96.6 18.2 %collective-permute-start.11 = (bf16[6,64,512]{2,1,0:T(8,128)(2,1)}, bf16[6,64,512]{2,1,0:T(8,128)(2,1)S(1)}, u32[]{:S(2)}, u32[]{:S(2)}) collective-permute-start(bf16[6,64,512]{2,1,0:T(8,128)(2,1)} %get-tuple-element.158), channel_id=1, source_target_pairs={{0,3},{1,2},{2,1},{3,0},{4,7},{5,6},{6,5},{7,4},{8,11},{9,10},{10,... | collective-permute-start | bytes 1179656 | tf_op jit(solution)/shard_map/ppermute | solution.py:591
  100.6 78.2 %collective-permute-start.15 = (bf16[6,64,512]{2,1,0:T(8,128)(2,1)}, bf16[6,64,512]{2,1,0:T(8,128)(2,1)S(1)}, u32[]{:S(2)}, u32[]{:S(2)}) collective-permute-start(bf16[6,64,512]{2,1,0:T(8,128)(2,1)} %get-tuple-element.165), channel_id=1, source_target_pairs={{0,1},{1,0},{2,3},{3,2},{4,5},{5,4},{6,7},{7,6},{8,9},{9,8},{10,11... | collective-permute-start | bytes 1179656 | tf_op jit(solution)/shard_map/ppermute | solution.py:591
  101.3 77.7 %collective-permute-start.16 = (bf16[6,64,512]{2,1,0:T(8,128)(2,1)}, bf16[6,64,512]{2,1,0:T(8,128)(2,1)S(1)}, u32[]{:S(2)}, u32[]{:S(2)}) collective-permute-start(bf16[6,64,512]{2,1,0:T(8,128)(2,1)} %get-tuple-element.166), channel_id=1, source_target_pairs={{0,2},{1,3},{2,0},{3,1},{4,6},{5,7},{6,4},{7,5},{8,10},{9,11},{10,... | collective-permute-start | bytes 1179656 | tf_op jit(solution)/shard_map/ppermute | solution.py:591
  102.5 76.6 %collective-permute-start.17 = (bf16[6,64,512]{2,1,0:T(8,128)(2,1)}, bf16[6,64,512]{2,1,0:T(8,128)(2,1)S(1)}, u32[]{:S(2)}, u32[]{:S(2)}) collective-permute-start(bf16[6,64,512]{2,1,0:T(8,128)(2,1)} %get-tuple-element.167), channel_id=1, source_target_pairs={{0,3},{1,2},{2,1},{3,0},{4,7},{5,6},{6,5},{7,4},{8,11},{9,10},{10,... | collective-permute-start | bytes 1179656 | tf_op jit(solution)/shard_map/ppermute | solution.py:591
  176.5 71.2 %collective-permute-start.12 = (bf16[6,64,512]{2,1,0:T(8,128)(2,1)}, bf16[6,64,512]{2,1,0:T(8,128)(2,1)S(1)}, u32[]{:S(2)}, u32[]{:S(2)}) collective-permute-start(bf16[6,64,512]{2,1,0:T(8,128)(2,1)} %get-tuple-element.161), channel_id=1, source_target_pairs={{0,1},{1,0},{2,3},{3,2},{4,5},{5,4},{6,7},{7,6},{8,9},{9,8},{10,11... | collective-permute-start | bytes 1179656 | tf_op jit(solution)/shard_map/ppermute | solution.py:591
  177.6 70.1 %collective-permute-start.13 = (bf16[6,64,512]{2,1,0:T(8,128)(2,1)}, bf16[6,64,512]{2,1,0:T(8,128)(2,1)S(1)}, u32[]{:S(2)}, u32[]{:S(2)}) collective-permute-start(bf16[6,64,512]{2,1,0:T(8,128)(2,1)} %get-tuple-element.162), channel_id=1, source_target_pairs={{0,2},{1,3},{2,0},{3,1},{4,6},{5,7},{6,4},{7,5},{8,10},{9,11},{10,... | collective-permute-start | bytes 1179656 | tf_op jit(solution)/shard_map/ppermute | solution.py:591
  178.8 69.0 %collective-permute-start.14 = (bf16[6,64,512]{2,1,0:T(8,128)(2,1)}, bf16[6,64,512]{2,1,0:T(8,128)(2,1)S(1)}, u32[]{:S(2)}, u32[]{:S(2)}) collective-permute-start(bf16[6,64,512]{2,1,0:T(8,128)(2,1)} %get-tuple-element.163), channel_id=1, source_target_pairs={{0,3},{1,2},{2,1},{3,0},{4,7},{5,6},{6,5},{7,4},{8,11},{9,10},{10,... | collective-permute-start | bytes 1179656 | tf_op jit(solution)/shard_map/ppermute | solution.py:591
  249.5 10.7 %collective-permute-start.19 = (bf16[6,32,512]{2,1,0:T(8,128)(2,1)}, bf16[6,32,512]{2,1,0:T(8,128)(2,1)S(1)}, u32[]{:S(2)}, u32[]{:S(2)}) collective-permute-start(bf16[6,32,512]{2,1,0:T(8,128)(2,1)} %get-tuple-element.198), channel_id=1, source_target_pairs={{0,2},{1,3},{2,0},{3,1},{4,6},{5,7},{6,4},{7,5},{8,10},{9,11},{10,... | collective-permute-start | bytes 589832 | tf_op jit(solution)/shard_map/ppermute | solution.py:591
  251.3 35.5 %collective-permute-start.24 = (bf16[6,32,512]{2,1,0:T(8,128)(2,1)}, bf16[6,32,512]{2,1,0:T(8,128)(2,1)}, u32[]{:S(2)}, u32[]{:S(2)}) collective-permute-start(bf16[6,32,512]{2,1,0:T(8,128)(2,1)} %get-tuple-element.218), channel_id=1, source_target_pairs={{0,1},{1,0},{2,3},{3,2},{4,5},{5,4},{6,7},{7,6},{8,9},{9,8},{10,11... | collective-permute-start | bytes 589832 | tf_op jit(solution)/shard_map/ppermute | solution.py:591
  255.3 31.5 %collective-permute-start.25 = (bf16[6,32,512]{2,1,0:T(8,128)(2,1)}, bf16[6,32,512]{2,1,0:T(8,128)(2,1)}, u32[]{:S(2)}, u32[]{:S(2)}) collective-permute-start(bf16[6,32,512]{2,1,0:T(8,128)(2,1)} %get-tuple-element.219), channel_id=1, source_target_pairs={{0,2},{1,3},{2,0},{3,1},{4,6},{5,7},{6,4},{7,5},{8,10},{9,11},{10,... | collective-permute-start | bytes 589832 | tf_op jit(solution)/shard_map/ppermute | solution.py:591
  259.5 27.3 %collective-permute-start.26 = (bf16[6,32,512]{2,1,0:T(8,128)(2,1)}, bf16[6,32,512]{2,1,0:T(8,128)(2,1)S(1)}, u32[]{:S(2)}, u32[]{:S(2)}) collective-permute-start(bf16[6,32,512]{2,1,0:T(8,128)(2,1)} %get-tuple-element.220), channel_id=1, source_target_pairs={{0,3},{1,2},{2,1},{3,0},{4,7},{5,6},{6,5},{7,4},{8,11},{9,10},{10,... | collective-permute-start | bytes 589832 | tf_op jit(solution)/shard_map/ppermute | solution.py:591
  262.4 24.5 %collective-permute-start.22 = (bf16[2,2,1,2,1,96,512]{6,5,4,3,2,1,0:T(8,128)(2,1)}, bf16[2,2,1,2,1,96,512]{6,5,4,3,2,1,0:T(8,128)(2,1)}, u32[]{:S(2)}, u32[]{:S(2)}) collective-permute-start(bf16[2,2,1,2,1,96,512]{6,5,4,3,2,1,0:T(8,128)(2,1)} %constant_dynamic-slice_fusion.13), channel_id=1, source_target_pairs={{0,4},{4,0},{8,12},{12,8},{16,20},{20,16},{24,28},{28,24},{1,5},{5... | collective-permute-start | bytes 2359304 | tf_op jit(solution)/shard_map/ppermute | solution.py:634
  264.7 22.9 %collective-permute-start.23 = (bf16[2,1,2,2,1,112,512]{6,5,4,3,2,1,0:T(8,128)(2,1)}, bf16[2,1,2,2,1,112,512]{6,5,4,3,2,1,0:T(8,128)(2,1)}, u32[]{:S(2)}, u32[]{:S(2)}) collective-permute-start(bf16[2,1,2,2,1,112,512]{6,5,4,3,2,1,0:T(8,128)(2,1)} %constant_dynamic-slice_fusion.12), channel_id=1, source_target_pairs={{0,8},{4,12},{8,0},{12,4},{16,24},{20,28},{24,16},{28,20},{1,9},{5... | collective-permute-start | bytes 2752520 | tf_op jit(solution)/shard_map/ppermute | solution.py:634
  290.8 27.5 %collective-permute-start.27 = (bf16[2,1,1,2,1,96,512]{6,5,4,3,2,1,0:T(8,128)(2,1)S(1)}, bf16[2,1,1,2,1,96,512]{6,5,4,3,2,1,0:T(8,128)(2,1)}, u32[]{:S(2)}, u32[]{:S(2)}) collective-permute-start(bf16[2,1,1,2,1,96,512]{6,5,4,3,2,1,0:T(8,128)(2,1)S(1)} %constant_dynamic-slice_fusion.11), channel_id=1, source_target_pairs={{0,8},{4,12},{8,0},{12,4},{16,24},{20,28},{24,16},{28,20},{1,9},{5... | collective-permute-start | bytes 1179656 | tf_op jit(solution)/shard_map/ppermute | solution.py:634
  292.3 26.1 %collective-permute-start.28 = (bf16[1,1,2,2,1,112,512]{6,5,4,3,2,1,0:T(8,128)(2,1)S(1)}, bf16[1,1,2,2,1,112,512]{6,5,4,3,2,1,0:T(8,128)(2,1)S(1)}, u32[]{:S(2)}, u32[]{:S(2)}) collective-permute-start(bf16[1,1,2,2,1,112,512]{6,5,4,3,2,1,0:T(8,128)(2,1)S(1)} %constant_dynamic-slice_fusion.10), channel_id=1, source_target_pairs={{0,16},{4,20},{8,24},{12,28},{16,0},{20,4},{24,8},{28,12},{1,17},{... | collective-permute-start | bytes 1376264 | tf_op jit(solution)/shard_map/ppermute | solution.py:634
  294.7 23.7 %collective-permute-start.29 = (bf16[12,32,512]{2,1,0:T(8,128)(2,1)}, bf16[12,32,512]{2,1,0:T(8,128)(2,1)S(1)}, u32[]{:S(2)}, u32[]{:S(2)}) collective-permute-start(bf16[12,32,512]{2,1,0:T(8,128)(2,1)} %get-tuple-element.230), channel_id=1, source_target_pairs={{0,1},{1,0},{2,3},{3,2},{4,5},{5,4},{6,7},{7,6},{8,9},{9,8},{10,11... | collective-permute-start | bytes 1179656 | tf_op jit(solution)/shard_map/ppermute | solution.py:591
  294.7 23.7 %collective-permute-start.30 = (bf16[12,32,512]{2,1,0:T(8,128)(2,1)}, bf16[12,32,512]{2,1,0:T(8,128)(2,1)S(1)}, u32[]{:S(2)}, u32[]{:S(2)}) collective-permute-start(bf16[12,32,512]{2,1,0:T(8,128)(2,1)} %get-tuple-element.231), channel_id=1, source_target_pairs={{0,2},{1,3},{2,0},{3,1},{4,6},{5,7},{6,4},{7,5},{8,10},{9,11},{10,... | collective-permute-start | bytes 1179656 | tf_op jit(solution)/shard_map/ppermute | solution.py:591
  295.7 22.7 %collective-permute-start.31 = (bf16[12,32,512]{2,1,0:T(8,128)(2,1)}, bf16[12,32,512]{2,1,0:T(8,128)(2,1)}, u32[]{:S(2)}, u32[]{:S(2)}) collective-permute-start(bf16[12,32,512]{2,1,0:T(8,128)(2,1)} %get-tuple-element.232), channel_id=1, source_target_pairs={{0,3},{1,2},{2,1},{3,0},{4,7},{5,6},{6,5},{7,4},{8,11},{9,10},{10,... | collective-permute-start | bytes 1179656 | tf_op jit(solution)/shard_map/ppermute | solution.py:591
  322.8 12.5 %collective-permute-start.32 = (bf16[1,1,1,2,1,96,512]{6,5,4,3,2,1,0:T(8,128)(2,1)}, bf16[1,1,1,2,1,96,512]{6,5,4,3,2,1,0:T(8,128)(2,1)}, u32[]{:S(2)}, u32[]{:S(2)}) collective-permute-start(bf16[1,1,1,2,1,96,512]{6,5,4,3,2,1,0:T(8,128)(2,1)} %constant_dynamic-slice_fusion.9), channel_id=1, source_target_pairs={{0,16},{4,20},{8,24},{12,28},{16,0},{20,4},{24,8},{28,12},{1,17},{... | collective-permute-start | bytes 589832 | tf_op jit(solution)/shard_map/ppermute | solution.py:634
  323.5 11.9 %collective-permute-start.33 = (bf16[1,1,1,2,1,112,512]{6,5,4,3,2,1,0:T(8,128)(2,1)S(1)}, bf16[1,1,1,2,1,112,512]{6,5,4,3,2,1,0:T(8,128)(2,1)S(1)}, u32[]{:S(2)}, u32[]{:S(2)}) collective-permute-start(bf16[1,1,1,2,1,112,512]{6,5,4,3,2,1,0:T(8,128)(2,1)S(1)} %constant_dynamic-slice_fusion.8), channel_id=1, source_target_pairs={{0,4},{4,0},{8,12},{12,8},{16,20},{20,16},{24,28},{28,24},{1,5},{5... | collective-permute-start | bytes 688136 | tf_op jit(solution)/shard_map/ppermute | solution.py:634
  324.1 20.6 %collective-permute-start.39 = (bf16[12,32,512]{2,1,0:T(8,128)(2,1)}, bf16[12,32,512]{2,1,0:T(8,128)(2,1)}, u32[]{:S(2)}, u32[]{:S(2)}) collective-permute-start(bf16[12,32,512]{2,1,0:T(8,128)(2,1)} %get-tuple-element.267), channel_id=1, source_target_pairs={{0,1},{1,0},{2,3},{3,2},{4,5},{5,4},{6,7},{7,6},{8,9},{9,8},{10,11... | collective-permute-start | bytes 1179656 | tf_op jit(solution)/shard_map/ppermute | solution.py:591
  324.1 21.9 %collective-permute-start.40 = (bf16[12,32,512]{2,1,0:T(8,128)(2,1)}, bf16[12,32,512]{2,1,0:T(8,128)(2,1)}, u32[]{:S(2)}, u32[]{:S(2)}) collective-permute-start(bf16[12,32,512]{2,1,0:T(8,128)(2,1)} %get-tuple-element.268), channel_id=1, source_target_pairs={{0,2},{1,3},{2,0},{3,1},{4,6},{5,7},{6,4},{7,5},{8,10},{9,11},{10,... | collective-permute-start | bytes 1179656 | tf_op jit(solution)/shard_map/ppermute | solution.py:591
  327.0 13.2 %collective-permute-start.35 = (bf16[2,2,1,2,1,16,1664]{6,5,4,3,2,1,0:T(8,128)(2,1)S(1)}, bf16[2,2,1,2,1,16,1664]{6,5,4,3,2,1,0:T(8,128)(2,1)S(1)}, u32[]{:S(2)}, u32[]{:S(2)}) collective-permute-start(bf16[2,2,1,2,1,16,1664]{6,5,4,3,2,1,0:T(8,128)(2,1)S(1)} %constant_dynamic-slice_fusion.6), channel_id=1, source_target_pairs={{0,4},{4,0},{8,12},{12,8},{16,20},{20,16},{24,28},{28,24},{1,5},{5... | collective-permute-start | bytes 1277960 | tf_op jit(solution)/shard_map/ppermute | solution.py:634
  335.2 12.1 %collective-permute-start.41 = (bf16[12,32,512]{2,1,0:T(8,128)(2,1)S(1)}, bf16[12,32,512]{2,1,0:T(8,128)(2,1)S(1)}, u32[]{:S(2)}, u32[]{:S(2)}) collective-permute-start(bf16[12,32,512]{2,1,0:T(8,128)(2,1)S(1)} %copy-done.10), channel_id=1, source_target_pairs={{0,3},{1,2},{2,1},{3,0},{4,7},{5,6},{6,5},{7,4},{8,11},{9,10},{10,... | collective-permute-start | bytes 1179656 | tf_op jit(solution)/shard_map/ppermute | solution.py:591
  341.4 11.1 %collective-permute-start.36 = (bf16[1,1,1,2,1,16,1664]{6,5,4,3,2,1,0:T(8,128)(2,1)S(1)}, bf16[1,1,1,2,1,16,1664]{6,5,4,3,2,1,0:T(8,128)(2,1)S(1)}, u32[]{:S(2)}, u32[]{:S(2)}) collective-permute-start(bf16[1,1,1,2,1,16,1664]{6,5,4,3,2,1,0:T(8,128)(2,1)S(1)} %get-tuple-element.302), channel_id=1, source_target_pairs={{0,8},{4,12},{8,0},{12,4},{16,24},{20,28},{24,16},{28,20},{1,9},{5... | collective-permute-start | bytes 319496 | tf_op jit(solution)/shard_map/ppermute | solution.py:681
  342.1 10.8 %collective-permute-start.37 = (bf16[1,1,1,2,1,16,1664]{6,5,4,3,2,1,0:T(8,128)(2,1)S(1)}, bf16[1,1,1,2,1,16,1664]{6,5,4,3,2,1,0:T(8,128)(2,1)S(1)}, u32[]{:S(2)}, u32[]{:S(2)}) collective-permute-start(bf16[1,1,1,2,1,16,1664]{6,5,4,3,2,1,0:T(8,128)(2,1)S(1)} %get-tuple-element.301), channel_id=1, source_target_pairs={{0,16},{4,20},{8,24},{12,28},{16,0},{20,4},{24,8},{28,12},{1,17},{... | collective-permute-start | bytes 319496 | tf_op jit(solution)/shard_map/ppermute | solution.py:681
  (39 other events, 260.7 us)
Sparse Core Ops, SparseCore 0:
  14.7 79.7 all-gather.2

commit v3 on v2

--- a/solution.py
+++ b/solution.py
@@ -1,3 +1,5 @@
+import math
+
 import jax
 import jax.numpy as jnp
 import numpy as np
@@ -19,12 +21,13 @@
 LOG2E = float(np.log2(np.e))
 VMEM = 60 * 1024 * 1024
 
-GRP2 = 4
+GRP2 = 8
 GRP = 4
+SHARE = 112
 ROWS_P = 16
 COST = pl.CostEstimate(flops=10**11, bytes_accessed=10**6, transcendentals=0)
 RC = 16
-FCH = 512
+FCH = 256
 FB = 2
 
 
@@ -72,13 +75,13 @@
     return h * cdf, cdf + h * e * (2 * np.pi) ** -0.5
 
 
-def put_rows(ref, start, x):
-    for c in range(HEADS):
-        ref[c, start : start + x.shape[0]] = x[:, c * 128 : c * 128 + 128]
-
-
-def get_row(ref, r, tot):
-    return jnp.concatenate([ref[c, pl.ds(r, tot, stride=RC), :] for c in range(HEADS)], axis=1)
+def by_rows(parts):
+    a = jnp.swapaxes(jnp.concatenate(parts, axis=0), 0, 1)
+    return a.reshape(a.shape[0] * a.shape[1], D)
+
+
+def by_features(a, tot):
+    return jnp.swapaxes(a.reshape(a.shape[0] // tot, tot, D), 0, 1)
 
 
 def full(shape):
@@ -92,11 +95,11 @@
     tot = n * feats
     pair = 2 * tot
     wide = bias.shape[1]
-    for k in range(n):
-        put_rows(xs, k * feats * RC, x_refs[k][...].reshape(feats * RC, D).astype(F32))
+    xs[...] = by_rows([x_refs[k][...] for k in range(n)])
     for r in range(RC):
-        xhat, _ = norm(get_row(xs, r, tot))
-        low[r * tot : (r + 1) * tot] = (xhat * gain[...] + shift[...]).astype(BF)
+        at = slice(r * tot, (r + 1) * tot)
+        xhat, _ = norm(xs[at].astype(F32))
+        low[at] = (xhat * gain[...] + shift[...]).astype(BF)
     rows = tot * RC
     qkv_ref[0, :rows] = mm(low[...], wqkv[...]).astype(BF)
     qkv_ref[0, rows:] = jnp.zeros((qkv_ref.shape[1] - rows, QKV), BF)
@@ -110,13 +113,11 @@
         os = [mm(p, qkv_ref[at(b, h, 2, wide)]) for p, (b, h) in zip(ps, jobs)]
         for p, o, (b, h) in zip(ps, os, jobs):
             p_ref[0, b, h] = p
-            for j in range(2):
-                hs[h, pl.ds(2 * b + j, tot, stride=RC), :] = o[j * tot : (j + 1) * tot]
+            hs[b * pair : (b + 1) * pair, h * 128 : h * 128 + 128] = o.astype(BF)
+    heads = by_features(hs[...], tot)
     for c, (f0, f1) in enumerate(cuts):
         for k in range(n):
-            for h in range(HEADS):
-                part = hs[h, (k * feats + f0) * RC : (k * feats + f1) * RC].reshape(f1 - f0, RC, 128)
-                h_refs[c * n + k][:, :, h * 128 : h * 128 + 128] = part.astype(BF)
+            h_refs[c * n + k][...] = heads[k * feats + f0 : k * feats + f1]
 
 
 def feature_forward(x_rows, xs, gain, shift, wqkv, bias, cuts, rows):
@@ -139,9 +140,9 @@
                 pl.BlockSpec((1, RC // 2, HEADS, 2 * tot, bias.shape[1]), lambda i, at: (i, 0, 0, 0, 0)),
             ],
             scratch_shapes=[
-                pltpu.VMEM((HEADS, tot * RC, 128), F32),
                 pltpu.VMEM((tot * RC, D), BF),
-                pltpu.VMEM((HEADS, tot * RC, 128), F32),
+                pltpu.VMEM((tot * RC, D), BF),
+                pltpu.VMEM((tot * RC, D), BF),
             ],
         ),
         out_shape=[sds((f1 - f0, rows, D), BF) for f0, f1 in cuts for _ in range(n)]
@@ -152,7 +153,7 @@
     )(x_rows, *xs, gain, shift, wqkv, bias)
 
 
-def feature_backward_kernel(_, *refs, n, feats, cuts, first, last):
+def feature_backward_kernel(at_ref, *refs, n, feats, cuts, first, last):
     it = iter(refs)
     take = lambda c: [next(it) for _ in range(c)]
     x_refs = take(n)
@@ -161,8 +162,8 @@
     carried = [] if first else take(3)
     others = take(4) if last else []
     d_refs = take(n)
-    outs = take(1) if last else take(3)
-    dgain, dshift, vecs, xs, gs, ns, low, gh, gqkv, acc = take(10)
+    outs = take(2) if last else take(3)
+    dgain, dshift, vecs, xs, xh, rs, ns, low, gh, gqkv, acc = take(11)
     if not last:
         acc, dgain, dshift = outs
     tot = n * feats
@@ -175,14 +176,14 @@
         for j, a in enumerate((acc, dgain, dshift)):
             a[...] = jnp.zeros_like(a) if first else carried[j][...]
 
-    for k in range(n):
-        put_rows(xs, k * feats * RC, x_refs[k][...].reshape(feats * RC, D).astype(F32))
-        for c, (f0, f1) in enumerate(cuts):
-            put_rows(gs, (k * feats + f0) * RC, g_refs[c * n + k][...].reshape((f1 - f0) * RC, D).astype(F32))
+    xs[...] = by_rows([x_refs[k][...] for k in range(n)])
+    gh[...] = by_rows([g_refs[c * n + k][...] for k in range(n) for c in range(len(cuts))])
     for r in range(RC):
-        gh[r * tot : (r + 1) * tot] = get_row(gs, r, tot).astype(BF)
-        xhat, _ = norm(get_row(xs, r, tot))
-        low[r * tot : (r + 1) * tot] = (xhat * gain[...] + shift[...]).astype(BF)
+        at = slice(r * tot, (r + 1) * tot)
+        xhat, rstd = norm(xs[at].astype(F32))
+        xh[at] = xhat
+        rs[at] = jnp.broadcast_to(rstd, (tot, 128))
+        low[at] = (xhat * gain[...] + shift[...]).astype(BF)
     for b0 in range(0, RC // 2, GRP):
         jobs = [(b, h) for b in range(b0, b0 + GRP) for h in range(HEADS)]
         at = lambda b, h, c, w: (0, slice(b * pair, b * pair + w), slice(c * D + h * 128, c * D + h * 128 + 128))
@@ -202,26 +203,31 @@
     acc[...] += tm(low[...], gqkv[...])
     ns[...] = mt(gqkv[...], wqkv[...])
     for r in range(RC):
-        xhat, rstd = norm(get_row(xs, r, tot))
-        nn = ns[r * tot : (r + 1) * tot]
+        at = slice(r * tot, (r + 1) * tot)
+        xhat = xh[at]
+        nn = ns[at]
         dgain[...] += fold8(nn * xhat)
         dshift[...] += fold8(nn)
-        d = norm_back(nn, xhat, rstd, gain[...])
-        for c in range(HEADS):
-            xs[c, pl.ds(r, tot, stride=RC), :] = d[:, c * 128 : c * 128 + 128]
+        xs[at] = norm_back(nn, xhat, rs[at, :1], gain[...]).astype(BF)
+    back = by_features(xs[...], tot)
     for k in range(n):
-        for c in range(HEADS):
-            d_refs[k][:, :, c * 128 : c * 128 + 128] = xs[c, k * feats * RC : (k + 1) * feats * RC].reshape(feats, RC, 128).astype(BF)
+        d_refs[k][...] = back[k * feats : (k + 1) * feats]
 
     if last:
 
         @pl.when(i == pl.num_programs(0) - 1)
         def _():
-            outs[0][:, :QKV] = acc[...].astype(BF)
+            core = at_ref[n]
             vecs[...] = jnp.zeros_like(vecs)
             for j, v in enumerate([dgain, dshift] + others):
                 vecs[j : j + 1] = jnp.sum(v[...], axis=0, keepdims=True)
-            outs[0][:, QKV:] = vecs[...].T.astype(BF)
+            turned = vecs[...].T.astype(BF).reshape(D // (2 * ROWS_P), 2, ROWS_P, 128)
+            outs[0][:, :, QKV:] = jnp.where(core == 0, turned[:, 0], turned[:, 1])
+            outs[1][:, :, QKV:] = jnp.where(core == 0, turned[:, 1], turned[:, 0])
+            for b in range(D // (2 * ROWS_P)):
+                for side, ref in ((core, outs[0]), (1 - core, outs[1])):
+                    row = pl.multiple_of((2 * b + side) * ROWS_P, ROWS_P)
+                    ref[b, :, :QKV] = acc[pl.ds(row, ROWS_P), :].astype(BF)
 
 
 def feature_backward(x_rows, xs, gs, qkv, p, gain, shift, wqkv, cuts, r0, r1, carried, others):
@@ -234,7 +240,8 @@
     at = lambda f, row: pl.BlockSpec((f, RC, D), lambda i, _: (0, i + (r0 - row) // RC, 0))
     sums = [(D, QKV), (8, D), (8, D)]
     if last:
-        out_specs, out_shape = [pl.BlockSpec((D, QKV + 128), lambda i, _: (0, 0))], [sds((D, QKV + 128), BF)]
+        each = (D // (2 * ROWS_P), ROWS_P, QKV + 128)
+        out_specs, out_shape = [pl.BlockSpec(each, lambda i, _: (0, 0, 0))] * 2, [sds(each, BF)] * 2
     else:
         out_specs, out_shape = [pl.BlockSpec(q, lambda i, _: (0, 0)) for q in sums], [sds(q, F32) for q in sums]
     return pl.pallas_call(
@@ -258,8 +265,9 @@
                 pltpu.VMEM((8, D), F32),
                 pltpu.VMEM((8, D), F32),
                 pltpu.VMEM((128, D), F32),
-                pltpu.VMEM((HEADS, tot * RC, 128), F32),
-                pltpu.VMEM((HEADS, tot * RC, 128), F32),
+                pltpu.VMEM((tot * RC, D), BF),
+                pltpu.VMEM((tot * RC, D), F32),
+                pltpu.VMEM((tot * RC, 128), F32),
                 pltpu.VMEM((tot * RC, D), F32),
                 pltpu.VMEM((tot * RC, D), BF),
                 pltpu.VMEM((tot * RC, D), BF),
@@ -298,17 +306,17 @@
     return copies
 
 
-def middle_kernel(me_ref, core_ref, *refs, n, rows, part, spans, first, last):
+def middle_kernel(me_ref, core_ref, *refs, n, rows, part, spans, first):
     it = iter(refs)
     take = lambda c: [next(it) for _ in range(c)]
     (x_ref,) = take(1)
     h_refs = take(n)
     cot_ref, bias, pack, g2, b2, g3, b3 = take(7)
-    carried = [] if first else take(9)
+    carried = [] if first else take(6)
     _ = [] if first else take(2)
     out_ref, gaf_ref = take(2)
     gh_refs = take(n * len(spans))
-    kept = take(2) if last else take(5)
+    kept = take(2)
     dg2, db2, dg3, db3 = take(4)
     h1_s, qkv_s, p_s, gq_s, heads_s, gh2_s, afo, arq, aro, ain, aout, wfo_s, wrq_s, wro_s, win_s, wout_s, sems, asems = take(18)
     i = pl.program_id(0)
@@ -321,15 +329,13 @@
         copies = unpack_copies(pack, (wfo_s, wrq_s, wro_s, win_s, wout_s), sems)
         for c in copies:
             c.start()
-        if first:
-            for a in (afo, arq, aro, ain, aout, dg2, db2, dg3, db3):
-                a[...] = jnp.zeros_like(a)
-        else:
-            more = [pltpu.make_async_copy(c, a, asems.at[j]) for j, (c, a) in enumerate(zip(carried, accs))]
-            for c in more:
-                c.start()
-            for c, a in zip(carried[5:], (dg2, db2, dg3, db3)):
-                a[...] = c[...]
+        for a in (afo, arq, aro, ain, aout):
+            a[...] = jnp.zeros_like(a)
+        for j, a in enumerate((dg2, db2, dg3, db3)):
+            a[...] = jnp.zeros_like(a) if first else carried[2 + j][...]
+        if not first:
+            for j in range(2):
+                pltpu.make_async_copy(carried[j], kept[j], asems.at[j]).start()
 
     def need(*which):
         @pl.when(i == 0)
@@ -340,22 +346,6 @@
                     if j in which:
                         pltpu.make_async_copy(pack.at[:, pl.ds(0, w.shape[1]), :], w.at[:, :, pl.ds(0, D)], sems.at[at]).wait()
                     at += 1
-
-    def settle(*which):
-        if not first:
-
-            @pl.when(i == 0)
-            def _():
-                for j in which:
-                    pltpu.make_async_copy(carried[j], accs[j], asems.at[j]).wait()
-
-    def keep(*which):
-        if not last:
-
-            @pl.when(i == pl.num_programs(0) - 1)
-            def _():
-                for j in which:
-                    pltpu.make_async_copy(accs[j], kept[j], asems.at[j]).start()
 
     wfo, wrq, wro, win, wout = (Flat(w) for w in (wfo_s, wrq_s, wro_s, win_s, wout_s))
     for k in range(n):
@@ -369,7 +359,6 @@
     xhat2, rstd2 = norm(after_feat)
     low2 = (xhat2 * g2[...] + b2[...]).astype(BF)
     need(1, 2, 3, 4)
-    settle(3, 4)
     qkv_s[...] = mm(low2, wrq[...]).astype(BF)
     mask = bias[...]
     jobs = [(f, h) for f in range(FB) for h in range(HEADS)]
@@ -389,25 +378,33 @@
     cot = cot_ref[0].reshape(m, D)
     out = after_row
     n3 = None
-    for j in range(FF // FCH):
-        cols = slice(j * FCH, (j + 1) * FCH)
-        act, slope = gelu_pair(mm(low3, win[:, cols]))
-        act = act.astype(BF)
-        out = out + mm(act, wout[cols, :])
-        ghid = (mt(cot, wout[cols, :]) * slope).astype(BF)
-        aout[:, cols] += tm(cot, act)
-        ain[:, cols] += tm(low3, ghid)
-        back = mt(ghid, win[:, cols])
-        n3 = back if n3 is None else n3 + back
-    keep(3, 4)
+    chunks = [slice(j * FCH, (j + 1) * FCH) for j in range(FF // FCH)]
+    hid = mm(low3, win[:, chunks[0]])
+    gact = mt(cot, wout[chunks[0], :])
+    waiting = None
+    for j, cols in enumerate(chunks + [None]):
+        if cols is not None:
+            act, slope = gelu_pair(hid)
+            act = act.astype(BF)
+            ghid = (gact * slope).astype(BF)
+            if j + 1 < len(chunks):
+                hid = mm(low3, win[:, chunks[j + 1]])
+                gact = mt(cot, wout[chunks[j + 1], :])
+        if waiting is not None:
+            a0, g0, c0 = waiting
+            out = out + mm(a0, wout[c0, :])
+            back = mt(g0, win[:, c0])
+            n3 = back if n3 is None else n3 + back
+            aout[:, c0] += tm(cot, a0)
+            ain[:, c0] += tm(low3, g0)
+        waiting = (act, ghid, cols)
     out_ref[0] = out.astype(BF).reshape(FB, rows, D)
     dg3[...] += fold8(n3 * xhat3)
     db3[...] += fold8(n3)
     g_row = cot.astype(F32) + norm_back(n3, xhat3, rstd3, g3[...])
     gb = g_row.astype(BF)
-    settle(0, 1, 2)
+    gh2_s[...] = mt(gb, wro[...]).astype(BF)
     aro[...] += tm(heads, gb)
-    gh2_s[...] = mt(gb, wro[...]).astype(BF)
     for g0 in range(0, len(jobs), GRP2):
         some = jobs[g0 : g0 + GRP2]
         gs = [gh2_s[at(f, h, 0)] for f, h in some]
@@ -420,15 +417,14 @@
             gq_s[at(f, h, 0)] = (mm(ds, qkv_s[at(f, h, 1)]) * SCALE).astype(BF)
             gq_s[at(f, h, 1)] = (tm(ds, qkv_s[at(f, h, 0)]) * SCALE).astype(BF)
     gq = gq_s[...]
-    arq[...] += tm(low2, gq)
     n2 = mt(gq, wrq[...])
     dg2[...] += fold8(n2 * xhat2)
     db2[...] += fold8(n2)
     g_feat = g_row + norm_back(n2, xhat2, rstd2, g2[...])
-    gaf_ref[...] = g_feat.reshape(FB, rows, D)
     gf = g_feat.astype(BF)
+    gaf_ref[...] = gf.reshape(FB, rows, D)
+    arq[...] += tm(low2, gq)
     afo[...] += tm(h1, gf)
-    keep(0, 1, 2)
     h1_s[...] = mt(gf, wfo[...]).astype(BF)
     for k in range(n):
         for f in range(FB):
@@ -438,29 +434,32 @@
 
     @pl.when(i == pl.num_programs(0) - 1)
     def _():
-        if not last:
-            for j in range(5):
-                pltpu.make_async_copy(accs[j], kept[j], asems.at[j]).wait()
-        else:
-            core = core_ref[0]
-            at = 0
-            for acc in accs[:4]:
-                for j in range(acc.shape[1] // D):
-                    for b in range(D // (2 * ROWS_P)):
-                        for side, ref in ((core, kept[0]), (1 - core, kept[1])):
-                            row = pl.multiple_of((2 * b + side) * ROWS_P, ROWS_P)
-                            ref[b, at : at + ROWS_P, :] = acc[pl.ds(row, ROWS_P), j * D : (j + 1) * D].astype(BF)
-                    at += ROWS_P
-            for j in range(FF // D):
-                unit = jnp.where(lax.broadcasted_iota(jnp.int32, (D, D), 0) == lax.broadcasted_iota(jnp.int32, (D, D), 1), 1.0, 0.0)
-                turned = mt(unit.astype(BF), aout[:, j * D : (j + 1) * D].astype(BF)).astype(BF).reshape(4, 2, 4 * ROWS_P, D)
-                even, odd = turned[:, 0], turned[:, 1]
-                blocks = slice(j * 4, (j + 1) * 4)
-                kept[0][blocks, at:, :] = jnp.where(core == 0, even, odd)
-                kept[1][blocks, at:, :] = jnp.where(core == 0, odd, even)
-
-
-def middle(me, core, x, hs, cot, bias, pack, g2, b2, g3, b3, f0, spans, carried, last):
+        if not first:
+            for j in range(2):
+                pltpu.make_async_copy(carried[j], kept[j], asems.at[j]).wait()
+
+        def put(ref, blocks, at, a):
+            ref[blocks, at] = (a if first else a + ref[blocks, at].astype(F32)).astype(BF)
+
+        core = core_ref[0]
+        row = 0
+        for acc in accs[:4]:
+            for j in range(acc.shape[1] // D):
+                for b in range(D // (2 * ROWS_P)):
+                    for side, ref in ((core, kept[0]), (1 - core, kept[1])):
+                        here = pl.multiple_of((2 * b + side) * ROWS_P, ROWS_P)
+                        put(ref, b, slice(row, row + ROWS_P), acc[pl.ds(here, ROWS_P), j * D : (j + 1) * D])
+                row += ROWS_P
+        unit = jnp.where(lax.broadcasted_iota(jnp.int32, (D, D), 0) == lax.broadcasted_iota(jnp.int32, (D, D), 1), 1.0, 0.0)
+        for j in range(FF // D):
+            turned = mt(unit.astype(BF), aout[:, j * D : (j + 1) * D].astype(BF)).reshape(4, 2, 4 * ROWS_P, D)
+            even, odd = turned[:, 0], turned[:, 1]
+            blocks = slice(j * 4, (j + 1) * 4)
+            put(kept[0], blocks, slice(row, None), jnp.where(core == 0, even, odd))
+            put(kept[1], blocks, slice(row, None), jnp.where(core == 0, odd, even))
+
+
+def middle(me, core, x, hs, cot, bias, pack, g2, b2, g3, b3, f0, spans, carried):
     n = len(hs)
     _, feats, rows, _ = x.shape
     part = rows // n
@@ -472,19 +471,19 @@
     hblk = lambda r: pl.BlockSpec((FB, r, D), lambda i, *_: (i, 0, 0))
     sds = jax.ShapeDtypeStruct
     sums = [(D, D), (D, QKV), (D, D), (D, FF), (D, FF)]
-    half = (pack.shape[0] // 2,) + pack.shape[1:]
-    kept_specs = [pl.BlockSpec(half, lambda i, *_: (0, 0, 0))] * 2 if last else [any_] * 5
-    kept_shape = [sds(half, BF)] * 2 if last else [sds(q, F32) for q in sums]
+    halves = [(pack.shape[0] // 2,) + pack.shape[1:]] * 2
+    kept_specs = [pl.BlockSpec(q, lambda i, *_: (0, 0, 0)) for q in halves]
+    kept_shape = [sds(q, BF) for q in halves]
     args = [x, *hs, cot, bias, pack, g2, b2, g3, b3, *carried]
     return pl.pallas_call(
-        lambda *r: middle_kernel(*r, n=n, rows=rows, part=part, spans=spans, first=first, last=last),
+        lambda *r: middle_kernel(*r, n=n, rows=rows, part=part, spans=spans, first=first),
         grid_spec=pltpu.PrefetchScalarGridSpec(
             num_scalar_prefetch=2,
             grid=(count // FB,),
             in_specs=[xblk]
             + [hblk(part)] * n
             + [xblk, full((rows, rows)), any_, full((1, D)), full((1, D)), full((1, D)), full((1, D))]
-            + ([] if first else [any_] * 5 + [full((8, D))] * 4 + [any_] * 2),
+            + ([] if first else [any_] * 2 + [full((8, D))] * 4 + [any_] * 2),
             out_specs=[xblk, pl.BlockSpec((FB, rows, D), lambda i, *_: (i + f0 // FB, 0, 0))]
             + [hblk(r1 - r0) for r0, r1 in spans for _ in range(n)]
             + kept_specs
@@ -505,10 +504,10 @@
                 pltpu.VMEM((32, ROWS_P, FF), BF),
                 pltpu.VMEM((32, 4 * ROWS_P, D), BF),
                 pltpu.SemaphoreType.DMA((10,)),
-                pltpu.SemaphoreType.DMA((5,)),
+                pltpu.SemaphoreType.DMA((2,)),
             ],
         ),
-        out_shape=[sds(x.shape, BF), sds((feats, rows, D), F32)]
+        out_shape=[sds(x.shape, BF), sds((feats, rows, D), BF)]
         + [sds((count, r1 - r0, D), BF) for r0, r1 in spans for _ in range(n)]
         + kept_shape
         + [sds((8, D), F32)] * 4,
@@ -522,10 +521,8 @@
 def final_kernel(me_ref, g_ref, *refs, n):
     out = refs[-1]
     for k in range(n):
-
-        @pl.when(pl.program_id(0) == k)
-        def _():
-            out[0] = g_ref[...] + refs[k][...].astype(F32)
+        at = pl.ds(me_ref[0] ^ k, 1)
+        out[0, :, at, 0] = g_ref[:, at, 0].astype(F32) + refs[k][...][:, None].astype(F32)
 
 
 def final(me, g, ds, r0, before):
@@ -533,24 +530,25 @@
     feats, rows, _ = g.shape
     count = ds[0].shape[1]
     each = rows // n // count
-    place = lambda i, me: (me[0] ^ i) * each + r0 // count
-    more = [] if before is None else [before]
-    return pl.pallas_call(
+    fb = next(q for q in (4, 3, 2, 1) if feats % q == 0)
+    more = [] if before is None else [before.reshape(1, feats, n, each, count, D)]
+    out = pl.pallas_call(
         lambda *r: final_kernel(*r, n=n),
         grid_spec=pltpu.PrefetchScalarGridSpec(
             num_scalar_prefetch=1,
-            grid=(n,),
-            in_specs=[pl.BlockSpec((feats, count, D), lambda i, me: (0, place(i, me), 0))]
-            + [full((feats, count, D))] * n
+            grid=(feats // fb,),
+            in_specs=[pl.BlockSpec((fb, n, 1, count, D), lambda i, me: (i, 0, r0 // count, 0, 0))]
+            + [pl.BlockSpec((fb, count, D), lambda i, me: (i, 0, 0))] * n
             + [pl.BlockSpec(memory_space=pl.ANY)] * len(more),
-            out_specs=pl.BlockSpec((1, feats, count, D), lambda i, me: (0, 0, place(i, me), 0)),
+            out_specs=pl.BlockSpec((1, fb, n, 1, count, D), lambda i, me: (0, i, 0, r0 // count, 0, 0)),
         ),
-        out_shape=jax.ShapeDtypeStruct((1, feats, rows, D), F32),
+        out_shape=jax.ShapeDtypeStruct((1, feats, n, each, count, D), F32),
         input_output_aliases={2 + n: 0} if more else {},
         compiler_params=pltpu.CompilerParams(vmem_limit_bytes=VMEM),
         cost_estimate=COST,
         name="final",
-    )(me, g, *ds, *more)
+    )(me, g.reshape(feats, n, each, count, D), *ds, *more)
+    return out.reshape(1, feats, rows, D)
 
 
 def pack_kernel(*refs):
@@ -591,14 +589,12 @@
     return [arrays[0]] + [lax.ppermute(arrays[k], "feat", [(d, d ^ k) for d in range(n)]) for k in range(1, n)]
 
 
-def exchange(x, me, n, after):
+def exchange(x, me, n):
     feats, rows, _ = x.shape
 
     def move(a, at, rows, bit):
         low = ((me // bit) % 2) * rows
         sent = lax.dynamic_slice(a, (0, at + rows - low, 0), (feats, rows, D))
-        if bit == n // 2:
-            sent, _ = together(sent, after)
         return lax.ppermute(sent, "feat", [(d, d ^ bit) for d in range(n)]), at + low
 
     bit = n // 2
@@ -662,12 +658,9 @@
         side = self.side(at) == 1
         return jnp.concatenate([jnp.where(side, q[1], q[0]), jnp.where(side, q[0], q[1])], axis=at)
 
-    def spread(self, a):
-        return a.reshape((2,) * len(self.bits) + a.shape[1:])
-
     def halve(self, a, at):
         side = self.side(at)
-        return lax.dynamic_index_in_dim(a, side, at, True), lax.dynamic_index_in_dim(a, 1 - side, at, True)
+        return [lax.dynamic_index_in_dim(a, i, at, True) for i in (side, 1 - side)]
 
     def quarter(self, a, at):
         high, low = self.side(at), self.side(at + 1)
@@ -680,24 +673,60 @@
         masks = (low, high, high | low)
         return [lax.ppermute(a, axis, [(d, d ^ mask) for d in range(self.sizes[axis])]) for a, mask in zip(parts, masks)]
 
-    def step(self, a, at, held=BF):
-        mine, others = self.halve(a, at)
-        return (mine.astype(F32) + self.other(others, at).astype(F32)).astype(held)
-
-    def scatter(self, a, order):
-        for at in order[:-1]:
-            a = self.step(a, at)
-        a = self.step(a, order[-1], F32)
-        return a.reshape(a.shape[-2:])
+
+def total(terms, held=BF):
+    return sum([a.astype(F32) for a in terms[1:]], terms[0].astype(F32)).astype(held)
 
 
 def begin(shards, sums, ats):
     halves = [shards.halve(a, at) for a, at in zip(sums, ats)]
-    return [mine for mine, _ in halves], [shards.other(others, at) for (_, others), at in zip(halves, ats)]
-
-
-def add(mine, got, held=BF):
-    return [(a.astype(F32) + b.astype(F32)).astype(held) for a, b in zip(mine, got)]
+    return [[mine, shards.other(others, at)] for (mine, others), at in zip(halves, ats)]
+
+
+def unpack_kernel(*refs, counts):
+    na, nb, nc = counts
+    ins, outs = refs[: na + nb + nc], refs[na + nb + nc :]
+    add = lambda terms, rows, cols=slice(None): sum([t[rows, cols].astype(F32) for t in terms[1:]], terms[0][rows, cols].astype(F32))
+    a, b, c = ins[:na], ins[na : na + nb], ins[na + nb :]
+    out_one, qkv_two, out_two, up, down, qkv_one, vectors = outs
+    r = out_one.shape[0]
+    at = 0
+    for ref in (out_one, qkv_two, out_two, up):
+        for j in range(ref.shape[1] // D):
+            terms, row = (a, at) if at < SHARE else (b, at - SHARE)
+            ref[:, j * D : (j + 1) * D] = add(terms, slice(row, row + r))
+            at += r
+    down[...] = add(b, slice(at - SHARE, at - SHARE + down.shape[0]))
+    qkv_one[...] = add(c, slice(None), slice(0, QKV))
+    vectors[...] = add(c, slice(None), slice(QKV, QKV + 128)).T
+
+
+def unpack(two, dfirst, r):
+    sums = [[a.reshape(a.shape[-2:]) for a in terms] for terms in (*two, dfirst)]
+    if r % ROWS_P:
+        pack = jnp.concatenate([total(sums[0], F32), total(sums[1], F32)])
+        piece = lambda a, b: jnp.concatenate([pack[j * r : (j + 1) * r] for j in range(a, b)], axis=1)
+        dfirst = total(sums[2], F32)
+        return piece(0, 1), piece(1, 4), piece(4, 5), piece(5, 9), pack[9 * r :], dfirst[:, :QKV], dfirst[:, QKV:].T
+    shapes = [(r, D), (r, QKV), (r, D), (r, FF), (4 * r, D), (r, QKV), (128, r)]
+    return pl.pallas_call(
+        lambda *refs: unpack_kernel(*refs, counts=[len(terms) for terms in sums]),
+        out_shape=[jax.ShapeDtypeStruct(q, F32) for q in shapes],
+        name="unpack",
+    )(*[a for terms in sums for a in terms])
+
+
+def split_sum(shards, mine, others, core):
+    if shards.count == D // ROWS_P:
+        terms = [mine, shards.other(others, shards.near)]
+        return [a.reshape((2,) * (len(shards.bits) - 1) + (1,) + a.shape[1:]) for a in terms]
+    both = jnp.where(core == 0, jnp.stack((mine, others), 1), jnp.stack((others, mine), 1))
+    both = both.reshape((D // ROWS_P,) + mine.shape[1:])
+    if mine.shape[1] == ROWS_P:
+        both = both.reshape(shards.count, -1, both.shape[2])
+    else:
+        both = repack(both, shards.count)
+    return begin(shards, [both.reshape((2,) * len(shards.bits) + both.shape[1:])], [shards.near])[0]
 
 
 def together(a, b):
@@ -730,7 +759,7 @@
     first, pack = pack_shards(vectors, qkv_one, (out_one, qkv_two, out_two, up), down)
     pack = repack(lax.all_gather(pack, ("rows", "feat"), axis=0), D // ROWS_P)
     first = shards.gather(first, shards.feat_bits[:1])
-    got, xs_at = exchange(inputs[0], me, n, first)
+    got, xs_at = exchange(together(inputs, first)[0][0], me, n)
     first = shards.gather(first, shards.feat_bits[1:] + shards.rows_bits)
     got[0], first = together(got[0], first)
     xs_at = xs_at()
@@ -740,7 +769,7 @@
     g1, b1, g2, b2, g3, b3 = [gains[j : j + 1] for j in range(6)]
 
     xs = [a for a, _ in xs_at]
-    x_rows = jnp.stack([jnp.asarray(at, jnp.int32) for _, at in xs_at]) // RC
+    x_rows = jnp.stack([jnp.asarray(at, jnp.int32) // RC for _, at in xs_at] + [core[0]])
     order = me ^ jnp.arange(n, dtype=jnp.int32)
     valid = jnp.take(feature_mask[0].reshape(n, feats), order, axis=0).reshape(tot) > 0
     wide = -(-2 * tot // 128) * 128
@@ -749,93 +778,72 @@
     bias_one = jnp.where(same & jnp.pad(jnp.tile(valid, 2), (0, wide - 2 * tot))[None, :], 0.0, MASKED).astype(F32)
     bias_two = jnp.where(row_allowed(segments[0], context[0]), 0.0, MASKED).astype(F32)
 
-    cut = feats // 2
+    cut = feats // 3 // FB * FB
     cuts = ((0, cut), (cut, feats))
     half = part // 2
     res = feature_forward(x_rows, xs, g1, b1, first, bias_one, cuts, part)
     qkv, p = res[2 * n :]
     h_a, h_b = swap(res[:n], n), swap(res[n : 2 * n], n)
     gains_two = (g2, b2, g3, b3)
-    res = middle(me_arr, core, inputs, h_a, cotangent, bias_two, pack, *gains_two, 0, ((0, part),), [], False)
+    res = middle(me_arr, core, inputs, h_a, cotangent, bias_two, pack, *gains_two, 0, ((0, part),), [])
     output, gaf, carried = res[0], res[1], res[2 + n :]
     g_a = swap(res[2 : 2 + n], n)
     spans = ((0, half), (half, part))
-    res = middle(me_arr, core, inputs, h_b, cotangent, bias_two, pack, *gains_two, cut, spans, [*carried, output, gaf], True)
+    res = middle(me_arr, core, inputs, h_b, cotangent, bias_two, pack, *gains_two, cut, spans, [*carried, output, gaf])
     g_a, res = together(g_a, res)
     output, gaf = res[:2]
     g_b, g_c = swap(res[2 : 2 + n], n), swap(res[2 + n : 2 + 2 * n], n)
     mine, others, *vector_grads = res[2 + 2 * n :]
 
     wide_first, tall_first = shards.rows_bits[::-1], shards.rows_bits[-2::-1] + shards.rows_bits[-1:]
-    if shards.count == D // ROWS_P:
-        dpack = (mine.astype(F32) + shards.other(others, shards.near).astype(F32)).astype(BF)
-        dpack = dpack.reshape((2,) * (len(shards.bits) - 1) + (1,) + dpack.shape[1:])
-    else:
-        dpack = jnp.where(core[0] == 0, jnp.stack((mine, others), 1), jnp.stack((others, mine), 1))
-        dpack = shards.step(shards.spread(repack(dpack.reshape(pack.shape), shards.count)), shards.near)
-    g_b, dpack = together(g_b, dpack)
-    share = dpack.shape[-2] // 2 // ROWS_P * ROWS_P
+    ways = [way + shards.feat_bits for way in (wide_first, tall_first)]
+    on = lambda i: [way[i] for way in ways]
+    dpack = total(split_sum(shards, mine, others, core[0]))
+    dpack, g_b = together(dpack, g_b)
+    share = SHARE if shards.count == D // ROWS_P else dpack.shape[-2] // 2
     two = [dpack[..., :share, :], dpack[..., share:, :]]
-    ways = [wide_first + shards.feat_bits, tall_first + shards.feat_bits]
-
-    mine, got = begin(shards, two, [way[0] for way in ways])
+
+    two = begin(shards, two, on(0))
     *d_a, acc, dg1, db1 = feature_backward(
         x_rows, xs, [(0, g_a), (0, g_b)], qkv, p, g1, b1, first, cuts, 0, half, [], []
     )
-    got, d_a, g_c = lax.optimization_barrier((got, d_a, g_c))
-    two = add(mine, got)
-    two, g_c = together(two, g_c)
-
-    mine, got = begin(shards, two, [way[1] for way in ways])
+    two, d_a, g_c = lax.optimization_barrier((two, d_a, g_c))
+    two, g_c = together([total(terms) for terms in two], g_c)
+
+    two = begin(shards, two, on(1))
     d_a = swap(d_a, n)
-    *d_b, dfirst = feature_backward(
+    *d_b, kept, others = feature_backward(
         x_rows, xs, [(0, g_a), (half, g_c)], qkv, p, g1, b1, first, cuts, half, part, [acc, dg1, db1], vector_grads
     )
-    got, d_a, d_b, dfirst = lax.optimization_barrier((got, d_a, d_b, dfirst))
+    two, d_a, d_b, kept, others = lax.optimization_barrier((two, d_a, d_b, kept, others))
+    dfirst = total(split_sum(shards, kept, others, core[0]))
     d_b = swap(d_b, n)
-    dfirst = shards.step(shards.spread(dfirst.reshape(shards.count, -1, QKV + 128)), shards.near)
-    two = add(mine, got)
+    two = [total(terms) for terms in two]
     for i in range(2, len(ways[0]) - 2):
-        two = add(*begin(shards, two, [way[i] for way in ways]))
+        two = [total(terms) for terms in begin(shards, two, on(i))]
     d_a, dfirst = together(d_a, dfirst)
 
-    mine, got = begin(shards, [*two, dfirst], [way[-2] for way in ways] + wide_first[:1])
+    *two, dfirst = begin(shards, [*two, dfirst], on(-2) + wide_first[:1])
     input_grad = final(me_arr, gaf, d_a, 0, None)
-    got, input_grad = together(got, input_grad)
-    *two, dfirst = add(mine, got)
+    two, dfirst, input_grad = lax.optimization_barrier((two, dfirst, input_grad))
+    two = begin(shards, [total(terms) for terms in two], on(-1))
+    dfirst = total(dfirst)
     last = wide_first[1:] + shards.feat_bits
     if len(last) == 3:
-        two, dfirst = together(two, dfirst)
-        mine, got = begin(shards, two, [way[-1] for way in ways])
         kept, others = shards.quarter(dfirst, last[1])
-        others, d_b, got = lax.optimization_barrier((shards.others(others, last[1]), d_b, got))
+        two, others, d_b = lax.optimization_barrier((two, shards.others(others, last[1]), d_b))
         input_grad = final(me_arr, gaf, d_b, half, input_grad)
-        others, input_grad, got = lax.optimization_barrier((others, input_grad, got))
-        dfirst = sum([b.astype(F32) for b in others], kept.astype(F32)).astype(BF)
+        two, others, input_grad = lax.optimization_barrier((two, others, input_grad))
+        dfirst = total([kept] + others)
         last = last[2:]
     else:
         input_grad = final(me_arr, gaf, d_b, half, input_grad)
-        mine, got = begin(shards, two, [way[-1] for way in ways])
-    dpack = jnp.concatenate([a.reshape(a.shape[-2:]) for a in add(mine, got, F32)])
-    dfirst = shards.scatter(dfirst, last)
-    piece = lambda a, b: jnp.concatenate([dpack[j * r : (j + 1) * r] for j in range(a, b)], axis=1)
-    v = [dfirst[:, QKV + j] for j in range(6)]
-    return (
-        output,
-        input_grad,
-        v[0],
-        v[1],
-        dfirst[:, :QKV],
-        piece(0, 1),
-        v[2],
-        v[3],
-        piece(1, 4),
-        piece(4, 5),
-        v[4],
-        v[5],
-        piece(5, 9),
-        dpack[9 * r :],
-    )
+    for at in last[:-1]:
+        dfirst = total(begin(shards, [dfirst], [at])[0])
+    dfirst = begin(shards, [dfirst], last[-1:])[0]
+    d_out_one, d_qkv_two, d_out_two, d_up, d_down, d_qkv_one, vectors = unpack(two, dfirst, r)
+    v = [vectors[j] for j in range(6)]
+    return (output, input_grad, v[0], v[1], d_qkv_one, d_out_one, v[2], v[3], d_qkv_two, d_out_two, v[4], v[5], d_up, d_down)
 
 
 def solution(mesh):

time: 377 us -> 357 us (0.947)
  Pallas kernels: 204 us -> 190 us
  other arithmetic: 16.7 us -> 11.5 us
    pallas_call x2, Pallas kernels: 42.5 us -> 34.8 us  [feature_backward(): pl.pallas_call(lambda *r: feature_backward_kernel(*r, n=n, feats=feats, c...]
    convert_element_type x10, other arithmetic: 10 us -> 5.31 us  [total(): sum([a.astype(F32) for a in terms[1:]], terms[0].astype(F32)).astype(held)]
    pallas_call x2, Pallas kernels: 129 us -> 124 us  [middle(): pl.pallas_call(lambda *r: middle_kernel(*r, n=n, rows=rows, part=part, sp...]
  transfers between devices with their start and end apart: 46 -> 46, of which waited for: 15 -> 18; matrix products, arithmetic and copies ran while one was open for 7% -> 6% of each run, Pallas kernels for 54% -> 52%
where the time goes in v3:
time: 357 us; the launch traced here: 352 us
  Pallas kernels  190 us (53%)
  waiting for transfers between devices  69.9 us (20%)
  starting transfers between devices  43.5 us (12%)
  local copies, waits for them, and re-layouts  21.2 us (6%)
  between operations  15.1 us (4%)
  other arithmetic  11.5 us (3%)
    pallas_call x2, Pallas kernels, middle(): pl.pallas_call(lambda *r: middle_kernel(*r, n=n, rows=rows, part=part, sp...  124 us
    pallas_call x2, Pallas kernels, feature_backward(): pl.pallas_call(lambda *r: feature_backward_kernel(*r, n=n, feats=feats, c...  34.8 us
    ppermute x15, waiting for transfers between devices, other(): lax.ppermute(a, axis, [(d, d ^ bit) for d in range(self.sizes[axis])])  29.7 us
    ppermute x3, waiting for transfers between devices, move(): lax.ppermute(sent, 'feat', [(d, d ^ bit) for d in range(n)])  20.5 us
    pallas_call x1, Pallas kernels, feature_forward(): pl.pallas_call(lambda *r: feature_forward_kernel(*r, n=n, feats=feats, cu...  19 us
    ppermute x15, starting transfers between devices, other(): lax.ppermute(a, axis, [(d, d ^ bit) for d in range(self.sizes[axis])])  18.3 us
    ppermute x21, starting transfers between devices, swap(): lax.ppermute(arrays[k], 'feat', [(d, d ^ k) for d in range(n)])  14 us
    ppermute x21, waiting for transfers between devices, swap(): lax.ppermute(arrays[k], 'feat', [(d, d ^ k) for d in range(n)])  9.81 us
  transfers between devices with their start and end apart: 46, of which 18 were waited for; matrix products, arithmetic and copies ran while one was open for 6% of the time, Pallas kernels for 52%

profile of v3, /device:TPU:0, one launch (start us, length us, event | category | flops | bytes accessed | tf_op | source)
XLA Modules:
  0.0 351.6 jit_solution(12192053212449478256)
XLA Ops:
  8.6 1.7 pack.1
  10.2 2.9 collective-permute-start
  16.7 1.8 collective-permute-start.5
  18.5 2.5 collective-permute-start.3
  21.1 1.6 dynamic-slice_bitcast_fusion
  24.3 2.5 collective-permute-done.3
  26.8 6.3 %collective-permute-done.4 = bf16[1,1,1,2,1,16,1664]{6,5,4,3,2,1,0:T(8,128)(2,1)S(1)} collective-permute-done((bf16[1,1,1,2,1,16,1664]{6,5,4,3,2,1,0:T(8,128)(2,1)S(1)}, bf16[1,1,1,2,1,16,1664]{6,5,4,3,2,1,0:T(8,128)(2,1)S(1)}, u32[]{:S(2)}, u32[]{:S(2)}) %collective-permute-start.4) | collective-permute-done | bytes 106528 | tf_op jit(solution)/shard_map/ppermute | solution.py:654
  33.2 1.6 collective-permute-start.6
  35.0 9.9 %collective-permute-done.6 = bf16[2,2,1,2,1,16,1664]{6,5,4,3,2,1,0:T(8,128)(2,1)S(1)} collective-permute-done((bf16[2,2,1,2,1,16,1664]{6,5,4,3,2,1,0:T(8,128)(2,1)S(1)}, bf16[2,2,1,2,1,16,1664]{6,5,4,3,2,1,0:T(8,128)(2,1)S(1)}, u32[]{:S(2)}, u32[]{:S(2)}) %collective-permute-start.6) | collective-permute-done | bytes 426016 | tf_op jit(solution)/shard_map/ppermute | solution.py:630
  45.1 20.4 %collective-permute-done.2.r_3_ = bf16[12,128,512]{2,1,0:T(8,128)(2,1)S(1)} collective-permute-done((bf16[12,128,512]{2,1,0:T(8,128)(2,1)S(1)}, bf16[12,128,512]{2,1,0:T(8,128)(2,1)S(1)}, u32[]{:S(2)}, u32[]{:S(2)}) %collective-permute-start.2) | collective-permute-done | bytes 1572896 | tf_op jit(solution)/shard_map/ppermute | solution.py:598
  73.9 19.0 %feature_forward.1 = (bf16[4,64,512]{2,1,0:T(8,128)(2,1)}, bf16[4,64,512]{2,1,0:T(8,128)(2,1)}, bf16[4,64,512]{2,1,0:T(8,128)(2,1)}, bf16[4,64,512]{2,1,0:T(8,12...) custom-call(s32[5]{0:T(128)} %stack.13.r_0_, ...), custom_call_target="tpu_custom_call" | custom-call | flops 99999997952 | bytes 1000000 | tf_op jit(solution)/shard_map/feature_forward/pallas_call | solution.py:130
  100.5 2.1 collective-permute-done.10.r_5_
  102.6 4.1 %collective-permute-done.11.r_6_ = bf16[4,64,512]{2,1,0:T(8,128)(2,1)S(1)} collective-permute-done((bf16[4,64,512]{2,1,0:T(8,128)(2,1)}, bf16[4,64,512]{2,1,0:T(8,128)(2,1)S(1)}, u32[]{:S(2)}, u32[]{:S(2)}) %collective-permute-start.11) | collective-permute-done | bytes 262176 | tf_op jit(solution)/shard_map/ppermute | solution.py:589
  107.4 40.2 %middle.2 = (bf16[1,12,256,512]{3,2,1,0:T(8,128)(2,1)}, bf16[12,256,512]{2,1,0:T(8,128)(2,1)}, bf16[4,64,512]{2,1,0:T(8,128)(2,1)}, bf16[4,64,512]{2,1,0:T(8,128...) custom-call(s32[1]{0:T(128)} %bitcast.r_0_, ...), custom_call_target="tpu_custom_call" | custom-call | flops 99999997952 | bytes 1000000 | tf_op jit(solution)/shard_map/middle/pallas_call | solution.py:478
  151.4 83.9 %middle.3 = (bf16[1,12,256,512]{3,2,1,0:T(8,128)(2,1)}, bf16[12,256,512]{2,1,0:T(8,128)(2,1)}, bf16[8,32,512]{2,1,0:T(8,128)(2,1)}, bf16[8,32,512]{2,1,0:T(8,128...) custom-call(s32[1]{0:T(128)} %bitcast.r_0_, ...), custom_call_target="tpu_custom_call", output_to_operand_aliasing={{0}: (20, {}), {1}: (21, {})} | custom-call | flops 99999997952 | bytes 1000000 | tf_op jit(solution)/shard_map/middle/pallas_call | solution.py:478
  239.1 3.7 %collective-permute-done.18 = bf16[16,208,512]{2,1,0:T(8,128)(2,1)S(1)} collective-permute-done((bf16[16,208,512]{2,1,0:T(8,128)(2,1)}, bf16[16,208,512]{2,1,0:T(8,128)(2,1)S(1)}, u32[]{:S(2)}, u32[]{:S(2)}) %collective-permute-start.18) | collective-permute-done | bytes 3407904 | tf_op jit(solution)/shard_map/ppermute | solution.py:630
  243.6 3.0 add_convert_fusion
  247.7 3.5 collective-permute-done.21.r_12_
  252.0 1.6 collective-permute-start.22
  256.1 16.9 %feature_backward.2 = (bf16[12,32,512]{2,1,0:T(8,128)(2,1)}, bf16[12,32,512]{2,1,0:T(8,128)(2,1)}, bf16[12,32,512]{2,1,0:T(8,128)(2,1)}, bf16[12,32,512]{2,1,0:T...) custom-call(s32[5]{0:T(128)} %stack.13.r_0_, bf16[12,256,512]{2,1,0:T(8,128)(2,1)} %bitcast.57, ...), custom_call_target="tpu_custom_call" | custom-call | flops 99999997952 | bytes 1000000 | tf_op jit(solution)/shard_map/feature_backward/pallas_call | solution.py:247
  273.1 1.6 collective-permute-done.23
  276.7 1.6 collective-permute-start.27
  278.3 1.8 collective-permute-start.28
  281.9 17.8 %feature_backward.3 = (bf16[12,32,512]{2,1,0:T(8,128)(2,1)}, bf16[12,32,512]{2,1,0:T(8,128)(2,1)}, bf16[12,32,512]{2,1,0:T(8,128)(2,1)}, bf16[12,32,512]{2,1,0:T...) custom-call(s32[5]{0:T(128)} %stack.13.r_0_, bf16[12,256,512]{2,1,0:T(8,128)(2,1)} %bitcast.58, ...), custom_call_target="tpu_custom_call" | custom-call | flops 99999997952 | bytes 1000000 | tf_op jit(solution)/shard_map/feature_backward/pallas_call | solution.py:247
  305.7 4.4 %final.2 = f32[1,12,4,2,32,512]{5,4,3,2,1,0:T(8,128)} custom-call(s32[1]{0:T(128)} %bitcast.r_0_, bf16[12,4,2,32,512]{4,3,2,1,0:T(8,128)(2,1)} %bitcast.77, bf16[12,32,512]{2,1,0:T(8,128)(2,1)} %get-tuple-element.275.r_2_, bf16[12,32,512]{2,1,0:T(8,128)(2,1)} %copy-done.12, bf16[12,32,512]{2,1,0:T(8,128)(2,1)} %collective-permute-done.30.r_4_, ...), custom_call_target="tpu_custom_call" | custom-call | flops 99999997952 | bytes 1000000 | tf_op jit(solution)/shard_map/final/pallas_call | solution.py:535
  311.0 3.6 %collective-permute-done.32 = bf16[1,1,1,2,1,112,512]{6,5,4,3,2,1,0:T(8,128)(2,1)S(1)} collective-permute-done((bf16[1,1,1,2,1,112,512]{6,5,4,3,2,1,0:T(8,128)(2,1)S(1)}, bf16[1,1,1,2,1,112,512]{6,5,4,3,2,1,0:T(8,128)(2,1)S(1)}, u32[]{:S(2)}, u32[]{:S(2)}) %collective-permute-start.32) | collective-permute-done | bytes 229408 | tf_op jit(solution)/shard_map/ppermute | solution.py:630
  314.6 3.8 %collective-permute-done.35 = bf16[2,2,1,2,1,16,1664]{6,5,4,3,2,1,0:T(8,128)(2,1)S(1)} collective-permute-done((bf16[2,2,1,2,1,16,1664]{6,5,4,3,2,1,0:T(8,128)(2,1)S(1)}, bf16[2,2,1,2,1,16,1664]{6,5,4,3,2,1,0:T(8,128)(2,1)S(1)}, u32[]{:S(2)}, u32[]{:S(2)}) %collective-permute-start.35) | collective-permute-done | bytes 426016 | tf_op jit(solution)/shard_map/ppermute | solution.py:630
  320.7 2.6 collective-permute-start.39
  326.6 3.4 collective-permute-done.37
  331.1 4.4 %final.3 = f32[1,12,4,2,32,512]{5,4,3,2,1,0:T(8,128)} custom-call(s32[1]{0:T(128)} %bitcast.r_0_, bf16[12,4,2,32,512]{4,3,2,1,0:T(8,128)(2,1)} %bitcast.78, bf16[12,32,512]{2,1,0:T(8,128)(2,1)} %get-tuple-element.296.r_2_, bf16[12,32,512]{2,1,0:T(8,128)(2,1)} %collective-permute-done.41.r_3_, ...), custom_call_target="tpu_custom_call", output_to_operand_aliasing={{}: (6, {})} | custom-call | flops 99999997952 | bytes 1000000 | tf_op jit(solution)/shard_map/final/pallas_call | solution.py:535
  337.2 3.2 collective-permute-done.44
  341.0 1.9 unpack.1
  (195 shorter events, 57.3 us)
Async XLA Ops:
  7.2 99.5 %all-gather.3.cloned.1.call-start = ((), (), s32[]{:S(2)}) async-start(), calls=%async_computation | async-start | bytes 7028736 | tf_op jit(solution)/shard_map/all_gather | solution.py:760
  21.0 12.1 %collective-permute-start.4 = (bf16[1,1,1,2,1,16,1664]{6,5,4,3,2,1,0:T(8,128)(2,1)S(1)}, bf16[1,1,1,2,1,16,1664]{6,5,4,3,2,1,0:T(8,128)(2,1)S(1)}, u32[]{:S(2)}, u32[]{:S(2)}) collective-permute-start(bf16[1,1,1,2,1,16,1664]{6,5,4,3,2,1,0:T(8,128)(2,1)S(1)} %pad_maximum_fusion.5), channel_id=1, source_target_pairs={{0,16},{4,20},{8,24},{12,28},{16,0},{20,4},{24,8},{28,12},{1,17},{... | collective-permute-start | bytes 319496 | tf_op jit(solution)/shard_map/ppermute | solution.py:654
  22.7 42.7 %collective-permute-start.2 = (bf16[12,128,512]{2,1,0:T(8,128)(2,1)S(1)}, bf16[12,128,512]{2,1,0:T(8,128)(2,1)S(1)}, u32[]{:S(2)}, u32[]{:S(2)}) collective-permute-start(bf16[12,128,512]{2,1,0:T(8,128)(2,1)S(1)} %dynamic-slice_bitcast_fusion), channel_id=1, source_target_pairs={{0,2},{1,3},{2,0},{3,1},{4,6},{5,7},{6,4},{7,5},{8,10},{9,11},{10,... | collective-permute-start | bytes 4718600 | tf_op jit(solution)/shard_map/ppermute | solution.py:598
  33.2 11.7 %collective-permute-start.6 = (bf16[2,2,1,2,1,16,1664]{6,5,4,3,2,1,0:T(8,128)(2,1)S(1)}, bf16[2,2,1,2,1,16,1664]{6,5,4,3,2,1,0:T(8,128)(2,1)S(1)}, u32[]{:S(2)}, u32[]{:S(2)}) collective-permute-start(bf16[2,2,1,2,1,16,1664]{6,5,4,3,2,1,0:T(8,128)(2,1)S(1)} %pad_maximum_fusion.2), channel_id=1, source_target_pairs={{0,4},{4,0},{8,12},{12,8},{16,20},{20,16},{24,28},{28,24},{1,5},{5... | collective-permute-start | bytes 1277960 | tf_op jit(solution)/shard_map/ppermute | solution.py:630
  94.0 12.7 %collective-permute-start.11 = (bf16[4,64,512]{2,1,0:T(8,128)(2,1)}, bf16[4,64,512]{2,1,0:T(8,128)(2,1)S(1)}, u32[]{:S(2)}, u32[]{:S(2)}) collective-permute-start(bf16[4,64,512]{2,1,0:T(8,128)(2,1)} %get-tuple-element.172), channel_id=1, source_target_pairs={{0,3},{1,2},{2,1},{3,0},{4,7},{5,6},{6,5},{7,4},{8,11},{9,10},{10,... | collective-permute-start | bytes 786440 | tf_op jit(solution)/shard_map/ppermute | solution.py:589
  98.6 51.3 %collective-permute-start.15 = (bf16[8,64,512]{2,1,0:T(8,128)(2,1)}, bf16[8,64,512]{2,1,0:T(8,128)(2,1)S(1)}, u32[]{:S(2)}, u32[]{:S(2)}) collective-permute-start(bf16[8,64,512]{2,1,0:T(8,128)(2,1)} %get-tuple-element.179), channel_id=1, source_target_pairs={{0,1},{1,0},{2,3},{3,2},{4,5},{5,4},{6,7},{7,6},{8,9},{9,8},{10,11... | collective-permute-start | bytes 1572872 | tf_op jit(solution)/shard_map/ppermute | solution.py:589
  99.2 51.3 %collective-permute-start.16 = (bf16[8,64,512]{2,1,0:T(8,128)(2,1)}, bf16[8,64,512]{2,1,0:T(8,128)(2,1)S(1)}, u32[]{:S(2)}, u32[]{:S(2)}) collective-permute-start(bf16[8,64,512]{2,1,0:T(8,128)(2,1)} %get-tuple-element.180), channel_id=1, source_target_pairs={{0,2},{1,3},{2,0},{3,1},{4,6},{5,7},{6,4},{7,5},{8,10},{9,11},{10,... | collective-permute-start | bytes 1572872 | tf_op jit(solution)/shard_map/ppermute | solution.py:589
  100.0 50.5 %collective-permute-start.17 = (bf16[8,64,512]{2,1,0:T(8,128)(2,1)}, bf16[8,64,512]{2,1,0:T(8,128)(2,1)S(1)}, u32[]{:S(2)}, u32[]{:S(2)}) collective-permute-start(bf16[8,64,512]{2,1,0:T(8,128)(2,1)} %get-tuple-element.181), channel_id=1, source_target_pairs={{0,3},{1,2},{2,1},{3,0},{4,7},{5,6},{6,5},{7,4},{8,11},{9,10},{10,... | collective-permute-start | bytes 1572872 | tf_op jit(solution)/shard_map/ppermute | solution.py:589
  147.7 87.7 %collective-permute-start.12 = (bf16[4,64,512]{2,1,0:T(8,128)(2,1)}, bf16[4,64,512]{2,1,0:T(8,128)(2,1)S(1)}, u32[]{:S(2)}, u32[]{:S(2)}) collective-permute-start(bf16[4,64,512]{2,1,0:T(8,128)(2,1)} %get-tuple-element.175), channel_id=1, source_target_pairs={{0,1},{1,0},{2,3},{3,2},{4,5},{5,4},{6,7},{7,6},{8,9},{9,8},{10,11... | collective-permute-start | bytes 786440 | tf_op jit(solution)/shard_map/ppermute | solution.py:589
  149.0 86.3 %collective-permute-start.13 = (bf16[4,64,512]{2,1,0:T(8,128)(2,1)}, bf16[4,64,512]{2,1,0:T(8,128)(2,1)S(1)}, u32[]{:S(2)}, u32[]{:S(2)}) collective-permute-start(bf16[4,64,512]{2,1,0:T(8,128)(2,1)} %get-tuple-element.176), channel_id=1, source_target_pairs={{0,2},{1,3},{2,0},{3,1},{4,6},{5,7},{6,4},{7,5},{8,10},{9,11},{10,... | collective-permute-start | bytes 786440 | tf_op jit(solution)/shard_map/ppermute | solution.py:589
  149.8 85.6 %collective-permute-start.14 = (bf16[4,64,512]{2,1,0:T(8,128)(2,1)}, bf16[4,64,512]{2,1,0:T(8,128)(2,1)S(1)}, u32[]{:S(2)}, u32[]{:S(2)}) collective-permute-start(bf16[4,64,512]{2,1,0:T(8,128)(2,1)} %get-tuple-element.177), channel_id=1, source_target_pairs={{0,3},{1,2},{2,1},{3,0},{4,7},{5,6},{6,5},{7,4},{8,11},{9,10},{10,... | collective-permute-start | bytes 786440 | tf_op jit(solution)/shard_map/ppermute | solution.py:589
  237.0 9.7 %collective-permute-start.19 = (bf16[8,32,512]{2,1,0:T(8,128)(2,1)}, bf16[8,32,512]{2,1,0:T(8,128)(2,1)S(1)}, u32[]{:S(2)}, u32[]{:S(2)}) collective-permute-start(bf16[8,32,512]{2,1,0:T(8,128)(2,1)} %get-tuple-element.210), channel_id=1, source_target_pairs={{0,1},{1,0},{2,3},{3,2},{4,5},{5,4},{6,7},{7,6},{8,9},{9,8},{10,11... | collective-permute-start | bytes 786440 | tf_op jit(solution)/shard_map/ppermute | solution.py:589
  237.0 10.7 %collective-permute-start.20 = (bf16[8,32,512]{2,1,0:T(8,128)(2,1)}, bf16[8,32,512]{2,1,0:T(8,128)(2,1)S(1)}, u32[]{:S(2)}, u32[]{:S(2)}) collective-permute-start(bf16[8,32,512]{2,1,0:T(8,128)(2,1)} %get-tuple-element.211), channel_id=1, source_target_pairs={{0,2},{1,3},{2,0},{3,1},{4,6},{5,7},{6,4},{7,5},{8,10},{9,11},{10,... | collective-permute-start | bytes 786440 | tf_op jit(solution)/shard_map/ppermute | solution.py:589
  237.8 13.4 %collective-permute-start.21 = (bf16[8,32,512]{2,1,0:T(8,128)(2,1)}, bf16[8,32,512]{2,1,0:T(8,128)(2,1)S(1)}, u32[]{:S(2)}, u32[]{:S(2)}) collective-permute-start(bf16[8,32,512]{2,1,0:T(8,128)(2,1)} %get-tuple-element.212), channel_id=1, source_target_pairs={{0,3},{1,2},{2,1},{3,0},{4,7},{5,6},{6,5},{7,4},{8,11},{9,10},{10,... | collective-permute-start | bytes 786440 | tf_op jit(solution)/shard_map/ppermute | solution.py:589
  238.8 34.2 %collective-permute-start.24 = (bf16[8,32,512]{2,1,0:T(8,128)(2,1)}, bf16[8,32,512]{2,1,0:T(8,128)(2,1)}, u32[]{:S(2)}, u32[]{:S(2)}) collective-permute-start(bf16[8,32,512]{2,1,0:T(8,128)(2,1)} %get-tuple-element.229), channel_id=1, source_target_pairs={{0,1},{1,0},{2,3},{3,2},{4,5},{5,4},{6,7},{7,6},{8,9},{9,8},{10,11... | collective-permute-start | bytes 786440 | tf_op jit(solution)/shard_map/ppermute | solution.py:589
  242.8 30.2 %collective-permute-start.25 = (bf16[8,32,512]{2,1,0:T(8,128)(2,1)}, bf16[8,32,512]{2,1,0:T(8,128)(2,1)}, u32[]{:S(2)}, u32[]{:S(2)}) collective-permute-start(bf16[8,32,512]{2,1,0:T(8,128)(2,1)} %get-tuple-element.230), channel_id=1, source_target_pairs={{0,2},{1,3},{2,0},{3,1},{4,6},{5,7},{6,4},{7,5},{8,10},{9,11},{10,... | collective-permute-start | bytes 786440 | tf_op jit(solution)/shard_map/ppermute | solution.py:589
  246.7 26.4 %collective-permute-start.26 = (bf16[8,32,512]{2,1,0:T(8,128)(2,1)}, bf16[8,32,512]{2,1,0:T(8,128)(2,1)S(1)}, u32[]{:S(2)}, u32[]{:S(2)}) collective-permute-start(bf16[8,32,512]{2,1,0:T(8,128)(2,1)} %get-tuple-element.231), channel_id=1, source_target_pairs={{0,3},{1,2},{2,1},{3,0},{4,7},{5,6},{6,5},{7,4},{8,11},{9,10},{10,... | collective-permute-start | bytes 786440 | tf_op jit(solution)/shard_map/ppermute | solution.py:589
  252.0 22.9 %collective-permute-start.22 = (bf16[2,2,1,2,1,112,512]{6,5,4,3,2,1,0:T(8,128)(2,1)S(1)}, bf16[2,2,1,2,1,112,512]{6,5,4,3,2,1,0:T(8,128)(2,1)S(1)}, u32[]{:S(2)}, u32[]{:S(2)}) collective-permute-start(bf16[2,2,1,2,1,112,512]{6,5,4,3,2,1,0:T(8,128)(2,1)S(1)} %get-tuple-element.318), channel_id=1, source_target_pairs={{0,4},{4,0},{8,12},{12,8},{16,20},{20,16},{24,28},{28,24},{1,5},{5... | collective-permute-start | bytes 2752520 | tf_op jit(solution)/shard_map/ppermute | solution.py:630
  254.6 20.1 %collective-permute-start.23 = (bf16[2,1,2,2,1,96,512]{6,5,4,3,2,1,0:T(8,128)(2,1)}, bf16[2,1,2,2,1,96,512]{6,5,4,3,2,1,0:T(8,128)(2,1)}, u32[]{:S(2)}, u32[]{:S(2)}) collective-permute-start(bf16[2,1,2,2,1,96,512]{6,5,4,3,2,1,0:T(8,128)(2,1)} %get-tuple-element.322), channel_id=1, source_target_pairs={{0,8},{4,12},{8,0},{12,4},{16,24},{20,28},{24,16},{28,20},{1,9},{5... | collective-permute-start | bytes 2359304 | tf_op jit(solution)/shard_map/ppermute | solution.py:630
  276.7 23.3 %collective-permute-start.27 = (bf16[2,1,1,2,1,112,512]{6,5,4,3,2,1,0:T(8,128)(2,1)S(1)}, bf16[2,1,1,2,1,112,512]{6,5,4,3,2,1,0:T(8,128)(2,1)S(1)}, u32[]{:S(2)}, u32[]{:S(2)}) collective-permute-start(bf16[2,1,1,2,1,112,512]{6,5,4,3,2,1,0:T(8,128)(2,1)S(1)} %get-tuple-element.324), channel_id=1, source_target_pairs={{0,8},{4,12},{8,0},{12,4},{16,24},{20,28},{24,16},{28,20},{1,9},{5... | collective-permute-start | bytes 1376264 | tf_op jit(solution)/shard_map/ppermute | solution.py:630
  278.3 21.5 %collective-permute-start.28 = (bf16[1,1,2,2,1,96,512]{6,5,4,3,2,1,0:T(8,128)(2,1)S(1)}, bf16[1,1,2,2,1,96,512]{6,5,4,3,2,1,0:T(8,128)(2,1)S(1)}, u32[]{:S(2)}, u32[]{:S(2)}) collective-permute-start(bf16[1,1,2,2,1,96,512]{6,5,4,3,2,1,0:T(8,128)(2,1)S(1)} %get-tuple-element.330), channel_id=1, source_target_pairs={{0,16},{4,20},{8,24},{12,28},{16,0},{20,4},{24,8},{28,12},{1,17},{... | collective-permute-start | bytes 1179656 | tf_op jit(solution)/shard_map/ppermute | solution.py:630
  280.1 19.7 %collective-permute-start.29 = (bf16[12,32,512]{2,1,0:T(8,128)(2,1)}, bf16[12,32,512]{2,1,0:T(8,128)(2,1)S(1)}, u32[]{:S(2)}, u32[]{:S(2)}) collective-permute-start(bf16[12,32,512]{2,1,0:T(8,128)(2,1)} %get-tuple-element.243), channel_id=1, source_target_pairs={{0,1},{1,0},{2,3},{3,2},{4,5},{5,4},{6,7},{7,6},{8,9},{9,8},{10,11... | collective-permute-start | bytes 1179656 | tf_op jit(solution)/shard_map/ppermute | solution.py:589
  280.1 19.8 %collective-permute-start.30 = (bf16[12,32,512]{2,1,0:T(8,128)(2,1)}, bf16[12,32,512]{2,1,0:T(8,128)(2,1)}, u32[]{:S(2)}, u32[]{:S(2)}) collective-permute-start(bf16[12,32,512]{2,1,0:T(8,128)(2,1)} %get-tuple-element.244), channel_id=1, source_target_pairs={{0,2},{1,3},{2,0},{3,1},{4,6},{5,7},{6,4},{7,5},{8,10},{9,11},{10,... | collective-permute-start | bytes 1179656 | tf_op jit(solution)/shard_map/ppermute | solution.py:589
  281.1 18.9 %collective-permute-start.31 = (bf16[12,32,512]{2,1,0:T(8,128)(2,1)}, bf16[12,32,512]{2,1,0:T(8,128)(2,1)}, u32[]{:S(2)}, u32[]{:S(2)}) collective-permute-start(bf16[12,32,512]{2,1,0:T(8,128)(2,1)} %get-tuple-element.245), channel_id=1, source_target_pairs={{0,3},{1,2},{2,1},{3,0},{4,7},{5,6},{6,5},{7,4},{8,11},{9,10},{10,... | collective-permute-start | bytes 1179656 | tf_op jit(solution)/shard_map/ppermute | solution.py:589
  301.1 13.6 %collective-permute-start.32 = (bf16[1,1,1,2,1,112,512]{6,5,4,3,2,1,0:T(8,128)(2,1)S(1)}, bf16[1,1,1,2,1,112,512]{6,5,4,3,2,1,0:T(8,128)(2,1)S(1)}, u32[]{:S(2)}, u32[]{:S(2)}) collective-permute-start(bf16[1,1,1,2,1,112,512]{6,5,4,3,2,1,0:T(8,128)(2,1)S(1)} %get-tuple-element.332), channel_id=1, source_target_pairs={{0,16},{4,20},{8,24},{12,28},{16,0},{20,4},{24,8},{28,12},{1,17},{... | collective-permute-start | bytes 688136 | tf_op jit(solution)/shard_map/ppermute | solution.py:630
  304.0 16.7 %collective-permute-start.41 = (bf16[12,32,512]{2,1,0:T(8,128)(2,1)}, bf16[12,32,512]{2,1,0:T(8,128)(2,1)}, u32[]{:S(2)}, u32[]{:S(2)}) collective-permute-start(bf16[12,32,512]{2,1,0:T(8,128)(2,1)} %get-tuple-element.286), channel_id=1, source_target_pairs={{0,1},{1,0},{2,3},{3,2},{4,5},{5,4},{6,7},{7,6},{8,9},{9,8},{10,11... | collective-permute-start | bytes 1179656 | tf_op jit(solution)/shard_map/ppermute | solution.py:589
  304.0 19.3 %collective-permute-start.42 = (bf16[12,32,512]{2,1,0:T(8,128)(2,1)}, bf16[12,32,512]{2,1,0:T(8,128)(2,1)}, u32[]{:S(2)}, u32[]{:S(2)}) collective-permute-start(bf16[12,32,512]{2,1,0:T(8,128)(2,1)} %get-tuple-element.287), channel_id=1, source_target_pairs={{0,2},{1,3},{2,0},{3,1},{4,6},{5,7},{6,4},{7,5},{8,10},{9,11},{10,... | collective-permute-start | bytes 1179656 | tf_op jit(solution)/shard_map/ppermute | solution.py:589
  305.2 13.2 %collective-permute-start.35 = (bf16[2,2,1,2,1,16,1664]{6,5,4,3,2,1,0:T(8,128)(2,1)S(1)}, bf16[2,2,1,2,1,16,1664]{6,5,4,3,2,1,0:T(8,128)(2,1)S(1)}, u32[]{:S(2)}, u32[]{:S(2)}) collective-permute-start(bf16[2,2,1,2,1,16,1664]{6,5,4,3,2,1,0:T(8,128)(2,1)S(1)} %get-tuple-element.326), channel_id=1, source_target_pairs={{0,4},{4,0},{8,12},{12,8},{16,20},{20,16},{24,28},{28,24},{1,5},{5... | collective-permute-start | bytes 1277960 | tf_op jit(solution)/shard_map/ppermute | solution.py:630
  310.3 15.0 %collective-permute-start.43 = (bf16[12,32,512]{2,1,0:T(8,128)(2,1)S(1)}, bf16[12,32,512]{2,1,0:T(8,128)(2,1)S(1)}, u32[]{:S(2)}, u32[]{:S(2)}) collective-permute-start(bf16[12,32,512]{2,1,0:T(8,128)(2,1)S(1)} %copy-done.11), channel_id=1, source_target_pairs={{0,3},{1,2},{2,1},{3,0},{4,7},{5,6},{6,5},{7,4},{8,11},{9,10},{10,... | collective-permute-start | bytes 1179656 | tf_op jit(solution)/shard_map/ppermute | solution.py:589
  319.1 11.9 %collective-permute-start.36 = (bf16[1,1,1,1,1,112,512]{6,5,4,3,2,1,0:T(8,128)(2,1)S(1)}, bf16[1,1,1,1,1,112,512]{6,5,4,3,2,1,0:T(8,128)(2,1)S(1)}, u32[]{:S(2)}, u32[]{:S(2)}) collective-permute-start(bf16[1,1,1,1,1,112,512]{6,5,4,3,2,1,0:T(8,128)(2,1)S(1)} %get-tuple-element.341), channel_id=1, source_target_pairs={{0,2},{1,3},{2,0},{3,1},{4,6},{5,7},{6,4},{7,5},{8,10},{9,11},{10,... | collective-permute-start | bytes 344072 | tf_op jit(solution)/shard_map/ppermute | solution.py:630
  320.1 9.9 %collective-permute-start.38 = (bf16[1,1,1,2,1,16,1664]{6,5,4,3,2,1,0:T(8,128)(2,1)S(1)}, bf16[1,1,1,2,1,16,1664]{6,5,4,3,2,1,0:T(8,128)(2,1)S(1)}, u32[]{:S(2)}, u32[]{:S(2)}) collective-permute-start(bf16[1,1,1,2,1,16,1664]{6,5,4,3,2,1,0:T(8,128)(2,1)S(1)} %get-tuple-element.336), channel_id=1, source_target_pairs={{0,8},{4,12},{8,0},{12,4},{16,24},{20,28},{24,16},{28,20},{1,9},{5... | collective-permute-start | bytes 319496 | tf_op jit(solution)/shard_map/ppermute | solution.py:674
  320.7 10.3 %collective-permute-start.39 = (bf16[1,1,1,2,1,16,1664]{6,5,4,3,2,1,0:T(8,128)(2,1)S(1)}, bf16[1,1,1,2,1,16,1664]{6,5,4,3,2,1,0:T(8,128)(2,1)S(1)}, u32[]{:S(2)}, u32[]{:S(2)}) collective-permute-start(bf16[1,1,1,2,1,16,1664]{6,5,4,3,2,1,0:T(8,128)(2,1)S(1)} %get-tuple-element.335), channel_id=1, source_target_pairs={{0,16},{4,20},{8,24},{12,28},{16,0},{20,4},{24,8},{28,12},{1,17},{... | collective-permute-start | bytes 319496 | tf_op jit(solution)/shard_map/ppermute | solution.py:674
  (38 other events, 210.4 us)
Sparse Core Ops, SparseCore 0:
  13.3 79.6 all-gather.2

commit v4 on v3

--- a/solution.py
+++ b/solution.py
@@ -22,7 +22,7 @@
 VMEM = 60 * 1024 * 1024
 
 GRP2 = 8
-GRP = 4
+GRP = 8
 SHARE = 112
 ROWS_P = 16
 COST = pl.CostEstimate(flops=10**11, bytes_accessed=10**6, transcendentals=0)
@@ -358,7 +358,7 @@
     after_feat = x + mm(h1, wfo[...])
     xhat2, rstd2 = norm(after_feat)
     low2 = (xhat2 * g2[...] + b2[...]).astype(BF)
-    need(1, 2, 3, 4)
+    need(*((1, 2, 3, 4) if first else (1,)))
     qkv_s[...] = mm(low2, wrq[...]).astype(BF)
     mask = bias[...]
     jobs = [(f, h) for f in range(FB) for h in range(HEADS)]
@@ -372,6 +372,8 @@
             p_s[f * HEADS + h] = p
             heads_s[at(f, h, 0)] = mm(p, qkv_s[at(f, h, 2)]).astype(BF)
     heads = heads_s[...]
+    if not first:
+        need(2, 3, 4)
     after_row = after_feat + mm(heads, wro[...])
     xhat3, rstd3 = norm(after_row)
     low3 = (xhat3 * g3[...] + b3[...]).astype(BF)

time: 357 us -> 356 us (level)
  no operation moved by 1% of the time
where the time goes in v4:
time: 356 us; the launch traced here: 350 us
  Pallas kernels  188 us (53%)
  waiting for transfers between devices  70.6 us (20%)
  starting transfers between devices  43.5 us (12%)
  local copies, waits for them, and re-layouts  20.9 us (6%)
  between operations  15.1 us (4%)
  other arithmetic  11.5 us (3%)
    pallas_call x2, Pallas kernels, middle(): pl.pallas_call(lambda *r: middle_kernel(*r, n=n, rows=rows, part=part, sp...  124 us
    pallas_call x2, Pallas kernels, feature_backward(): pl.pallas_call(lambda *r: feature_backward_kernel(*r, n=n, feats=feats, c...  34.1 us
    ppermute x15, waiting for transfers between devices, other(): lax.ppermute(a, axis, [(d, d ^ bit) for d in range(self.sizes[axis])])  30 us
    ppermute x3, waiting for transfers between devices, move(): lax.ppermute(sent, 'feat', [(d, d ^ bit) for d in range(n)])  20.5 us
    ppermute x15, starting transfers between devices, other(): lax.ppermute(a, axis, [(d, d ^ bit) for d in range(self.sizes[axis])])  18.4 us
    pallas_call x1, Pallas kernels, feature_forward(): pl.pallas_call(lambda *r: feature_forward_kernel(*r, n=n, feats=feats, cu...  18.2 us
    ppermute x21, starting transfers between devices, swap(): lax.ppermute(arrays[k], 'feat', [(d, d ^ k) for d in range(n)])  14 us
    ppermute x21, waiting for transfers between devices, swap(): lax.ppermute(arrays[k], 'feat', [(d, d ^ k) for d in range(n)])  10.1 us
  transfers between devices with their start and end apart: 46, of which 18 were waited for; matrix products, arithmetic and copies ran while one was open for 6% of the time, Pallas kernels for 52%

profile of v4, /device:TPU:0, one launch (start us, length us, event | category | flops | bytes accessed | tf_op | source)
XLA Modules:
  0.0 350.1 jit_solution(12759370735574664166)
XLA Ops:
  8.6 1.7 pack.1
  10.2 2.9 collective-permute-start
  16.7 1.8 collective-permute-start.5
  18.5 2.5 collective-permute-start.3
  24.3 2.5 collective-permute-done.3
  26.8 6.3 %collective-permute-done.4 = bf16[1,1,1,2,1,16,1664]{6,5,4,3,2,1,0:T(8,128)(2,1)S(1)} collective-permute-done((bf16[1,1,1,2,1,16,1664]{6,5,4,3,2,1,0:T(8,128)(2,1)S(1)}, bf16[1,1,1,2,1,16,1664]{6,5,4,3,2,1,0:T(8,128)(2,1)S(1)}, u32[]{:S(2)}, u32[]{:S(2)}) %collective-permute-start.4) | collective-permute-done | bytes 106528 | tf_op jit(solution)/shard_map/ppermute | solution.py:656
  33.2 1.6 collective-permute-start.6
  35.0 9.9 %collective-permute-done.6 = bf16[2,2,1,2,1,16,1664]{6,5,4,3,2,1,0:T(8,128)(2,1)S(1)} collective-permute-done((bf16[2,2,1,2,1,16,1664]{6,5,4,3,2,1,0:T(8,128)(2,1)S(1)}, bf16[2,2,1,2,1,16,1664]{6,5,4,3,2,1,0:T(8,128)(2,1)S(1)}, u32[]{:S(2)}, u32[]{:S(2)}) %collective-permute-start.6) | collective-permute-done | bytes 426016 | tf_op jit(solution)/shard_map/ppermute | solution.py:632
  45.1 20.4 %collective-permute-done.2.r_3_ = bf16[12,128,512]{2,1,0:T(8,128)(2,1)S(1)} collective-permute-done((bf16[12,128,512]{2,1,0:T(8,128)(2,1)S(1)}, bf16[12,128,512]{2,1,0:T(8,128)(2,1)S(1)}, u32[]{:S(2)}, u32[]{:S(2)}) %collective-permute-start.2) | collective-permute-done | bytes 1572896 | tf_op jit(solution)/shard_map/ppermute | solution.py:600
  73.9 18.2 %feature_forward.1 = (bf16[4,64,512]{2,1,0:T(8,128)(2,1)}, bf16[4,64,512]{2,1,0:T(8,128)(2,1)}, bf16[4,64,512]{2,1,0:T(8,128)(2,1)}, bf16[4,64,512]{2,1,0:T(8,12...) custom-call(s32[5]{0:T(128)} %stack.13.r_0_, ...), custom_call_target="tpu_custom_call" | custom-call | flops 99999997952 | bytes 1000000 | tf_op jit(solution)/shard_map/feature_forward/pallas_call | solution.py:130
  99.7 2.1 collective-permute-done.10.r_5_
  101.8 4.1 %collective-permute-done.11.r_6_ = bf16[4,64,512]{2,1,0:T(8,128)(2,1)S(1)} collective-permute-done((bf16[4,64,512]{2,1,0:T(8,128)(2,1)}, bf16[4,64,512]{2,1,0:T(8,128)(2,1)S(1)}, u32[]{:S(2)}, u32[]{:S(2)}) %collective-permute-start.11) | collective-permute-done | bytes 262176 | tf_op jit(solution)/shard_map/ppermute | solution.py:591
  106.6 40.2 %middle.2 = (bf16[1,12,256,512]{3,2,1,0:T(8,128)(2,1)}, bf16[12,256,512]{2,1,0:T(8,128)(2,1)}, bf16[4,64,512]{2,1,0:T(8,128)(2,1)}, bf16[4,64,512]{2,1,0:T(8,128...) custom-call(s32[1]{0:T(128)} %bitcast.r_0_, ...), custom_call_target="tpu_custom_call" | custom-call | flops 99999997952 | bytes 1000000 | tf_op jit(solution)/shard_map/middle/pallas_call | solution.py:480
  150.6 83.6 %middle.3 = (bf16[1,12,256,512]{3,2,1,0:T(8,128)(2,1)}, bf16[12,256,512]{2,1,0:T(8,128)(2,1)}, bf16[8,32,512]{2,1,0:T(8,128)(2,1)}, bf16[8,32,512]{2,1,0:T(8,128...) custom-call(s32[1]{0:T(128)} %bitcast.r_0_, ...), custom_call_target="tpu_custom_call", output_to_operand_aliasing={{0}: (20, {}), {1}: (21, {})} | custom-call | flops 99999997952 | bytes 1000000 | tf_op jit(solution)/shard_map/middle/pallas_call | solution.py:480
  238.0 3.7 %collective-permute-done.18 = bf16[16,208,512]{2,1,0:T(8,128)(2,1)S(1)} collective-permute-done((bf16[16,208,512]{2,1,0:T(8,128)(2,1)}, bf16[16,208,512]{2,1,0:T(8,128)(2,1)S(1)}, u32[]{:S(2)}, u32[]{:S(2)}) %collective-permute-start.18) | collective-permute-done | bytes 3407904 | tf_op jit(solution)/shard_map/ppermute | solution.py:632
  242.5 3.0 add_convert_fusion
  246.5 3.5 collective-permute-done.21.r_12_
  250.9 1.6 collective-permute-start.22
  255.0 16.5 %feature_backward.2 = (bf16[12,32,512]{2,1,0:T(8,128)(2,1)}, bf16[12,32,512]{2,1,0:T(8,128)(2,1)}, bf16[12,32,512]{2,1,0:T(8,128)(2,1)}, bf16[12,32,512]{2,1,0:T...) custom-call(s32[5]{0:T(128)} %stack.13.r_0_, bf16[12,256,512]{2,1,0:T(8,128)(2,1)} %bitcast.57, ...), custom_call_target="tpu_custom_call" | custom-call | flops 99999997952 | bytes 1000000 | tf_op jit(solution)/shard_map/feature_backward/pallas_call | solution.py:247
  271.5 2.0 collective-permute-done.23
  275.5 1.6 collective-permute-start.27
  277.2 1.8 collective-permute-start.28
  280.8 17.5 %feature_backward.3 = (bf16[12,32,512]{2,1,0:T(8,128)(2,1)}, bf16[12,32,512]{2,1,0:T(8,128)(2,1)}, bf16[12,32,512]{2,1,0:T(8,128)(2,1)}, bf16[12,32,512]{2,1,0:T...) custom-call(s32[5]{0:T(128)} %stack.13.r_0_, bf16[12,256,512]{2,1,0:T(8,128)(2,1)} %bitcast.58, ...), custom_call_target="tpu_custom_call" | custom-call | flops 99999997952 | bytes 1000000 | tf_op jit(solution)/shard_map/feature_backward/pallas_call | solution.py:247
  301.0 1.6 collective-permute-start.33
  304.2 4.4 %final.2 = f32[1,12,4,2,32,512]{5,4,3,2,1,0:T(8,128)} custom-call(s32[1]{0:T(128)} %bitcast.r_0_, bf16[12,4,2,32,512]{4,3,2,1,0:T(8,128)(2,1)} %bitcast.77, bf16[12,32,512]{2,1,0:T(8,128)(2,1)} %get-tuple-element.275.r_2_, bf16[12,32,512]{2,1,0:T(8,128)(2,1)} %copy-done.12, bf16[12,32,512]{2,1,0:T(8,128)(2,1)} %collective-permute-done.30.r_4_, ...), custom_call_target="tpu_custom_call" | custom-call | flops 99999997952 | bytes 1000000 | tf_op jit(solution)/shard_map/final/pallas_call | solution.py:537
  309.5 3.6 %collective-permute-done.32 = bf16[1,1,1,2,1,112,512]{6,5,4,3,2,1,0:T(8,128)(2,1)S(1)} collective-permute-done((bf16[1,1,1,2,1,112,512]{6,5,4,3,2,1,0:T(8,128)(2,1)S(1)}, bf16[1,1,1,2,1,112,512]{6,5,4,3,2,1,0:T(8,128)(2,1)S(1)}, u32[]{:S(2)}, u32[]{:S(2)}) %collective-permute-start.32) | collective-permute-done | bytes 229408 | tf_op jit(solution)/shard_map/ppermute | solution.py:632
  313.2 3.8 %collective-permute-done.35 = bf16[2,2,1,2,1,16,1664]{6,5,4,3,2,1,0:T(8,128)(2,1)S(1)} collective-permute-done((bf16[2,2,1,2,1,16,1664]{6,5,4,3,2,1,0:T(8,128)(2,1)S(1)}, bf16[2,2,1,2,1,16,1664]{6,5,4,3,2,1,0:T(8,128)(2,1)S(1)}, u32[]{:S(2)}, u32[]{:S(2)}) %collective-permute-start.35) | collective-permute-done | bytes 426016 | tf_op jit(solution)/shard_map/ppermute | solution.py:632
  319.3 2.6 collective-permute-start.39
  325.1 3.4 collective-permute-done.37
  329.6 4.4 %final.3 = f32[1,12,4,2,32,512]{5,4,3,2,1,0:T(8,128)} custom-call(s32[1]{0:T(128)} %bitcast.r_0_, bf16[12,4,2,32,512]{4,3,2,1,0:T(8,128)(2,1)} %bitcast.78, bf16[12,32,512]{2,1,0:T(8,128)(2,1)} %get-tuple-element.296.r_2_, bf16[12,32,512]{2,1,0:T(8,128)(2,1)} %collective-permute-done.41.r_3_, ...), custom_call_target="tpu_custom_call", output_to_operand_aliasing={{}: (6, {})} | custom-call | flops 99999997952 | bytes 1000000 | tf_op jit(solution)/shard_map/final/pallas_call | solution.py:537
  335.7 3.2 collective-permute-done.44
  339.5 1.9 unpack.1
  (195 shorter events, 57.3 us)
Async XLA Ops:
  7.2 98.7 %all-gather.3.cloned.1.call-start = ((), (), s32[]{:S(2)}) async-start(), calls=%async_computation | async-start | bytes 7028736 | tf_op jit(solution)/shard_map/all_gather | solution.py:762
  21.0 12.1 %collective-permute-start.4 = (bf16[1,1,1,2,1,16,1664]{6,5,4,3,2,1,0:T(8,128)(2,1)S(1)}, bf16[1,1,1,2,1,16,1664]{6,5,4,3,2,1,0:T(8,128)(2,1)S(1)}, u32[]{:S(2)}, u32[]{:S(2)}) collective-permute-start(bf16[1,1,1,2,1,16,1664]{6,5,4,3,2,1,0:T(8,128)(2,1)S(1)} %pad_maximum_fusion.5), channel_id=1, source_target_pairs={{0,16},{4,20},{8,24},{12,28},{16,0},{20,4},{24,8},{28,12},{1,17},{... | collective-permute-start | bytes 319496 | tf_op jit(solution)/shard_map/ppermute | solution.py:656
  22.7 42.7 %collective-permute-start.2 = (bf16[12,128,512]{2,1,0:T(8,128)(2,1)S(1)}, bf16[12,128,512]{2,1,0:T(8,128)(2,1)S(1)}, u32[]{:S(2)}, u32[]{:S(2)}) collective-permute-start(bf16[12,128,512]{2,1,0:T(8,128)(2,1)S(1)} %dynamic-slice_bitcast_fusion), channel_id=1, source_target_pairs={{0,2},{1,3},{2,0},{3,1},{4,6},{5,7},{6,4},{7,5},{8,10},{9,11},{10,... | collective-permute-start | bytes 4718600 | tf_op jit(solution)/shard_map/ppermute | solution.py:600
  33.2 11.7 %collective-permute-start.6 = (bf16[2,2,1,2,1,16,1664]{6,5,4,3,2,1,0:T(8,128)(2,1)S(1)}, bf16[2,2,1,2,1,16,1664]{6,5,4,3,2,1,0:T(8,128)(2,1)S(1)}, u32[]{:S(2)}, u32[]{:S(2)}) collective-permute-start(bf16[2,2,1,2,1,16,1664]{6,5,4,3,2,1,0:T(8,128)(2,1)S(1)} %pad_maximum_fusion.2), channel_id=1, source_target_pairs={{0,4},{4,0},{8,12},{12,8},{16,20},{20,16},{24,28},{28,24},{1,5},{5... | collective-permute-start | bytes 1277960 | tf_op jit(solution)/shard_map/ppermute | solution.py:632
  93.2 12.7 %collective-permute-start.11 = (bf16[4,64,512]{2,1,0:T(8,128)(2,1)}, bf16[4,64,512]{2,1,0:T(8,128)(2,1)S(1)}, u32[]{:S(2)}, u32[]{:S(2)}) collective-permute-start(bf16[4,64,512]{2,1,0:T(8,128)(2,1)} %get-tuple-element.172), channel_id=1, source_target_pairs={{0,3},{1,2},{2,1},{3,0},{4,7},{5,6},{6,5},{7,4},{8,11},{9,10},{10,... | collective-permute-start | bytes 786440 | tf_op jit(solution)/shard_map/ppermute | solution.py:591
  97.8 51.3 %collective-permute-start.15 = (bf16[8,64,512]{2,1,0:T(8,128)(2,1)}, bf16[8,64,512]{2,1,0:T(8,128)(2,1)S(1)}, u32[]{:S(2)}, u32[]{:S(2)}) collective-permute-start(bf16[8,64,512]{2,1,0:T(8,128)(2,1)} %get-tuple-element.179), channel_id=1, source_target_pairs={{0,1},{1,0},{2,3},{3,2},{4,5},{5,4},{6,7},{7,6},{8,9},{9,8},{10,11... | collective-permute-start | bytes 1572872 | tf_op jit(solution)/shard_map/ppermute | solution.py:591
  98.4 51.3 %collective-permute-start.16 = (bf16[8,64,512]{2,1,0:T(8,128)(2,1)}, bf16[8,64,512]{2,1,0:T(8,128)(2,1)S(1)}, u32[]{:S(2)}, u32[]{:S(2)}) collective-permute-start(bf16[8,64,512]{2,1,0:T(8,128)(2,1)} %get-tuple-element.180), channel_id=1, source_target_pairs={{0,2},{1,3},{2,0},{3,1},{4,6},{5,7},{6,4},{7,5},{8,10},{9,11},{10,... | collective-permute-start | bytes 1572872 | tf_op jit(solution)/shard_map/ppermute | solution.py:591
  99.2 50.5 %collective-permute-start.17 = (bf16[8,64,512]{2,1,0:T(8,128)(2,1)}, bf16[8,64,512]{2,1,0:T(8,128)(2,1)S(1)}, u32[]{:S(2)}, u32[]{:S(2)}) collective-permute-start(bf16[8,64,512]{2,1,0:T(8,128)(2,1)} %get-tuple-element.181), channel_id=1, source_target_pairs={{0,3},{1,2},{2,1},{3,0},{4,7},{5,6},{6,5},{7,4},{8,11},{9,10},{10,... | collective-permute-start | bytes 1572872 | tf_op jit(solution)/shard_map/ppermute | solution.py:591
  146.9 87.3 %collective-permute-start.12 = (bf16[4,64,512]{2,1,0:T(8,128)(2,1)}, bf16[4,64,512]{2,1,0:T(8,128)(2,1)S(1)}, u32[]{:S(2)}, u32[]{:S(2)}) collective-permute-start(bf16[4,64,512]{2,1,0:T(8,128)(2,1)} %get-tuple-element.175), channel_id=1, source_target_pairs={{0,1},{1,0},{2,3},{3,2},{4,5},{5,4},{6,7},{7,6},{8,9},{9,8},{10,11... | collective-permute-start | bytes 786440 | tf_op jit(solution)/shard_map/ppermute | solution.py:591
  148.2 86.0 %collective-permute-start.13 = (bf16[4,64,512]{2,1,0:T(8,128)(2,1)}, bf16[4,64,512]{2,1,0:T(8,128)(2,1)S(1)}, u32[]{:S(2)}, u32[]{:S(2)}) collective-permute-start(bf16[4,64,512]{2,1,0:T(8,128)(2,1)} %get-tuple-element.176), channel_id=1, source_target_pairs={{0,2},{1,3},{2,0},{3,1},{4,6},{5,7},{6,4},{7,5},{8,10},{9,11},{10,... | collective-permute-start | bytes 786440 | tf_op jit(solution)/shard_map/ppermute | solution.py:591
  149.0 85.2 %collective-permute-start.14 = (bf16[4,64,512]{2,1,0:T(8,128)(2,1)}, bf16[4,64,512]{2,1,0:T(8,128)(2,1)S(1)}, u32[]{:S(2)}, u32[]{:S(2)}) collective-permute-start(bf16[4,64,512]{2,1,0:T(8,128)(2,1)} %get-tuple-element.177), channel_id=1, source_target_pairs={{0,3},{1,2},{2,1},{3,0},{4,7},{5,6},{6,5},{7,4},{8,11},{9,10},{10,... | collective-permute-start | bytes 786440 | tf_op jit(solution)/shard_map/ppermute | solution.py:591
  235.8 9.7 %collective-permute-start.19 = (bf16[8,32,512]{2,1,0:T(8,128)(2,1)}, bf16[8,32,512]{2,1,0:T(8,128)(2,1)S(1)}, u32[]{:S(2)}, u32[]{:S(2)}) collective-permute-start(bf16[8,32,512]{2,1,0:T(8,128)(2,1)} %get-tuple-element.210), channel_id=1, source_target_pairs={{0,1},{1,0},{2,3},{3,2},{4,5},{5,4},{6,7},{7,6},{8,9},{9,8},{10,11... | collective-permute-start | bytes 786440 | tf_op jit(solution)/shard_map/ppermute | solution.py:591
  235.8 10.7 %collective-permute-start.20 = (bf16[8,32,512]{2,1,0:T(8,128)(2,1)}, bf16[8,32,512]{2,1,0:T(8,128)(2,1)S(1)}, u32[]{:S(2)}, u32[]{:S(2)}) collective-permute-start(bf16[8,32,512]{2,1,0:T(8,128)(2,1)} %get-tuple-element.211), channel_id=1, source_target_pairs={{0,2},{1,3},{2,0},{3,1},{4,6},{5,7},{6,4},{7,5},{8,10},{9,11},{10,... | collective-permute-start | bytes 786440 | tf_op jit(solution)/shard_map/ppermute | solution.py:591
  236.6 13.4 %collective-permute-start.21 = (bf16[8,32,512]{2,1,0:T(8,128)(2,1)}, bf16[8,32,512]{2,1,0:T(8,128)(2,1)S(1)}, u32[]{:S(2)}, u32[]{:S(2)}) collective-permute-start(bf16[8,32,512]{2,1,0:T(8,128)(2,1)} %get-tuple-element.212), channel_id=1, source_target_pairs={{0,3},{1,2},{2,1},{3,0},{4,7},{5,6},{6,5},{7,4},{8,11},{9,10},{10,... | collective-permute-start | bytes 786440 | tf_op jit(solution)/shard_map/ppermute | solution.py:591
  237.7 33.8 %collective-permute-start.24 = (bf16[8,32,512]{2,1,0:T(8,128)(2,1)}, bf16[8,32,512]{2,1,0:T(8,128)(2,1)}, u32[]{:S(2)}, u32[]{:S(2)}) collective-permute-start(bf16[8,32,512]{2,1,0:T(8,128)(2,1)} %get-tuple-element.229), channel_id=1, source_target_pairs={{0,1},{1,0},{2,3},{3,2},{4,5},{5,4},{6,7},{7,6},{8,9},{9,8},{10,11... | collective-permute-start | bytes 786440 | tf_op jit(solution)/shard_map/ppermute | solution.py:591
  241.7 29.8 %collective-permute-start.25 = (bf16[8,32,512]{2,1,0:T(8,128)(2,1)}, bf16[8,32,512]{2,1,0:T(8,128)(2,1)}, u32[]{:S(2)}, u32[]{:S(2)}) collective-permute-start(bf16[8,32,512]{2,1,0:T(8,128)(2,1)} %get-tuple-element.230), channel_id=1, source_target_pairs={{0,2},{1,3},{2,0},{3,1},{4,6},{5,7},{6,4},{7,5},{8,10},{9,11},{10,... | collective-permute-start | bytes 786440 | tf_op jit(solution)/shard_map/ppermute | solution.py:591
  245.5 26.0 %collective-permute-start.26 = (bf16[8,32,512]{2,1,0:T(8,128)(2,1)}, bf16[8,32,512]{2,1,0:T(8,128)(2,1)S(1)}, u32[]{:S(2)}, u32[]{:S(2)}) collective-permute-start(bf16[8,32,512]{2,1,0:T(8,128)(2,1)} %get-tuple-element.231), channel_id=1, source_target_pairs={{0,3},{1,2},{2,1},{3,0},{4,7},{5,6},{6,5},{7,4},{8,11},{9,10},{10,... | collective-permute-start | bytes 786440 | tf_op jit(solution)/shard_map/ppermute | solution.py:591
  250.9 22.9 %collective-permute-start.22 = (bf16[2,2,1,2,1,112,512]{6,5,4,3,2,1,0:T(8,128)(2,1)S(1)}, bf16[2,2,1,2,1,112,512]{6,5,4,3,2,1,0:T(8,128)(2,1)S(1)}, u32[]{:S(2)}, u32[]{:S(2)}) collective-permute-start(bf16[2,2,1,2,1,112,512]{6,5,4,3,2,1,0:T(8,128)(2,1)S(1)} %get-tuple-element.318), channel_id=1, source_target_pairs={{0,4},{4,0},{8,12},{12,8},{16,20},{20,16},{24,28},{28,24},{1,5},{5... | collective-permute-start | bytes 2752520 | tf_op jit(solution)/shard_map/ppermute | solution.py:632
  253.4 20.1 %collective-permute-start.23 = (bf16[2,1,2,2,1,96,512]{6,5,4,3,2,1,0:T(8,128)(2,1)}, bf16[2,1,2,2,1,96,512]{6,5,4,3,2,1,0:T(8,128)(2,1)}, u32[]{:S(2)}, u32[]{:S(2)}) collective-permute-start(bf16[2,1,2,2,1,96,512]{6,5,4,3,2,1,0:T(8,128)(2,1)} %get-tuple-element.322), channel_id=1, source_target_pairs={{0,8},{4,12},{8,0},{12,4},{16,24},{20,28},{24,16},{28,20},{1,9},{5... | collective-permute-start | bytes 2359304 | tf_op jit(solution)/shard_map/ppermute | solution.py:632
  275.5 23.3 %collective-permute-start.27 = (bf16[2,1,1,2,1,112,512]{6,5,4,3,2,1,0:T(8,128)(2,1)S(1)}, bf16[2,1,1,2,1,112,512]{6,5,4,3,2,1,0:T(8,128)(2,1)S(1)}, u32[]{:S(2)}, u32[]{:S(2)}) collective-permute-start(bf16[2,1,1,2,1,112,512]{6,5,4,3,2,1,0:T(8,128)(2,1)S(1)} %get-tuple-element.324), channel_id=1, source_target_pairs={{0,8},{4,12},{8,0},{12,4},{16,24},{20,28},{24,16},{28,20},{1,9},{5... | collective-permute-start | bytes 1376264 | tf_op jit(solution)/shard_map/ppermute | solution.py:632
  277.2 21.2 %collective-permute-start.28 = (bf16[1,1,2,2,1,96,512]{6,5,4,3,2,1,0:T(8,128)(2,1)S(1)}, bf16[1,1,2,2,1,96,512]{6,5,4,3,2,1,0:T(8,128)(2,1)S(1)}, u32[]{:S(2)}, u32[]{:S(2)}) collective-permute-start(bf16[1,1,2,2,1,96,512]{6,5,4,3,2,1,0:T(8,128)(2,1)S(1)} %get-tuple-element.330), channel_id=1, source_target_pairs={{0,16},{4,20},{8,24},{12,28},{16,0},{20,4},{24,8},{28,12},{1,17},{... | collective-permute-start | bytes 1179656 | tf_op jit(solution)/shard_map/ppermute | solution.py:632
  278.9 19.4 %collective-permute-start.29 = (bf16[12,32,512]{2,1,0:T(8,128)(2,1)}, bf16[12,32,512]{2,1,0:T(8,128)(2,1)S(1)}, u32[]{:S(2)}, u32[]{:S(2)}) collective-permute-start(bf16[12,32,512]{2,1,0:T(8,128)(2,1)} %get-tuple-element.243), channel_id=1, source_target_pairs={{0,1},{1,0},{2,3},{3,2},{4,5},{5,4},{6,7},{7,6},{8,9},{9,8},{10,11... | collective-permute-start | bytes 1179656 | tf_op jit(solution)/shard_map/ppermute | solution.py:591
  278.9 19.4 %collective-permute-start.30 = (bf16[12,32,512]{2,1,0:T(8,128)(2,1)}, bf16[12,32,512]{2,1,0:T(8,128)(2,1)}, u32[]{:S(2)}, u32[]{:S(2)}) collective-permute-start(bf16[12,32,512]{2,1,0:T(8,128)(2,1)} %get-tuple-element.244), channel_id=1, source_target_pairs={{0,2},{1,3},{2,0},{3,1},{4,6},{5,7},{6,4},{7,5},{8,10},{9,11},{10,... | collective-permute-start | bytes 1179656 | tf_op jit(solution)/shard_map/ppermute | solution.py:591
  279.9 18.9 %collective-permute-start.31 = (bf16[12,32,512]{2,1,0:T(8,128)(2,1)}, bf16[12,32,512]{2,1,0:T(8,128)(2,1)}, u32[]{:S(2)}, u32[]{:S(2)}) collective-permute-start(bf16[12,32,512]{2,1,0:T(8,128)(2,1)} %get-tuple-element.245), channel_id=1, source_target_pairs={{0,3},{1,2},{2,1},{3,0},{4,7},{5,6},{6,5},{7,4},{8,11},{9,10},{10,... | collective-permute-start | bytes 1179656 | tf_op jit(solution)/shard_map/ppermute | solution.py:591
  299.5 13.6 %collective-permute-start.32 = (bf16[1,1,1,2,1,112,512]{6,5,4,3,2,1,0:T(8,128)(2,1)S(1)}, bf16[1,1,1,2,1,112,512]{6,5,4,3,2,1,0:T(8,128)(2,1)S(1)}, u32[]{:S(2)}, u32[]{:S(2)}) collective-permute-start(bf16[1,1,1,2,1,112,512]{6,5,4,3,2,1,0:T(8,128)(2,1)S(1)} %get-tuple-element.332), channel_id=1, source_target_pairs={{0,16},{4,20},{8,24},{12,28},{16,0},{20,4},{24,8},{28,12},{1,17},{... | collective-permute-start | bytes 688136 | tf_op jit(solution)/shard_map/ppermute | solution.py:632
  302.6 16.7 %collective-permute-start.41 = (bf16[12,32,512]{2,1,0:T(8,128)(2,1)}, bf16[12,32,512]{2,1,0:T(8,128)(2,1)}, u32[]{:S(2)}, u32[]{:S(2)}) collective-permute-start(bf16[12,32,512]{2,1,0:T(8,128)(2,1)} %get-tuple-element.286), channel_id=1, source_target_pairs={{0,1},{1,0},{2,3},{3,2},{4,5},{5,4},{6,7},{7,6},{8,9},{9,8},{10,11... | collective-permute-start | bytes 1179656 | tf_op jit(solution)/shard_map/ppermute | solution.py:591
  302.6 19.3 %collective-permute-start.42 = (bf16[12,32,512]{2,1,0:T(8,128)(2,1)}, bf16[12,32,512]{2,1,0:T(8,128)(2,1)}, u32[]{:S(2)}, u32[]{:S(2)}) collective-permute-start(bf16[12,32,512]{2,1,0:T(8,128)(2,1)} %get-tuple-element.287), channel_id=1, source_target_pairs={{0,2},{1,3},{2,0},{3,1},{4,6},{5,7},{6,4},{7,5},{8,10},{9,11},{10,... | collective-permute-start | bytes 1179656 | tf_op jit(solution)/shard_map/ppermute | solution.py:591
  303.7 13.2 %collective-permute-start.35 = (bf16[2,2,1,2,1,16,1664]{6,5,4,3,2,1,0:T(8,128)(2,1)S(1)}, bf16[2,2,1,2,1,16,1664]{6,5,4,3,2,1,0:T(8,128)(2,1)S(1)}, u32[]{:S(2)}, u32[]{:S(2)}) collective-permute-start(bf16[2,2,1,2,1,16,1664]{6,5,4,3,2,1,0:T(8,128)(2,1)S(1)} %get-tuple-element.326), channel_id=1, source_target_pairs={{0,4},{4,0},{8,12},{12,8},{16,20},{20,16},{24,28},{28,24},{1,5},{5... | collective-permute-start | bytes 1277960 | tf_op jit(solution)/shard_map/ppermute | solution.py:632
  308.8 15.0 %collective-permute-start.43 = (bf16[12,32,512]{2,1,0:T(8,128)(2,1)S(1)}, bf16[12,32,512]{2,1,0:T(8,128)(2,1)S(1)}, u32[]{:S(2)}, u32[]{:S(2)}) collective-permute-start(bf16[12,32,512]{2,1,0:T(8,128)(2,1)S(1)} %copy-done.11), channel_id=1, source_target_pairs={{0,3},{1,2},{2,1},{3,0},{4,7},{5,6},{6,5},{7,4},{8,11},{9,10},{10,... | collective-permute-start | bytes 1179656 | tf_op jit(solution)/shard_map/ppermute | solution.py:591
  317.7 11.9 %collective-permute-start.36 = (bf16[1,1,1,1,1,112,512]{6,5,4,3,2,1,0:T(8,128)(2,1)S(1)}, bf16[1,1,1,1,1,112,512]{6,5,4,3,2,1,0:T(8,128)(2,1)S(1)}, u32[]{:S(2)}, u32[]{:S(2)}) collective-permute-start(bf16[1,1,1,1,1,112,512]{6,5,4,3,2,1,0:T(8,128)(2,1)S(1)} %get-tuple-element.341), channel_id=1, source_target_pairs={{0,2},{1,3},{2,0},{3,1},{4,6},{5,7},{6,4},{7,5},{8,10},{9,11},{10,... | collective-permute-start | bytes 344072 | tf_op jit(solution)/shard_map/ppermute | solution.py:632
  318.6 9.9 %collective-permute-start.38 = (bf16[1,1,1,2,1,16,1664]{6,5,4,3,2,1,0:T(8,128)(2,1)S(1)}, bf16[1,1,1,2,1,16,1664]{6,5,4,3,2,1,0:T(8,128)(2,1)S(1)}, u32[]{:S(2)}, u32[]{:S(2)}) collective-permute-start(bf16[1,1,1,2,1,16,1664]{6,5,4,3,2,1,0:T(8,128)(2,1)S(1)} %get-tuple-element.336), channel_id=1, source_target_pairs={{0,8},{4,12},{8,0},{12,4},{16,24},{20,28},{24,16},{28,20},{1,9},{5... | collective-permute-start | bytes 319496 | tf_op jit(solution)/shard_map/ppermute | solution.py:676
  319.3 10.3 %collective-permute-start.39 = (bf16[1,1,1,2,1,16,1664]{6,5,4,3,2,1,0:T(8,128)(2,1)S(1)}, bf16[1,1,1,2,1,16,1664]{6,5,4,3,2,1,0:T(8,128)(2,1)S(1)}, u32[]{:S(2)}, u32[]{:S(2)}) collective-permute-start(bf16[1,1,1,2,1,16,1664]{6,5,4,3,2,1,0:T(8,128)(2,1)S(1)} %get-tuple-element.335), channel_id=1, source_target_pairs={{0,16},{4,20},{8,24},{12,28},{16,0},{20,4},{24,8},{28,12},{1,17},{... | collective-permute-start | bytes 319496 | tf_op jit(solution)/shard_map/ppermute | solution.py:676
  (38 other events, 210.8 us)
Sparse Core Ops, SparseCore 0:
  13.3 79.6 all-gather.2
